TPU v7x, 512 devices: a whole 4x4x16 slice. The times are simulated.
512 devices in a mesh: ctx: 32 (over x, z_lo), nbr: 4 (over z_hi, core), mp: 4 (over y).
Axes of the slice: x: 4, y: 4, z: 16 (z_hi: 2, z_lo: 8; z = z_hi * 8 + z_lo), core: 2. Of those that a mesh axis runs over, the one named last changes fastest.
Arguments:
- self_queries: bfloat16 [32768, 4096], P(('ctx', 'nbr'), 'mp'), may hold values from -6 to 6
- self_keys: bfloat16 [32768, 4096], P(('ctx', 'nbr'), 'mp'), may hold values from -6 to 6
- self_values: bfloat16 [32768, 4096], P(('ctx', 'nbr'), 'mp'), may hold values from -6 to 6
- cross_queries: bfloat16 [32768, 4096], P(('ctx', 'nbr'), 'mp'), may hold values from -6 to 6
- neighbour_keys: bfloat16 [384, 128, 4096], P(('ctx', 'nbr'), None, 'mp'), may hold values from -6 to 6
- neighbour_values: bfloat16 [384, 128, 4096], P(('ctx', 'nbr'), None, 'mp'), may hold values from -6 to 6
- neighbour_table: int32 [512, 2], replicated, may hold values from 0 to 11, as said below
- doc_lengths: int32 [33], replicated, may hold values from 1 to 2048, 32768 in all
Outputs:
- self_out: bfloat16 [32768, 4096], P(('ctx', 'nbr'), 'mp')
- cross_out: bfloat16 [32768, 4096], P(('ctx', 'nbr'), 'mp')
Inputs may be any that keep to these rules, and one draw needn't show every extreme that they name: `neighbour_table`: id // 3 is the index along nbr of the device of the stretch's ctx group that holds the encoding, id % 3 its slot there. The 2 ids of a stretch differ. The rows of the stretches of one index of ctx+nbr name exactly 2 distinct encodings held by each device of its ctx group.
All inputs are finite; a program needn't handle non-finite values.
Results may differ from a plain program's by a relative error of at most 0.005.
Values may be sent and summed in bfloat16 or wider, within the bound.
No kernel may reach another device: no remote copies, remote signals or barrier semaphores. Data moves between devices by JAX's collectives and lax.ppermute only.
A program may use at most 64 MiB of HBM per device.

v0:
```python
import jax
import jax.numpy as jnp
from jax import lax
from jax.sharding import PartitionSpec as P

HD = 128
STRETCH = 64


def from_behind(value, axis, steps):
    count = lax.axis_size(axis)
    initial, last = (max(0, -steps), min(count, count - steps))
    return lax.ppermute(value, axis, [(source, source + steps) for source in range(initial, last)])


def doc_starts(doc_lengths, positions):
    ends = jnp.cumsum(doc_lengths)
    chosen = jnp.where(ends[None, :] <= positions[:, None], doc_lengths[None, :], 0)
    return jnp.sum(chosen, axis=1)


def shards(
    self_queries,
    self_keys,
    self_values,
    cross_queries,
    neighbour_keys,
    neighbour_values,
    neighbour_table,
    doc_lengths,
):
    tokens_here, width = self_queries.shape
    heads = width // HD
    scale = HD ** (-0.5)
    span = min(8, lax.axis_size(("ctx", "nbr")) // 2)
    device = lax.axis_index(("ctx", "nbr"))
    offsets = jnp.arange(tokens_here, dtype=jnp.int32)
    query_pos = device * tokens_here + offsets
    query_start = doc_starts(doc_lengths, query_pos)
    queries = self_queries.reshape(tokens_here, heads, HD)

    def attend(state, block, first):
        run_max, run_total, context = state
        keys = block[0].reshape(tokens_here, heads, HD)
        values = block[1].reshape(tokens_here, heads, HD)
        key_pos = first + offsets
        visible = (
            (key_pos[None, :] <= query_pos[:, None]) & (key_pos[None, :] >= query_start[:, None])
        )[None]
        scores = (
            jnp.einsum("qhd,khd->hqk", queries, keys, preferred_element_type=jnp.float32) * scale
        )
        scores = jnp.where(visible, scores, -1e30)
        new_max = jnp.maximum(run_max, jnp.max(scores, axis=-1))
        factor = jnp.exp(run_max - new_max)
        weights = jnp.where(visible, jnp.exp(scores - new_max[..., None]), 0.0)
        new_total = run_total * factor + jnp.sum(weights, axis=-1)
        added = jnp.einsum(
            "hqk,khd->hqd", weights.astype(jnp.bfloat16), values, preferred_element_type=jnp.float32
        )
        return (new_max, new_total, context * factor[..., None] + added)

    start_state = (
        jnp.full((heads, tokens_here), -1e30, jnp.float32),
        jnp.zeros((heads, tokens_here), jnp.float32),
        jnp.zeros((heads, tokens_here, HD), jnp.float32),
    )
    own_block = jnp.stack([self_keys, self_values])
    state = attend(start_state, own_block, device * tokens_here)

    def advance(index, carry):
        block, inner_state = carry
        block = from_behind(block, ("ctx", "nbr"), 1)
        first = (device - index) * tokens_here
        inner_state = attend(inner_state, block, first)
        return (block, inner_state)

    final_block, state = lax.fori_loop(1, span + 1, advance, (own_block, state))
    run_max, run_total, context = state
    self_out = (
        (context / run_total[..., None])
        .transpose(1, 0, 2)
        .reshape(tokens_here, width)
        .astype(jnp.bfloat16)
    )
    per_device = tokens_here // STRETCH
    neighbours = neighbour_table.shape[1]
    requests = per_device * neighbours
    length = neighbour_keys.shape[1]
    cross_width = cross_queries.shape[1]
    cross_heads = cross_width // HD
    mine = lax.dynamic_slice_in_dim(neighbour_table, device * per_device, per_device, 0).reshape(
        requests
    )
    all_keys, all_values = (
        lax.all_gather(neighbour_keys, "nbr", axis=0, tiled=True),
        lax.all_gather(neighbour_values, "nbr", axis=0, tiled=True),
    )
    picked_keys = all_keys[mine]
    picked_values = all_values[mine]
    stretch_queries = cross_queries.reshape(per_device, STRETCH, cross_heads, HD)
    stretch_keys = picked_keys.reshape(per_device, neighbours * length, cross_heads, HD)
    stretch_values = picked_values.reshape(per_device, neighbours * length, cross_heads, HD)
    scores = (
        jnp.einsum(
            "cqhd,ckhd->chqk", stretch_queries, stretch_keys, preferred_element_type=jnp.float32
        )
        * scale
    )
    highest = jnp.max(scores, axis=-1, keepdims=True)
    weights = jnp.exp(scores - highest)
    totals = jnp.sum(weights, axis=-1)
    summed = jnp.einsum(
        "chqk,ckhd->cqhd",
        weights.astype(jnp.bfloat16),
        stretch_values,
        preferred_element_type=jnp.float32,
    )
    cross_out = (
        (summed / jnp.transpose(totals, (0, 2, 1))[..., None])
        .reshape(tokens_here, cross_width)
        .astype(jnp.bfloat16)
    )
    return (self_out, cross_out)


def solution(mesh):
    placed = (
        P(("ctx", "nbr"), "mp"),
        P(("ctx", "nbr"), "mp"),
        P(("ctx", "nbr"), "mp"),
        P(("ctx", "nbr"), "mp"),
        P(("ctx", "nbr"), None, "mp"),
        P(("ctx", "nbr"), None, "mp"),
        P(),
        P(),
    )
    return jax.shard_map(
        shards,
        mesh=mesh,
        in_specs=placed,
        out_specs=(P(("ctx", "nbr"), "mp"), P(("ctx", "nbr"), "mp")),
        check_vma=False,
    )
```

profile of v0, /device:TPU:48, one launch (start us, length us, event | category | flops | bytes accessed | tf_op | source)
XLA Modules:
  0.0 913.6 jit_solution(16195083185899345604)
XLA Ops:
  9.0 2.0 copy.83
  12.0 1.0 copy.59
  13.0 1.5 fusion.21
  15.1 1.2 copy.60
  16.3 3.1 convolution_add_fusion.1
  19.4 1.1 pad_maximum_fusion
  21.0 868.4 %while.20 = (s32[]{:T(128)}, bf16[2,256,1024]{1,2,0:T(8,128)(2,1)}, f32[8,256]{1,0:T(8,128)S(1)}, f32[8,256]{1,0:T(8,128)S(1)}, f32[8,256,128]{2,1,0:T(8,128)S(1...) while((s32[]{:T(128)}, bf16[2,256,1024]{1,2,0:T(8,128)(2,1)}, ...), condition=%wide.region_7.8_spmd.clone, body=%wide.region_4.7_spmd.clone.sunk | while | flops 275976704 | bytes 18748596 | solution.py:78
  21.0 1.9 collective-permute-start
  23.1 608.7 %collective-permute-done = bf16[2,256,1024]{1,2,0:T(8,128)(2,1)S(1)} collective-permute-done((bf16[2,256,1024]{1,2,0:T(8,128)(2,1)}, bf16[2,256,1024]{1,2,0:T(8,128)(2,1)S(1)}, u32[]{:S(2)}, u32[]{:S(2)}) %collective-permute-start) | collective-permute-done | bytes 1048608 | tf_op jit(solution)/shard_map/while/body/eval_jaxpr/ppermute | solution.py:13
  632.9 1.1 convolution_add_fusion.3
  634.0 1.0 copy.126
  635.0 1.9 collective-permute-start
  637.1 41.5 %collective-permute-done = bf16[2,256,1024]{1,2,0:T(8,128)(2,1)S(1)} collective-permute-done((bf16[2,256,1024]{1,2,0:T(8,128)(2,1)}, bf16[2,256,1024]{1,2,0:T(8,128)(2,1)S(1)}, u32[]{:S(2)}, u32[]{:S(2)}) %collective-permute-start) | collective-permute-done | bytes 1048608 | tf_op jit(solution)/shard_map/while/body/eval_jaxpr/ppermute | solution.py:13
  679.7 1.1 convolution_add_fusion.3
  680.8 1.0 copy.126
  681.8 1.9 collective-permute-start
  683.8 44.7 %collective-permute-done = bf16[2,256,1024]{1,2,0:T(8,128)(2,1)S(1)} collective-permute-done((bf16[2,256,1024]{1,2,0:T(8,128)(2,1)}, bf16[2,256,1024]{1,2,0:T(8,128)(2,1)S(1)}, u32[]{:S(2)}, u32[]{:S(2)}) %collective-permute-start) | collective-permute-done | bytes 1048608 | tf_op jit(solution)/shard_map/while/body/eval_jaxpr/ppermute | solution.py:13
  729.8 1.1 convolution_add_fusion.3
  730.8 1.0 copy.126
  731.8 1.9 collective-permute-start
  733.9 22.2 %collective-permute-done = bf16[2,256,1024]{1,2,0:T(8,128)(2,1)S(1)} collective-permute-done((bf16[2,256,1024]{1,2,0:T(8,128)(2,1)}, bf16[2,256,1024]{1,2,0:T(8,128)(2,1)S(1)}, u32[]{:S(2)}, u32[]{:S(2)}) %collective-permute-start) | collective-permute-done | bytes 1048608 | tf_op jit(solution)/shard_map/while/body/eval_jaxpr/ppermute | solution.py:13
  757.3 1.1 convolution_add_fusion.3
  758.3 1.0 copy.126
  759.3 1.9 collective-permute-start
  761.4 33.4 %collective-permute-done = bf16[2,256,1024]{1,2,0:T(8,128)(2,1)S(1)} collective-permute-done((bf16[2,256,1024]{1,2,0:T(8,128)(2,1)}, bf16[2,256,1024]{1,2,0:T(8,128)(2,1)S(1)}, u32[]{:S(2)}, u32[]{:S(2)}) %collective-permute-start) | collective-permute-done | bytes 1048608 | tf_op jit(solution)/shard_map/while/body/eval_jaxpr/ppermute | solution.py:13
  796.0 1.1 convolution_add_fusion.3
  797.1 1.0 copy.126
  798.1 1.9 collective-permute-start
  800.1 31.2 %collective-permute-done = bf16[2,256,1024]{1,2,0:T(8,128)(2,1)S(1)} collective-permute-done((bf16[2,256,1024]{1,2,0:T(8,128)(2,1)}, bf16[2,256,1024]{1,2,0:T(8,128)(2,1)S(1)}, u32[]{:S(2)}, u32[]{:S(2)}) %collective-permute-start) | collective-permute-done | bytes 1048608 | tf_op jit(solution)/shard_map/while/body/eval_jaxpr/ppermute | solution.py:13
  832.5 1.1 convolution_add_fusion.3
  833.6 1.0 copy.126
  834.6 1.9 collective-permute-start
  836.7 22.1 %collective-permute-done = bf16[2,256,1024]{1,2,0:T(8,128)(2,1)S(1)} collective-permute-done((bf16[2,256,1024]{1,2,0:T(8,128)(2,1)}, bf16[2,256,1024]{1,2,0:T(8,128)(2,1)S(1)}, u32[]{:S(2)}, u32[]{:S(2)}) %collective-permute-start) | collective-permute-done | bytes 1048608 | tf_op jit(solution)/shard_map/while/body/eval_jaxpr/ppermute | solution.py:13
  859.9 1.1 convolution_add_fusion.3
  861.0 1.0 copy.126
  862.0 1.9 collective-permute-start
  864.0 22.1 %collective-permute-done = bf16[2,256,1024]{1,2,0:T(8,128)(2,1)S(1)} collective-permute-done((bf16[2,256,1024]{1,2,0:T(8,128)(2,1)}, bf16[2,256,1024]{1,2,0:T(8,128)(2,1)S(1)}, u32[]{:S(2)}, u32[]{:S(2)}) %collective-permute-start) | collective-permute-done | bytes 1048608 | tf_op jit(solution)/shard_map/while/body/eval_jaxpr/ppermute | solution.py:13
  887.3 1.1 convolution_add_fusion.3
  888.4 1.0 copy.126
  889.4 1.1 copy_bitcast_fusion.1
  890.5 3.9 gather_fusion.1
  894.4 2.2 copy.82
  896.7 3.9 gather_fusion
  900.6 2.3 copy.84
  902.9 0.9 bitcast_reduce_fusion
  903.8 0.8 fusion.22
  904.6 0.9 fusion.32
  905.9 0.9 copy.114
  (101 shorter events, 14.3 us)
Async XLA Ops:
  7.2 1.5 copy-start
  7.2 3.8 copy-start.6
  7.2 4.3 copy-start.5
  7.2 883.3 %all-gather.5.cloned.1.call-start = ((), (), s32[]{:S(2)}) async-start(), calls=%async_computation.1 | async-start | bytes 3932160 | tf_op jit(solution)/shard_map/all_gather | solution.py:96
  7.9 4.1 copy-start.1
  7.9 888.7 %all-gather.3.cloned.1.call-start = ((), (), s32[]{:S(2)}) async-start(), calls=%async_computation | async-start | bytes 3932160 | tf_op jit(solution)/shard_map/all_gather | solution.py:97
  16.3 3.1 copy-start.3
  19.4 1.6 copy-start.4
  21.0 610.7 %collective-permute-start = (bf16[2,256,1024]{1,2,0:T(8,128)(2,1)}, bf16[2,256,1024]{1,2,0:T(8,128)(2,1)S(1)}, u32[]{:S(2)}, u32[]{:S(2)}) collective-permute-start(bf16[2,256,1024]{1,2,0:T(8,128)(2,1)} %get-tuple-element.338), channel_id=1, source_target_pairs={{0,4},{4,8},{8,12},{12,16},{16,20},{20,24},{24,28},{28,32},{32,36}... | collective-permute-start | bytes 3145736 | tf_op jit(solution)/shard_map/while/body/eval_jaxpr/ppermute | solution.py:13
  635.0 43.5 %collective-permute-start = (bf16[2,256,1024]{1,2,0:T(8,128)(2,1)}, bf16[2,256,1024]{1,2,0:T(8,128)(2,1)S(1)}, u32[]{:S(2)}, u32[]{:S(2)}) collective-permute-start(bf16[2,256,1024]{1,2,0:T(8,128)(2,1)} %get-tuple-element.338), channel_id=1, source_target_pairs={{0,4},{4,8},{8,12},{12,16},{16,20},{20,24},{24,28},{28,32},{32,36}... | collective-permute-start | bytes 3145736 | tf_op jit(solution)/shard_map/while/body/eval_jaxpr/ppermute | solution.py:13
  681.8 46.8 %collective-permute-start = (bf16[2,256,1024]{1,2,0:T(8,128)(2,1)}, bf16[2,256,1024]{1,2,0:T(8,128)(2,1)S(1)}, u32[]{:S(2)}, u32[]{:S(2)}) collective-permute-start(bf16[2,256,1024]{1,2,0:T(8,128)(2,1)} %get-tuple-element.338), channel_id=1, source_target_pairs={{0,4},{4,8},{8,12},{12,16},{16,20},{20,24},{24,28},{28,32},{32,36}... | collective-permute-start | bytes 3145736 | tf_op jit(solution)/shard_map/while/body/eval_jaxpr/ppermute | solution.py:13
  731.8 24.2 %collective-permute-start = (bf16[2,256,1024]{1,2,0:T(8,128)(2,1)}, bf16[2,256,1024]{1,2,0:T(8,128)(2,1)S(1)}, u32[]{:S(2)}, u32[]{:S(2)}) collective-permute-start(bf16[2,256,1024]{1,2,0:T(8,128)(2,1)} %get-tuple-element.338), channel_id=1, source_target_pairs={{0,4},{4,8},{8,12},{12,16},{16,20},{20,24},{24,28},{28,32},{32,36}... | collective-permute-start | bytes 3145736 | tf_op jit(solution)/shard_map/while/body/eval_jaxpr/ppermute | solution.py:13
  759.3 35.5 %collective-permute-start = (bf16[2,256,1024]{1,2,0:T(8,128)(2,1)}, bf16[2,256,1024]{1,2,0:T(8,128)(2,1)S(1)}, u32[]{:S(2)}, u32[]{:S(2)}) collective-permute-start(bf16[2,256,1024]{1,2,0:T(8,128)(2,1)} %get-tuple-element.338), channel_id=1, source_target_pairs={{0,4},{4,8},{8,12},{12,16},{16,20},{20,24},{24,28},{28,32},{32,36}... | collective-permute-start | bytes 3145736 | tf_op jit(solution)/shard_map/while/body/eval_jaxpr/ppermute | solution.py:13
  798.1 33.3 %collective-permute-start = (bf16[2,256,1024]{1,2,0:T(8,128)(2,1)}, bf16[2,256,1024]{1,2,0:T(8,128)(2,1)S(1)}, u32[]{:S(2)}, u32[]{:S(2)}) collective-permute-start(bf16[2,256,1024]{1,2,0:T(8,128)(2,1)} %get-tuple-element.338), channel_id=1, source_target_pairs={{0,4},{4,8},{8,12},{12,16},{16,20},{20,24},{24,28},{28,32},{32,36}... | collective-permute-start | bytes 3145736 | tf_op jit(solution)/shard_map/while/body/eval_jaxpr/ppermute | solution.py:13
  834.6 24.1 %collective-permute-start = (bf16[2,256,1024]{1,2,0:T(8,128)(2,1)}, bf16[2,256,1024]{1,2,0:T(8,128)(2,1)S(1)}, u32[]{:S(2)}, u32[]{:S(2)}) collective-permute-start(bf16[2,256,1024]{1,2,0:T(8,128)(2,1)} %get-tuple-element.338), channel_id=1, source_target_pairs={{0,4},{4,8},{8,12},{12,16},{16,20},{20,24},{24,28},{28,32},{32,36}... | collective-permute-start | bytes 3145736 | tf_op jit(solution)/shard_map/while/body/eval_jaxpr/ppermute | solution.py:13
  862.0 24.1 %collective-permute-start = (bf16[2,256,1024]{1,2,0:T(8,128)(2,1)}, bf16[2,256,1024]{1,2,0:T(8,128)(2,1)S(1)}, u32[]{:S(2)}, u32[]{:S(2)}) collective-permute-start(bf16[2,256,1024]{1,2,0:T(8,128)(2,1)} %get-tuple-element.338), channel_id=1, source_target_pairs={{0,4},{4,8},{8,12},{12,16},{16,20},{20,24},{24,28},{28,32},{32,36}... | collective-permute-start | bytes 3145736 | tf_op jit(solution)/shard_map/while/body/eval_jaxpr/ppermute | solution.py:13
  900.6 2.3 copy-start.2
Sparse Core Ops, SparseCore 0:
  10.1 109.5 all-gather.4
  121.8 235.9 all-gather.2
where the time goes:
time: 914 us
  waiting for transfers between devices  827 us (90%)
  local copies, waits for them, and re-layouts  27.8 us (3%)
  matrix products  19.3 us (2%)
  starting transfers between devices  15.3 us (2%)
  between operations  14.2 us (2%)
  other arithmetic  9.17 us (1%)
    ppermute x8, waiting for transfers between devices, from_behind(): lax.ppermute(value, axis, [(source, source + steps) for source in range(i...  826 us
  transfers between devices with their start and end apart: 10, of which 8 were waited for; matrix products, arithmetic and copies ran while one was open for 5% of the time, Pallas kernels for 0%

commit v1 on v0

v1 whole, which is shorter than its diff:
```python
import functools
import jax
import jax.numpy as jnp
from jax import lax
from jax.experimental import pallas as pl
from jax.experimental.pallas import tpu as pltpu
from jax.sharding import PartitionSpec as P

HD = 128
STRETCH = 64
LOG2E = 1.4426950408889634
EXP_SCALE = LOG2E * HD**-0.5
HIDDEN = -1e30
FLOOR = -1e29
ALL = ("ctx", "nbr")


def shift(value, by):
    count = lax.axis_size(ALL)
    return lax.ppermute(value, ALL, [(d, (d + by) % count) for d in range(count)])


def swap(value, bit):
    count = lax.axis_size(ALL)
    return lax.ppermute(value, ALL, [(d, d ^ bit) for d in range(count)])


def self_kernel(blocks, first, last, meta, *refs):
    refs = list(refs)
    q_ref = refs.pop(0)
    start_ref = refs.pop(0)
    keys = [refs.pop(0) for _ in blocks]
    values = [refs.pop(0) for _ in blocks]
    if not first:
        acc_in, top_in, total_in = refs.pop(0), refs.pop(0), refs.pop(0)
    if last:
        out_ref = refs.pop(0)
        acc, top, total = refs
    else:
        acc, top, total = refs
    half = q_ref.shape[0] // 2
    if first:
        acc[...] = jnp.zeros_like(acc)
        top[...] = jnp.full_like(top, FLOOR)
        total[...] = jnp.zeros_like(total)
    else:
        acc[...] = acc_in[...]
        top[...] = top_in[...]
        total[...] = total_in[...]
    for qi in range(2):
        rows = pl.ds(qi * half, half)
        q_base = meta[qi]
        q_first = meta[2 + qi]
        for bi, back in enumerate(blocks):
            for ki in range(2):
                k_base = meta[ki] - back * 2 * half
                seen = (k_base <= q_base + half - 1) & (k_base + half - 1 >= q_first)

                @pl.when(seen)
                def _(rows=rows, bi=bi, ki=ki, k_base=k_base, q_base=q_base):
                    cols = pl.ds(ki * half, half)
                    scores = lax.dot_general(
                        q_ref[rows, :],
                        keys[bi][cols, :],
                        (((1,), (1,)), ((), ())),
                        preferred_element_type=jnp.float32,
                    )
                    k_pos = k_base + lax.broadcasted_iota(jnp.int32, (half, half), 1)
                    q_pos = q_base + lax.broadcasted_iota(jnp.int32, (half, half), 0)
                    begin = start_ref[rows, :]
                    begin = jnp.concatenate([begin] * (half // HD), axis=1)
                    scores = jnp.where((k_pos <= q_pos) & (k_pos >= begin), scores, HIDDEN)
                    old = top[0, rows, :]
                    new = jnp.maximum(old, jnp.max(scores, axis=1, keepdims=True))
                    wide = jnp.concatenate([new] * (half // HD), axis=1)
                    weights = jnp.exp2((scores - wide) * EXP_SCALE)
                    factor = jnp.exp2((old - new) * EXP_SCALE)
                    top[0, rows, :] = new
                    total[0, rows, :] = total[0, rows, :] * factor + jnp.sum(
                        weights, axis=1, keepdims=True
                    )
                    acc[rows, :] = acc[rows, :] * factor + jnp.dot(
                        weights.astype(jnp.bfloat16),
                        values[bi][cols, :],
                        preferred_element_type=jnp.float32,
                    )

    if last:
        out_ref[...] = (acc[...] / total[0]).astype(out_ref.dtype)


def self_part(meta, queries, starts, blocks, keys, values, state, last):
    rows, width = queries.shape
    heads = width // HD
    column = pl.BlockSpec((rows, HD), lambda h: (0, h))
    stat = pl.BlockSpec((1, rows, HD), lambda h: (h, 0, 0))
    first = state is None
    n = len(blocks)
    in_specs = [
        pl.BlockSpec(memory_space=pltpu.SMEM),
        column,
        pl.BlockSpec((rows, HD), lambda h: (0, 0)),
    ] + [column] * (2 * n)
    args = [meta, queries, starts, *keys, *values]
    if not first:
        in_specs += [column, stat, stat]
        args += list(state)
    state_shapes = (
        jax.ShapeDtypeStruct((rows, width), jnp.float32),
        jax.ShapeDtypeStruct((heads, rows, HD), jnp.float32),
        jax.ShapeDtypeStruct((heads, rows, HD), jnp.float32),
    )
    if last:
        out_shape = jax.ShapeDtypeStruct((rows, width), jnp.bfloat16)
        out_specs = column
        scratch = [
            pltpu.VMEM((rows, HD), jnp.float32),
            pltpu.VMEM((1, rows, HD), jnp.float32),
            pltpu.VMEM((1, rows, HD), jnp.float32),
        ]
    else:
        out_shape = state_shapes
        out_specs = (column, stat, stat)
        scratch = []
    return pl.pallas_call(
        functools.partial(self_kernel, tuple(blocks), first, last),
        grid=(heads,),
        in_specs=in_specs,
        out_specs=out_specs,
        out_shape=out_shape,
        scratch_shapes=scratch,
        compiler_params=pltpu.CompilerParams(vmem_limit_bytes=32 * 1024 * 1024),
    )(*args)


def cross_kernel(per, meta, q_ref, k_ref, v_ref, o_ref, stat_ref, column):
    length = k_ref.shape[1]
    requests = 2 * per
    side = lax.broadcasted_iota(jnp.int32, (STRETCH, 2 * length), 1) < length
    lane = lax.broadcasted_iota(jnp.int32, (STRETCH, HD), 1)
    for t in range(per):
        rows = pl.ds(t * STRETCH, STRETCH)
        a, b = meta[2 * t], meta[2 * t + 1]
        have_a, have_b = meta[requests + 2 * t], meta[requests + 2 * t + 1]
        k = jnp.concatenate([k_ref[a], k_ref[b]], axis=0)
        v = jnp.concatenate([v_ref[a], v_ref[b]], axis=0)
        scores = lax.dot_general(
            q_ref[rows, :], k, (((1,), (1,)), ((), ())), preferred_element_type=jnp.float32
        )
        have = jnp.where(side, have_a, have_b)
        scores = jnp.where(have > 0, scores, HIDDEN)
        top = jnp.maximum(jnp.max(scores, axis=1, keepdims=True), FLOOR)
        weights = jnp.exp2((scores - top) * EXP_SCALE)
        total = jnp.sum(weights, axis=1, keepdims=True)
        o_ref[rows, :] = jnp.dot(
            weights.astype(jnp.bfloat16), v, preferred_element_type=jnp.float32
        ).astype(o_ref.dtype)
        column[rows, :] = jnp.where(lane == 0, top, jnp.where(lane == 1, total, 0.0))
    stat_ref[0] = jnp.transpose(column[...])[:8, :]


def cross_part(meta, queries, keys, values, out_type):
    rows, width = queries.shape
    heads = width // HD
    per = rows // STRETCH
    held, length, _ = keys.shape
    column = pl.BlockSpec((rows, HD), lambda h: (0, h))
    pool = pl.BlockSpec((held, length, HD), lambda h: (0, 0, h))
    return pl.pallas_call(
        functools.partial(cross_kernel, per),
        grid=(heads,),
        in_specs=[pl.BlockSpec(memory_space=pltpu.SMEM), column, pool, pool],
        out_specs=(column, pl.BlockSpec((1, 8, rows), lambda h: (h, 0, 0))),
        out_shape=(
            jax.ShapeDtypeStruct((rows, width), out_type),
            jax.ShapeDtypeStruct((heads, 8, rows), jnp.float32),
        ),
        scratch_shapes=[pltpu.VMEM((rows, HD), jnp.float32)],
        compiler_params=pltpu.CompilerParams(vmem_limit_bytes=32 * 1024 * 1024),
    )(meta, queries, keys, values)


def merge_kernel(oa_ref, ob_ref, sa_ref, sb_ref, out_ref):
    rows = oa_ref.shape[0]
    fill = jnp.zeros((HD - 16, rows), jnp.float32)
    stats = jnp.transpose(jnp.concatenate([sa_ref[0], sb_ref[0], fill], axis=0))
    top_a, total_a = stats[:, 0:1], stats[:, 1:2]
    top_b, total_b = stats[:, 8:9], stats[:, 9:10]
    top = jnp.maximum(top_a, top_b)
    part_a = jnp.exp2((top_a - top) * EXP_SCALE)
    part_b = jnp.exp2((top_b - top) * EXP_SCALE)
    total = total_a * part_a + total_b * part_b
    summed = oa_ref[...] * part_a + ob_ref[...].astype(jnp.float32) * part_b
    out_ref[...] = (summed / total).astype(out_ref.dtype)


def merge(oa, ob, sa, sb):
    rows, width = oa.shape
    heads = width // HD
    column = pl.BlockSpec((rows, HD), lambda h: (0, h))
    stat = pl.BlockSpec((1, 8, rows), lambda h: (h, 0, 0))
    return pl.pallas_call(
        merge_kernel,
        grid=(heads,),
        in_specs=[column, column, stat, stat],
        out_specs=column,
        out_shape=jax.ShapeDtypeStruct((rows, width), jnp.bfloat16),
    )(oa, ob, sa, sb)


def shards(
    self_queries,
    self_keys,
    self_values,
    cross_queries,
    neighbour_keys,
    neighbour_values,
    neighbour_table,
    doc_lengths,
):
    tokens, width = self_queries.shape
    part = width // 2
    device = lax.axis_index(ALL)
    core = device % 2
    zhi = (device // 2) % 2
    chip = device // 2

    far_queries = swap(cross_queries, 2)
    keys_beside = swap(neighbour_keys, 1)
    values_beside = swap(neighbour_values, 1)

    def mine(x):
        return lax.dynamic_slice_in_dim(x, core * part, part, 1)

    def other(x):
        return lax.dynamic_slice_in_dim(x, (1 - core) * part, part, 1)

    trio = (self_keys, self_values, self_queries)
    beside = swap(jnp.stack([other(x) for x in trio]), 1)
    k0, v0, q0 = (jnp.concatenate([mine(x), beside[i]], axis=0) for i, x in enumerate(trio))

    k2 = shift(k0, 4)
    v3 = shift(v0, 6)
    v2 = shift(v0, 4)
    k4 = shift(k2, 4)
    v1 = shift(v3, -4)
    v4 = shift(v2, 4)
    k1 = shift(k4, -6)
    k3 = shift(k1, 4)

    base = jnp.stack([chip * 2 * tokens + core * tokens, chip * 2 * tokens + (1 - core) * tokens])
    positions = (base[:, None] + jnp.arange(tokens, dtype=jnp.int32)[None, :]).reshape(-1)
    ends = jnp.cumsum(doc_lengths)
    starts = jnp.sum(jnp.where(ends[None, :] <= positions[:, None], doc_lengths[None, :], 0), axis=1)
    self_meta = jnp.stack([base[0], base[1], starts[0], starts[tokens]]).astype(jnp.int32)
    starts_wide = jnp.broadcast_to(starts[:, None], (2 * tokens, HD)).astype(jnp.int32)

    def pool_meta(owner):
        per = tokens // STRETCH
        ids = lax.dynamic_slice_in_dim(neighbour_table, owner * per, per, 0).reshape(-1)
        holder, slot = ids // neighbour_keys.shape[0], ids % neighbour_keys.shape[0]
        index = jnp.where(holder % 2 == core, slot, slot + neighbour_keys.shape[0])
        return jnp.concatenate([index, (holder // 2 == zhi).astype(jnp.int32)]).astype(jnp.int32)

    pool_keys = jnp.concatenate([neighbour_keys, keys_beside], axis=0)
    pool_values = jnp.concatenate([neighbour_values, values_beside], axis=0)
    far_sum, far_stat = cross_part(
        pool_meta(device ^ 2), far_queries, pool_keys, pool_values, jnp.bfloat16
    )
    back_sum = swap(far_sum, 2)
    back_stat = swap(far_stat, 2)
    near_sum, near_stat = cross_part(
        pool_meta(device), cross_queries, pool_keys, pool_values, jnp.float32
    )

    state = self_part(self_meta, q0, starts_wide, (0, 2), (k0, k2), (v0, v2), None, False)
    state = self_part(self_meta, q0, starts_wide, (4,), (k4,), (v4,), state, False)
    state = self_part(self_meta, q0, starts_wide, (1,), (k1,), (v1,), state, False)
    both = self_part(self_meta, q0, starts_wide, (3,), (k3,), (v3,), state, True)
    returned = swap(both[tokens:], 1)
    kept = both[:tokens]
    self_out = jnp.where(
        core == 0,
        jnp.concatenate([kept, returned], axis=1),
        jnp.concatenate([returned, kept], axis=1),
    )
    cross_out = merge(near_sum, back_sum, near_stat, back_stat)
    return self_out, cross_out


def solution(mesh):
    rows = P(("ctx", "nbr"), "mp")
    pool = P(("ctx", "nbr"), None, "mp")
    return jax.shard_map(
        shards,
        mesh=mesh,
        in_specs=(rows, rows, rows, rows, pool, pool, P(), P()),
        out_specs=(rows, rows),
        check_vma=False,
    )
```

time: 914 us -> 336 us (0.37)
  the two profiles are of different devices: /device:TPU:48 before, /device:TPU:38 now
where the time goes in v1:
time: 336 us; the launch traced here: 335 us
  starting transfers between devices  169 us (50%)
  waiting for transfers between devices  83.6 us (25%)
  Pallas kernels  63.2 us (19%)
  local copies, waits for them, and re-layouts  13.7 us (4%)
  other arithmetic  4.22 us (1%)
    ppermute x8, starting transfers between devices, shift(): lax.ppermute(value, ALL, [(d, (d + by) % count) for d in range(count)])  144 us
    ppermute x8, waiting for transfers between devices, shift(): lax.ppermute(value, ALL, [(d, (d + by) % count) for d in range(count)])  45.4 us
    ppermute x7, waiting for transfers between devices, swap(): return lax.ppermute(value, ALL, [(d, d ^ bit) for d in range(count)])  38.2 us
    pallas_call x4, Pallas kernels, self_part(): pl.pallas_call(functools.partial(self_kernel, tuple(blocks), first, last)...  35.4 us
    ppermute x7, starting transfers between devices, swap(): return lax.ppermute(value, ALL, [(d, d ^ bit) for d in range(count)])  25.3 us
    pallas_call x2, Pallas kernels, cross_part(): pl.pallas_call(functools.partial(cross_kernel, per), grid=(heads,), in_sp...  20.6 us
    pallas_call x1, Pallas kernels, merge(): pl.pallas_call(merge_kernel, grid=(heads,), in_specs=[column, column, sta...  7.19 us
  transfers between devices with their start and end apart: 15, of which 6 were waited for; matrix products, arithmetic and copies ran while one was open for 3% of the time, Pallas kernels for 19%

profile of v1, /device:TPU:38, one launch (start us, length us, event | category | flops | bytes accessed | tf_op | source)
XLA Modules:
  0.0 335.1 jit_solution(1472646685930297764)
XLA Ops:
  0.7 1.1 constant_dynamic-slice_fusion.4
  1.7 2.0 constant_dynamic-slice_fusion.2
  3.8 1.9 collective-permute-start
  5.7 2.3 collective-permute-done
  8.0 0.8 slice_bitcast_fusion
  8.9 3.8 %collective-permute-start.1 = (bf16[512,512]{1,0:T(8,128)(2,1)S(1)}, bf16[512,512]{1,0:T(8,128)(2,1)}, u32[]{:S(2)}, u32[]{:S(2)}) collective-permute-start(bf16[512,512]{1,0:T(8,128)(2,1)S(1)} %pad_maximum_fusion.2.refs_2_), channel_id=1, source_target_pairs={{0,16},{4,20},{8,24},{12,28},{16,32},{20,36},{24,40},{28,44},{32,4... | collective-permute-start | bytes 1572872 | tf_op jit(solution)/shard_map/ppermute | solution.py:20
  12.7 1.9 collective-permute-start.10
  14.6 2.4 collective-permute-start.11
  17.3 7.5 %collective-permute-done.1.refs_3_ = bf16[512,512]{1,0:T(8,128)(2,1)} collective-permute-done((bf16[512,512]{1,0:T(8,128)(2,1)S(1)}, bf16[512,512]{1,0:T(8,128)(2,1)}, u32[]{:S(2)}, u32[]{:S(2)}) %collective-permute-start.1) | collective-permute-done | bytes 524320 | tf_op jit(solution)/shard_map/ppermute | solution.py:20
  24.8 3.8 %collective-permute-start.2 = (bf16[512,512]{1,0:T(8,128)(2,1)}, bf16[512,512]{1,0:T(8,128)(2,1)S(1)}, u32[]{:S(2)}, u32[]{:S(2)}) collective-permute-start(bf16[512,512]{1,0:T(8,128)(2,1)} %collective-permute-done.1.refs_3_), channel_id=1, source_target_pairs={{0,16},{4,20},{8,24},{12,28},{16,32},{20,36},{24,40},{28,44},{32,4... | collective-permute-start | bytes 1572872 | tf_op jit(solution)/shard_map/ppermute | solution.py:20
  29.4 0.1 copy.25
  29.6 0.1 copy.28
  29.8 0.1 copy.24
  30.0 0.1 reduce
  30.1 1.2 constant_dynamic-update-slice_fusion.1
  31.4 1.0 pad_maximum_fusion.3.refs_4_
  32.4 4.4 %collective-permute-start.7 = (bf16[512,512]{1,0:T(8,128)(2,1)S(1)}, bf16[512,512]{1,0:T(8,128)(2,1)}, u32[]{:S(2)}, u32[]{:S(2)}) collective-permute-start(bf16[512,512]{1,0:T(8,128)(2,1)S(1)} %pad_maximum_fusion.3.refs_4_), channel_id=1, source_target_pairs={{0,16},{4,20},{8,24},{12,28},{16,32},{20,36},{24,40},{28,44},{32,4... | collective-permute-start | bytes 1572872 | tf_op jit(solution)/shard_map/ppermute | solution.py:20
  36.8 13.3 %collective-permute-start.5 = (bf16[512,512]{1,0:T(8,128)(2,1)S(1)}, bf16[512,512]{1,0:T(8,128)(2,1)}, u32[]{:S(2)}, u32[]{:S(2)}) collective-permute-start(bf16[512,512]{1,0:T(8,128)(2,1)S(1)} %pad_maximum_fusion.3.refs_4_), channel_id=1, source_target_pairs={{0,24},{4,28},{8,32},{12,36},{16,40},{20,44},{24,48},{28,52},{32,5... | collective-permute-start | bytes 1572872 | tf_op jit(solution)/shard_map/ppermute | solution.py:20
  50.1 104.5 %collective-permute-start.3 = (bf16[512,512]{1,0:T(8,128)(2,1)S(1)}, bf16[512,512]{1,0:T(8,128)(2,1)}, u32[]{:S(2)}, u32[]{:S(2)}) collective-permute-start(bf16[512,512]{1,0:T(8,128)(2,1)S(1)} %collective-permute-done.2.refs_2_), channel_id=1, source_target_pairs={{0,488},{4,492},{8,496},{12,500},{16,504},{20,508},{24,0},{28,4},{... | collective-permute-start | bytes 1572872 | tf_op jit(solution)/shard_map/ppermute | solution.py:20
  154.7 0.5 fusion.1
  155.2 1.9 collective-permute-start.12
  157.2 10.5 %collective-permute-start.8 = (bf16[512,512]{1,0:T(8,128)(2,1)}, bf16[512,512]{1,0:T(8,128)(2,1)}, u32[]{:S(2)}, u32[]{:S(2)}) collective-permute-start(bf16[512,512]{1,0:T(8,128)(2,1)} %collective-permute-done.7.refs_5_), channel_id=1, source_target_pairs={{0,16},{4,20},{8,24},{12,28},{16,32},{20,36},{24,40},{28,44},{32,4... | collective-permute-start | bytes 1572872 | tf_op jit(solution)/shard_map/ppermute | solution.py:20
  167.8 23.9 %collective-permute-done.5.refs_3_ = bf16[512,512]{1,0:T(8,128)(2,1)} collective-permute-done((bf16[512,512]{1,0:T(8,128)(2,1)S(1)}, bf16[512,512]{1,0:T(8,128)(2,1)}, u32[]{:S(2)}, u32[]{:S(2)}) %collective-permute-start.5) | collective-permute-done | bytes 524320 | tf_op jit(solution)/shard_map/ppermute | solution.py:20
  191.6 1.9 collective-permute-start.6
  193.6 14.0 %collective-permute-done.3.refs_2_ = bf16[512,512]{1,0:T(8,128)(2,1)} collective-permute-done((bf16[512,512]{1,0:T(8,128)(2,1)S(1)}, bf16[512,512]{1,0:T(8,128)(2,1)}, u32[]{:S(2)}, u32[]{:S(2)}) %collective-permute-start.3) | collective-permute-done | bytes 524320 | tf_op jit(solution)/shard_map/ppermute | solution.py:20
  207.5 1.9 collective-permute-start.4
  209.4 1.4 pad_add_fusion.1.meta
  210.8 1.2 constant_dynamic-update-slice_fusion.3
  212.0 1.2 constant_dynamic-update-slice_fusion.k_ref
  213.2 1.2 constant_dynamic-update-slice_fusion.2.v_ref
  214.4 34.8 %collective-permute-done.12.q_ref = bf16[256,1024]{1,0:T(8,128)(2,1)} collective-permute-done((bf16[256,1024]{1,0:T(8,128)(2,1)}, bf16[256,1024]{1,0:T(8,128)(2,1)}, u32[]{:S(2)}, u32[]{:S(2)}) %collective-permute-start.12) | collective-permute-done | bytes 524320 | tf_op jit(solution)/shard_map/ppermute | solution.py:25
  249.1 10.4 %shard_map.100 = (bf16[256,1024]{1,0:T(8,128)(2,1)S(1)}, f32[8,8,256]{2,1,0:T(8,128)S(1)}) custom-call(s32[16]{0:T(128)S(1)} %pad_add_fusion.3.meta, bf16[256,1024]{1,0:T(8,128)(2,1)} %collective-permute-done.12.q_ref, bf16[6,128,1024]{2,1,0:T(8,128)(2,1)S(1)} %constant_dynamic-update-slice_fusion.k_ref, ...), custom_call_target="tpu_custom_call" | custom-call | tf_op jit(solution)/shard_map/pallas_call | solution.py:169
  259.5 13.2 %collective-permute-start.13 = (bf16[256,1024]{1,0:T(8,128)(2,1)S(1)}, bf16[256,1024]{1,0:T(8,128)(2,1)S(1)}, u32[]{:S(2)}, u32[]{:S(2)}) collective-permute-start(bf16[256,1024]{1,0:T(8,128)(2,1)S(1)} %get-tuple-element.25), channel_id=1, source_target_pairs={{0,8},{4,12},{8,0},{12,4},{16,24},{20,28},{24,16},{28,20},{32,40},... | collective-permute-start | bytes 1572872 | tf_op jit(solution)/shard_map/ppermute | solution.py:25
  272.8 0.1 broadcast_in_dim.24.refs_1_
  273.0 13.5 %shard_map.95 = (f32[512,512]{1,0:T(8,128)S(1)}, f32[4,512,128]{2,1,0:T(8,128)S(1)}, f32[4,512,128]{2,1,0:T(8,128)S(1)}) custom-call(s32[4]{0:T(128)S(1)} %pad_add_fusion.1.meta, bf16[512,512]{1,0:T(8,128)(2,1)S(1)} %pad_maximum_fusion.1.refs_0_, s32[512,128]{1,0:T(8,128)S(1)} %broadcast_in_dim.24.refs_1_, bf16[512,512]{1,0:T(8,128)(2,1)S(1)} %pad_maximum_fusion.2.refs_2_, ...), custom_call_target="tpu_custom_call" | custom-call | tf_op jit(solution)/shard_map/pallas_call | solution.py:125
  286.5 5.0 %shard_map.96 = (f32[512,512]{1,0:T(8,128)S(1)}, f32[4,512,128]{2,1,0:T(8,128)S(1)}, f32[4,512,128]{2,1,0:T(8,128)S(1)}) custom-call(s32[4]{0:T(128)S(1)} %pad_add_fusion.1.meta, bf16[512,512]{1,0:T(8,128)(2,1)S(1)} %pad_maximum_fusion.1.refs_0_, s32[512,128]{1,0:T(8,128)S(1)} %broadcast_in_dim.24.refs_1_, ...), custom_call_target="tpu_custom_call" | custom-call | tf_op jit(solution)/shard_map/pallas_call | solution.py:125
  291.5 8.3 %shard_map.97 = (f32[512,512]{1,0:T(8,128)S(1)}, f32[4,512,128]{2,1,0:T(8,128)S(1)}, f32[4,512,128]{2,1,0:T(8,128)S(1)}) custom-call(s32[4]{0:T(128)S(1)} %pad_add_fusion.1.meta, bf16[512,512]{1,0:T(8,128)(2,1)S(1)} %pad_maximum_fusion.1.refs_0_, s32[512,128]{1,0:T(8,128)S(1)} %broadcast_in_dim.24.refs_1_, bf16[512,512]{1,0:T(8,128)(2,1)} %collective-permute-done.3.refs_2_, ...), custom_call_target="tpu_custom_call" | custom-call | tf_op jit(solution)/shard_map/pallas_call | solution.py:125
  299.9 8.5 %shard_map.98 = bf16[512,512]{1,0:T(8,128)(2,1)S(1)} custom-call(s32[4]{0:T(128)S(1)} %pad_add_fusion.1.meta, bf16[512,512]{1,0:T(8,128)(2,1)S(1)} %pad_maximum_fusion.1.refs_0_, s32[512,128]{1,0:T(8,128)S(1)} %broadcast_in_dim.24.refs_1_, bf16[512,512]{1,0:T(8,128)(2,1)} %collective-permute-done.4.refs_2_, bf16[512,512]{1,0:T(8,128)(2,1)} %collective-permute-done.5.refs_3_, ...), custom_call_target="tpu_custom_call" | custom-call | tf_op jit(solution)/shard_map/pallas_call | solution.py:125
  308.4 0.7 fusion
  309.1 1.9 collective-permute-start.9
  311.1 1.9 collective-permute-start.14
  313.1 10.3 %shard_map.99 = (f32[256,1024]{1,0:T(8,128)S(1)}, f32[8,8,256]{2,1,0:T(8,128)S(1)}) custom-call(s32[16]{0:T(128)S(1)} %pad_add_fusion.2.meta, bf16[256,1024]{1,0:T(8,128)(2,1)S(1)} %copy-done.1, bf16[6,128,1024]{2,1,0:T(8,128)(2,1)S(1)} %constant_dynamic-update-slice_fusion.k_ref, bf16[6,128,1024]{2,1,0:T(8,128)(2,1)S(1)} %constant_dynamic-update-slice_fusion.2.v_ref), custom_call_target="tpu_custom_call" | custom-call | tf_op jit(solution)/shard_map/pallas_call | solution.py:169
  323.4 1.0 copy-done
  324.4 0.6 copy-done.2
  325.0 1.2 collective-permute-done.14.sb_ref
  326.2 0.8 copy-done.5
  327.0 7.2 %shard_map.101 = bf16[256,1024]{1,0:T(8,128)(2,1)} custom-call(f32[256,1024]{1,0:T(8,128)} %copy-done, bf16[256,1024]{1,0:T(8,128)(2,1)} %copy-done.5, f32[8,8,256]{2,1,0:T(8,128)} %copy-done.2, f32[8,8,256]{2,1,0:T(8,128)} %copy-done.6), custom_call_target="tpu_custom_call" | custom-call | tf_op jit(solution)/shard_map/pallas_call | solution.py:202
  334.2 0.9 maximum_select_fusion
  (49 shorter events, 1.8 us)
Async XLA Ops:
  3.8 13.4 %copy-start.7 = (s32[512,2]{0,1:T(2,128)S(1)}, s32[512,2]{0,1:T(2,128)}, u32[]{:S(2)}) copy-start(s32[512,2]{0,1:T(2,128)} %param.14) | copy-start | bytes 12292
  3.8 26.0 %copy-start.8 = (s32[33]{0:T(128)S(1)}, s32[33]{0:T(128)}, u32[]{:S(2)}) copy-start(s32[33]{0:T(128)} %param.15) | copy-start | bytes 400
  3.8 4.2 %collective-permute-start = (bf16[3,256,512]{2,1,0:T(8,128)(2,1)S(1)}, bf16[3,256,512]{2,1,0:T(8,128)(2,1)S(1)}, u32[]{:S(2)}, u32[]{:S(2)}) collective-permute-start(bf16[3,256,512]{2,1,0:T(8,128)(2,1)S(1)} %pad_maximum_fusion), channel_id=1, source_target_pairs={{0,4},{4,0},{8,12},{12,8},{16,20},{20,16},{24,28},{28,24},{32,36},... | collective-permute-start | bytes 2359304 | tf_op jit(solution)/shard_map/ppermute | solution.py:25
  8.9 16.0 %collective-permute-start.1 = (bf16[512,512]{1,0:T(8,128)(2,1)S(1)}, bf16[512,512]{1,0:T(8,128)(2,1)}, u32[]{:S(2)}, u32[]{:S(2)}) collective-permute-start(bf16[512,512]{1,0:T(8,128)(2,1)S(1)} %pad_maximum_fusion.2.refs_2_), channel_id=1, source_target_pairs={{0,16},{4,20},{8,24},{12,28},{16,32},{20,36},{24,40},{28,44},{32,4... | collective-permute-start | bytes 1572872 | tf_op jit(solution)/shard_map/ppermute | solution.py:20
  12.7 142.5 %collective-permute-start.10 = (bf16[3,128,1024]{2,1,0:T(8,128)(2,1)}, bf16[3,128,1024]{2,1,0:T(8,128)(2,1)}, u32[]{:S(2)}, u32[]{:S(2)}) collective-permute-start(bf16[3,128,1024]{2,1,0:T(8,128)(2,1)} %param.12), channel_id=1, source_target_pairs={{0,4},{4,0},{8,12},{12,8},{16,20},{20,16},{24,28},{28,24},{32,36},... | collective-permute-start | bytes 2359304 | tf_op jit(solution)/shard_map/ppermute | solution.py:25
  14.6 198.6 %collective-permute-start.11 = (bf16[3,128,1024]{2,1,0:T(8,128)(2,1)}, bf16[3,128,1024]{2,1,0:T(8,128)(2,1)}, u32[]{:S(2)}, u32[]{:S(2)}) collective-permute-start(bf16[3,128,1024]{2,1,0:T(8,128)(2,1)} %param.13), channel_id=1, source_target_pairs={{0,4},{4,0},{8,12},{12,8},{16,20},{20,16},{24,28},{28,24},{32,36},... | collective-permute-start | bytes 2359304 | tf_op jit(solution)/shard_map/ppermute | solution.py:25
  24.8 25.2 %collective-permute-start.2 = (bf16[512,512]{1,0:T(8,128)(2,1)}, bf16[512,512]{1,0:T(8,128)(2,1)S(1)}, u32[]{:S(2)}, u32[]{:S(2)}) collective-permute-start(bf16[512,512]{1,0:T(8,128)(2,1)} %collective-permute-done.1.refs_3_), channel_id=1, source_target_pairs={{0,16},{4,20},{8,24},{12,28},{16,32},{20,36},{24,40},{28,44},{32,4... | collective-permute-start | bytes 1572872 | tf_op jit(solution)/shard_map/ppermute | solution.py:20
  30.1 1.3 copy-start.4
  32.4 124.8 %collective-permute-start.7 = (bf16[512,512]{1,0:T(8,128)(2,1)S(1)}, bf16[512,512]{1,0:T(8,128)(2,1)}, u32[]{:S(2)}, u32[]{:S(2)}) collective-permute-start(bf16[512,512]{1,0:T(8,128)(2,1)S(1)} %pad_maximum_fusion.3.refs_4_), channel_id=1, source_target_pairs={{0,16},{4,20},{8,24},{12,28},{16,32},{20,36},{24,40},{28,44},{32,4... | collective-permute-start | bytes 1572872 | tf_op jit(solution)/shard_map/ppermute | solution.py:20
  36.8 154.9 %collective-permute-start.5 = (bf16[512,512]{1,0:T(8,128)(2,1)S(1)}, bf16[512,512]{1,0:T(8,128)(2,1)}, u32[]{:S(2)}, u32[]{:S(2)}) collective-permute-start(bf16[512,512]{1,0:T(8,128)(2,1)S(1)} %pad_maximum_fusion.3.refs_4_), channel_id=1, source_target_pairs={{0,24},{4,28},{8,32},{12,36},{16,40},{20,44},{24,48},{28,52},{32,5... | collective-permute-start | bytes 1572872 | tf_op jit(solution)/shard_map/ppermute | solution.py:20
  50.1 157.5 %collective-permute-start.3 = (bf16[512,512]{1,0:T(8,128)(2,1)S(1)}, bf16[512,512]{1,0:T(8,128)(2,1)}, u32[]{:S(2)}, u32[]{:S(2)}) collective-permute-start(bf16[512,512]{1,0:T(8,128)(2,1)S(1)} %collective-permute-done.2.refs_2_), channel_id=1, source_target_pairs={{0,488},{4,492},{8,496},{12,500},{16,504},{20,508},{24,0},{28,4},{... | collective-permute-start | bytes 1572872 | tf_op jit(solution)/shard_map/ppermute | solution.py:20
  155.2 93.9 %collective-permute-start.12 = (bf16[256,1024]{1,0:T(8,128)(2,1)}, bf16[256,1024]{1,0:T(8,128)(2,1)}, u32[]{:S(2)}, u32[]{:S(2)}) collective-permute-start(bf16[256,1024]{1,0:T(8,128)(2,1)} %q_ref.1), channel_id=1, source_target_pairs={{0,8},{4,12},{8,0},{12,4},{16,24},{20,28},{24,16},{28,20},{32,40},... | collective-permute-start | bytes 1572872 | tf_op jit(solution)/shard_map/ppermute | solution.py:25
  157.2 129.2 %collective-permute-start.8 = (bf16[512,512]{1,0:T(8,128)(2,1)}, bf16[512,512]{1,0:T(8,128)(2,1)}, u32[]{:S(2)}, u32[]{:S(2)}) collective-permute-start(bf16[512,512]{1,0:T(8,128)(2,1)} %collective-permute-done.7.refs_5_), channel_id=1, source_target_pairs={{0,16},{4,20},{8,24},{12,28},{16,32},{20,36},{24,40},{28,44},{32,4... | collective-permute-start | bytes 1572872 | tf_op jit(solution)/shard_map/ppermute | solution.py:20
  191.6 99.8 %collective-permute-start.6 = (bf16[512,512]{1,0:T(8,128)(2,1)}, bf16[512,512]{1,0:T(8,128)(2,1)}, u32[]{:S(2)}, u32[]{:S(2)}) collective-permute-start(bf16[512,512]{1,0:T(8,128)(2,1)} %collective-permute-done.5.refs_3_), channel_id=1, source_target_pairs={{0,496},{4,500},{8,504},{12,508},{16,0},{20,4},{24,8},{28,12},{32,... | collective-permute-start | bytes 1572872 | tf_op jit(solution)/shard_map/ppermute | solution.py:20
  207.5 92.3 %collective-permute-start.4 = (bf16[512,512]{1,0:T(8,128)(2,1)}, bf16[512,512]{1,0:T(8,128)(2,1)}, u32[]{:S(2)}, u32[]{:S(2)}) collective-permute-start(bf16[512,512]{1,0:T(8,128)(2,1)} %collective-permute-done.3.refs_2_), channel_id=1, source_target_pairs={{0,16},{4,20},{8,24},{12,28},{16,32},{20,36},{24,40},{28,44},{32,4... | collective-permute-start | bytes 1572872 | tf_op jit(solution)/shard_map/ppermute | solution.py:20
  214.4 58.4 %copy-start.3 = (bf16[256,512]{1,0:T(8,128)(2,1)S(1)}, bf16[256,512]{1,0:T(8,128)(2,1)}, u32[]{:S(2)}) copy-start(bf16[256,512]{1,0:T(8,128)(2,1)} %get-tuple-element.34) | copy-start | bytes 786436
  259.5 66.7 %collective-permute-start.13 = (bf16[256,1024]{1,0:T(8,128)(2,1)S(1)}, bf16[256,1024]{1,0:T(8,128)(2,1)S(1)}, u32[]{:S(2)}, u32[]{:S(2)}) collective-permute-start(bf16[256,1024]{1,0:T(8,128)(2,1)S(1)} %get-tuple-element.25), channel_id=1, source_target_pairs={{0,8},{4,12},{8,0},{12,4},{16,24},{20,28},{24,16},{28,20},{32,40},... | collective-permute-start | bytes 1572872 | tf_op jit(solution)/shard_map/ppermute | solution.py:25
  299.9 13.2 %copy-start.1 = (bf16[256,1024]{1,0:T(8,128)(2,1)S(1)}, bf16[256,1024]{1,0:T(8,128)(2,1)}, u32[]{:S(2)}) copy-start(bf16[256,1024]{1,0:T(8,128)(2,1)} %q_ref.1) | copy-start | bytes 1572868
  309.1 25.1 %collective-permute-start.9 = (bf16[256,512]{1,0:T(8,128)(2,1)}, bf16[256,512]{1,0:T(8,128)(2,1)S(1)}, u32[]{:S(2)}, u32[]{:S(2)}) collective-permute-start(bf16[256,512]{1,0:T(8,128)(2,1)} %get-tuple-element.36), channel_id=1, source_target_pairs={{0,4},{4,0},{8,12},{12,8},{16,20},{20,16},{24,28},{28,24},{32,36},... | collective-permute-start | bytes 786440 | tf_op jit(solution)/shard_map/ppermute | solution.py:25
  311.1 15.1 %collective-permute-start.14 = (f32[8,8,256]{2,1,0:T(8,128)S(1)}, f32[8,8,256]{2,1,0:T(8,128)S(1)}, u32[]{:S(2)}, u32[]{:S(2)}) collective-permute-start(f32[8,8,256]{2,1,0:T(8,128)S(1)} %get-tuple-element.27), channel_id=1, source_target_pairs={{0,8},{4,12},{8,0},{12,4},{16,24},{20,28},{24,16},{28,20},{32,40},... | collective-permute-start | bytes 196616 | tf_op jit(solution)/shard_map/ppermute | solution.py:25
  323.4 1.0 copy-start
  324.4 0.6 copy-start.2
  326.2 0.8 copy-start.6
  326.2 0.8 copy-start.5

commit v2 on v1

v2 whole, which is shorter than its diff:
```python
import functools
import jax
import jax.numpy as jnp
from jax import lax
from jax.experimental import pallas as pl
from jax.experimental.pallas import tpu as pltpu
from jax.sharding import PartitionSpec as P

HD = 128
STRETCH = 64
LOG2E = 1.4426950408889634
EXP_SCALE = LOG2E * HD**-0.5
HIDDEN = -1e30
FLOOR = -1e29
ALL = ("ctx", "nbr")
RUN = 8
SMALL = pl.CostEstimate(flops=1, bytes_accessed=1, transcendentals=0)
LARGE = pl.CostEstimate(flops=10**11, bytes_accessed=10**8, transcendentals=0)


def place(d):
    return d // 4 % RUN, d // 2 % 2


def shift(value, by, to=lambda low, high: True):
    count = lax.axis_size(ALL)
    pairs = [(d, (d + by) % count) for d in range(count)]
    return lax.ppermute(value, ALL, [(a, b) for a, b in pairs if to(*place(b))])


def swap(value, bit):
    count = lax.axis_size(ALL)
    return lax.ppermute(value, ALL, [(d, d ^ bit) for d in range(count)])


def around(value, by):
    count = lax.axis_size(ALL)

    def target(d):
        low, high = place(d)
        z = (high * RUN + low + by) % (2 * RUN)
        return d + (z % RUN - low) * 4 + (z // RUN - high) * 2

    return lax.ppermute(value, ALL, [(d, target(d)) for d in range(count)])


def held_back(value, after):
    hbm = pl.BlockSpec(memory_space=pl.ANY)
    return pl.pallas_call(
        lambda *refs: None,
        in_specs=[hbm] * (1 + len(after)),
        out_specs=hbm,
        out_shape=jax.ShapeDtypeStruct(value.shape, value.dtype),
        input_output_aliases={0: 0},
        cost_estimate=SMALL,
    )(value, *after)


def self_kernel(blocks, first, last, skip, meta, *refs):
    refs = list(refs)
    q_ref = refs.pop(0)
    start_ref = refs.pop(0)
    pairs = [refs.pop(0) for _ in blocks]
    if not first:
        acc_in, top_in, total_in = refs.pop(0), refs.pop(0), refs.pop(0)
    refs = refs[skip:]
    if last:
        kept_ref, sent_ref = refs.pop(0), refs.pop(0)
    acc, top, total = refs
    rows = q_ref.shape[0]
    half = rows // 2
    if first:
        acc[...] = jnp.zeros_like(acc)
        top[...] = jnp.full_like(top, FLOOR)
        total[...] = jnp.zeros_like(total)
    else:
        acc[...] = acc_in[...]
        top[...] = top_in[...]
        total[...] = total_in[...]
    for bi, (back, flag) in enumerate(blocks):
        away = back * rows
        chip_first = jnp.minimum(meta[0], meta[1])
        seen = (chip_first - away + rows - 1 >= meta[2]) & (chip_first >= away)
        if flag:
            seen &= meta[2 + flag] > 0
        for qi in range(2):

            @pl.when(seen)
            def _(qi=qi, bi=bi, away=away):
                mine = pl.ds(qi * half, half)
                scores = lax.dot_general(
                    q_ref[mine, :],
                    pairs[bi][0],
                    (((1,), (1,)), ((), ())),
                    preferred_element_type=jnp.float32,
                )
                spot = lax.broadcasted_iota(jnp.int32, (half, half), 1)
                k_pos = jnp.concatenate([spot + meta[0], spot + meta[1]], axis=1) - away
                q_pos = meta[qi] + lax.broadcasted_iota(jnp.int32, (half, rows), 0)
                begin = jnp.concatenate([start_ref[mine, :]] * (rows // HD), axis=1)
                scores = jnp.where((k_pos <= q_pos) & (k_pos >= begin), scores, HIDDEN)
                old = top[0, mine, :]
                new = jnp.maximum(old, jnp.max(scores, axis=1, keepdims=True))
                wide = jnp.concatenate([new] * (rows // HD), axis=1)
                weights = jnp.exp2((scores - wide) * EXP_SCALE)
                factor = jnp.exp2((old - new) * EXP_SCALE)
                top[0, mine, :] = new
                total[0, mine, :] = total[0, mine, :] * factor + jnp.sum(
                    weights, axis=1, keepdims=True
                )
                acc[mine, :] = acc[mine, :] * factor + jnp.dot(
                    weights.astype(jnp.bfloat16), pairs[bi][1], preferred_element_type=jnp.float32
                )

    if last:
        out = (acc[...] / total[0]).astype(kept_ref.dtype)
        kept_ref[...] = out[:half]
        sent_ref[...] = out[half:]


def self_part(meta, queries, starts, blocks, pairs, state, last, after, cost):
    rows, width = queries.shape
    heads = width // HD
    column = pl.BlockSpec((rows, HD), lambda h: (0, h))
    pair = pl.BlockSpec((2, rows, HD), lambda h: (0, 0, h))
    stat = pl.BlockSpec((1, rows, HD), lambda h: (h, 0, 0))
    first = state is None
    in_specs = [
        pl.BlockSpec(memory_space=pltpu.SMEM),
        column,
        pl.BlockSpec((rows, HD), lambda h: (0, 0)),
    ] + [pair] * len(blocks)
    args = [meta, queries, starts, *pairs]
    if not first:
        in_specs += [column, stat, stat]
        args += list(state)
    in_specs += [pl.BlockSpec(memory_space=pl.ANY)] * len(after)
    args += list(after)
    if last:
        out_shape = (jax.ShapeDtypeStruct((rows // 2, width), jnp.bfloat16),) * 2
        out_specs = (pl.BlockSpec((rows // 2, HD), lambda h: (0, h)),) * 2
        scratch = [
            pltpu.VMEM((rows, HD), jnp.float32),
            pltpu.VMEM((1, rows, HD), jnp.float32),
            pltpu.VMEM((1, rows, HD), jnp.float32),
        ]
    else:
        out_shape = (
            jax.ShapeDtypeStruct((rows, width), jnp.float32),
            jax.ShapeDtypeStruct((heads, rows, HD), jnp.float32),
            jax.ShapeDtypeStruct((heads, rows, HD), jnp.float32),
        )
        out_specs = (column, stat, stat)
        scratch = []
    return pl.pallas_call(
        functools.partial(self_kernel, tuple(blocks), first, last, len(after)),
        grid=(heads,),
        in_specs=in_specs,
        out_specs=out_specs,
        out_shape=out_shape,
        scratch_shapes=scratch,
        compiler_params=pltpu.CompilerParams(vmem_limit_bytes=32 * 1024 * 1024),
        cost_estimate=cost,
    )(*args)


def cross_kernel(per, travels, meta, q_ref, k_here, v_here, side, *refs):
    if travels:
        o_ref, column = refs[-2:]
    else:
        o_ref, stat_ref, column = refs[-3:]
    k_side, v_side = side.at[0], side.at[1]
    length = k_here.shape[1]
    rows, width = q_ref.shape
    heads = width // HD
    requests = 2 * per

    def pick(here, side, r, cols):
        slot, beside = meta[r], meta[requests + r]
        return jnp.where(beside > 0, side[slot, :, cols], here[slot, :, cols])

    shape = (STRETCH, 2 * length)
    first = lax.broadcasted_iota(jnp.int32, shape, 1) < length
    have = jnp.concatenate(
        [
            jnp.where(first, meta[2 * requests + 2 * t], meta[2 * requests + 2 * t + 1])
            for t in range(per)
        ],
        axis=0,
    )
    lane = lax.broadcasted_iota(jnp.int32, (rows, HD), 1)
    stats = jnp.zeros((rows, HD), jnp.float32)
    for h in range(heads):
        cols = slice(h * HD, (h + 1) * HD)
        scores = []
        for t in range(per):
            keys = jnp.concatenate([pick(k_here, k_side, 2 * t + j, cols) for j in range(2)], axis=0)
            scores.append(
                lax.dot_general(
                    q_ref[t * STRETCH : (t + 1) * STRETCH, cols],
                    keys,
                    (((1,), (1,)), ((), ())),
                    preferred_element_type=jnp.float32,
                )
            )
        scores = jnp.where(have > 0, jnp.concatenate(scores, axis=0), HIDDEN)
        top = jnp.maximum(jnp.max(scores, axis=1, keepdims=True), FLOOR)
        weights = jnp.exp2((scores - top) * EXP_SCALE)
        total = jnp.sum(weights, axis=1, keepdims=True)
        weights = weights.astype(jnp.bfloat16)
        stats = jnp.where(lane == h, top, jnp.where(lane == heads + h, total, stats))
        for t in range(per):
            values = jnp.concatenate([pick(v_here, v_side, 2 * t + j, cols) for j in range(2)], axis=0)
            o_ref[t * STRETCH : (t + 1) * STRETCH, cols] = jnp.dot(
                weights[t * STRETCH : (t + 1) * STRETCH],
                values,
                preferred_element_type=jnp.float32,
            ).astype(o_ref.dtype)
    column[...] = stats
    stats = jnp.transpose(column[...])[: 2 * heads, :]
    if travels:
        for i in range(3):
            piece = stats.astype(jnp.bfloat16)
            o_ref[rows : rows + 2 * heads, i * rows : (i + 1) * rows] = piece
            stats = stats - piece.astype(jnp.float32)
        o_ref[rows : rows + 2 * heads, 3 * rows :] = jnp.zeros(
            (2 * heads, width - 3 * rows), jnp.bfloat16
        )
    else:
        stat_ref[...] = stats


def cross_part(meta, queries, pool, travels, after, cost):
    rows, width = queries.shape
    heads = width // HD
    vmem = pl.BlockSpec(memory_space=pltpu.VMEM)
    if travels:
        out_specs = vmem
        out_shape = jax.ShapeDtypeStruct((rows + 2 * heads, width), jnp.bfloat16)
    else:
        out_specs = (vmem, vmem)
        out_shape = (
            jax.ShapeDtypeStruct((rows, width), jnp.float32),
            jax.ShapeDtypeStruct((2 * heads, rows), jnp.float32),
        )
    return pl.pallas_call(
        functools.partial(cross_kernel, rows // STRETCH, travels),
        in_specs=[pl.BlockSpec(memory_space=pltpu.SMEM)]
        + [vmem] * 4
        + [pl.BlockSpec(memory_space=pl.ANY)] * len(after),
        out_specs=out_specs,
        out_shape=out_shape,
        scratch_shapes=[pltpu.VMEM((rows, HD), jnp.float32)],
        compiler_params=pltpu.CompilerParams(vmem_limit_bytes=32 * 1024 * 1024),
        cost_estimate=cost,
    )(meta, queries, *pool, *after)


def merge_kernel(oa_ref, ob_ref, sa_ref, out_ref):
    rows, width = oa_ref.shape
    heads = width // HD
    pieces = ob_ref[rows : rows + 2 * heads, : 3 * rows].astype(jnp.float32)
    far = pieces[:, :rows] + pieces[:, rows : 2 * rows] + pieces[:, 2 * rows :]
    fill = jnp.zeros((HD - 4 * heads, rows), jnp.float32)
    stats = jnp.transpose(jnp.concatenate([sa_ref[...], far, fill], axis=0))
    for h in range(heads):
        cols = slice(h * HD, (h + 1) * HD)
        top_a, total_a, top_b, total_b = (
            stats[:, i * heads + h : i * heads + h + 1] for i in range(4)
        )
        top = jnp.maximum(top_a, top_b)
        part_a = jnp.exp2((top_a - top) * EXP_SCALE)
        part_b = jnp.exp2((top_b - top) * EXP_SCALE)
        share = 1.0 / (total_a * part_a + total_b * part_b)
        out_ref[:, cols] = (
            oa_ref[:, cols] * (part_a * share)
            + ob_ref[:rows, cols].astype(jnp.float32) * (part_b * share)
        ).astype(out_ref.dtype)


def merge(oa, ob, sa):
    rows, width = oa.shape
    vmem = pl.BlockSpec(memory_space=pltpu.VMEM)
    return pl.pallas_call(
        merge_kernel,
        in_specs=[vmem] * 3,
        out_specs=vmem,
        out_shape=jax.ShapeDtypeStruct((rows, width), jnp.bfloat16),
        compiler_params=pltpu.CompilerParams(vmem_limit_bytes=32 * 1024 * 1024),
        cost_estimate=SMALL,
    )(oa, ob, sa)


def shards(
    self_queries,
    self_keys,
    self_values,
    cross_queries,
    neighbour_keys,
    neighbour_values,
    neighbour_table,
    doc_lengths,
):
    tokens, width = self_queries.shape
    part = width // 2
    device = lax.axis_index(ALL)
    core = device % 2
    zhi = (device // 2) % 2
    chip = device // 2

    far_queries = swap(cross_queries, 2)

    def mine(x):
        return lax.dynamic_slice_in_dim(x, core * part, part, 1)

    def other(x):
        return lax.dynamic_slice_in_dim(x, (1 - core) * part, part, 1)

    trio = (self_keys, self_values, self_queries)
    beside = swap(jnp.stack([other(x) for x in trio]), 1)
    kv0 = jnp.stack([jnp.concatenate([mine(x), beside[i]]) for i, x in enumerate(trio[:2])])
    q0 = jnp.concatenate([mine(self_queries), beside[2]])
    pool = held_back(jnp.stack([neighbour_keys, neighbour_values]), (kv0,))
    pool_beside = swap(pool, 1)

    base = jnp.stack([chip * 2 * tokens + core * tokens, chip * 2 * tokens + (1 - core) * tokens])
    positions = (base[:, None] + jnp.arange(tokens, dtype=jnp.int32)[None, :]).reshape(-1)
    ends = jnp.cumsum(doc_lengths)
    starts = jnp.sum(jnp.where(ends[None, :] <= positions[:, None], doc_lengths[None, :], 0), axis=1)
    low, high = place(device)
    flags = [low > 0, low == 0, low < RUN - 1, low == RUN - 1]
    self_meta = jnp.stack(
        [base[0], base[1], jnp.minimum(starts[0], starts[tokens]), *flags], dtype=jnp.int32
    )
    starts_wide = jnp.broadcast_to(starts[:, None], (2 * tokens, HD)).astype(jnp.int32)

    def attend(blocks, pairs, state, last=False, after=(), cost=SMALL):
        return self_part(
            self_meta, q0, starts_wide, blocks, pairs, state, last, after, cost
        )

    kv3 = shift(kv0, 6)
    kv2 = shift(kv0, 4)
    kv4_far = shift(kv0, 8, lambda low, high: low == 0)

    state = attend(((0, 0),), (kv0,), None, cost=LARGE)
    def pool_meta(owner):
        per = tokens // STRETCH
        ids = lax.dynamic_slice_in_dim(neighbour_table, owner * per, per, 0).reshape(-1)
        holder, slot = ids // neighbour_keys.shape[0], ids % neighbour_keys.shape[0]
        return jnp.concatenate([slot, holder % 2 != core, holder // 2 == zhi]).astype(jnp.int32)

    pool = (neighbour_keys, neighbour_values, pool_beside)
    near_sum, near_stat = cross_part(
        pool_meta(device), cross_queries, pool, False, state[:1], SMALL
    )
    far_sum = cross_part(
        pool_meta(device ^ 2), far_queries, pool, True, (near_stat,), SMALL
    )
    nearly = around(far_sum, 7)
    kv2 = held_back(kv2, (nearly,))
    kv4 = shift(kv2, 4, lambda low, high: low > 0)
    kv1_edge = lax.ppermute(
        jnp.where(high == 0, kv2, kv4_far),
        ALL,
        [
            (d, (d - 2 - 4 * place(d)[1]) % lax.axis_size(ALL))
            for d in range(lax.axis_size(ALL))
            if place(d)[0] == 0
        ],
    )
    state = attend(
        ((2, 0), (4, 1), (4, 2)),
        (kv2, kv4, kv4_far),
        state,
        after=(far_sum,),
    )
    kv3 = held_back(kv3, (kv2,))
    kv1 = shift(kv3, -4, lambda low, high: low < RUN - 1)
    back_sum = around(nearly, 1)
    state = attend(((3, 0),), (kv3,), state)
    kept, sent = attend(((1, 3), (1, 4)), (kv1, kv1_edge), state, True)
    returned = swap(sent, 1)
    self_out = jnp.where(
        core == 0,
        jnp.concatenate([kept, returned], axis=1),
        jnp.concatenate([returned, kept], axis=1),
    )
    cross_out = merge(near_sum, back_sum, near_stat)
    return self_out, cross_out


def solution(mesh):
    rows = P(("ctx", "nbr"), "mp")
    pool = P(("ctx", "nbr"), None, "mp")
    return jax.shard_map(
        shards,
        mesh=mesh,
        in_specs=(rows, rows, rows, rows, pool, pool, P(), P()),
        out_specs=(rows, rows),
        check_vma=False,
    )
```

time: 336 us -> 288 us (0.86)
  the two profiles are of different devices: /device:TPU:38 before, /device:TPU:29 now
where the time goes in v2:
time: 288 us; the launch traced here: 287 us
  waiting for transfers between devices  124 us (43%)
  starting transfers between devices  111 us (39%)
  Pallas kernels  31.3 us (11%)
  local copies, waits for them, and re-layouts  9.79 us (3%)
  other arithmetic  8.48 us (3%)
    ppermute x5, waiting for transfers between devices, shift(): return lax.ppermute(value, ALL, [(a, b) for a, b in pairs if to(*place(b))])  116 us
    ppermute x2, starting transfers between devices, around(): return lax.ppermute(value, ALL, [(d, target(d)) for d in range(count)])  71.3 us
    ppermute x4, starting transfers between devices, swap(): return lax.ppermute(value, ALL, [(d, d ^ bit) for d in range(count)])  23.8 us
    pallas_call x4, Pallas kernels, self_part(): pl.pallas_call(functools.partial(self_kernel, tuple(blocks), first, last,...  18.3 us
    ppermute x5, starting transfers between devices, shift(): return lax.ppermute(value, ALL, [(a, b) for a, b in pairs if to(*place(b))])  13.4 us
    pallas_call x2, Pallas kernels, cross_part(): pl.pallas_call(functools.partial(cross_kernel, rows // STRETCH, travels),...  10.1 us
    ppermute x1, waiting for transfers between devices, shards(): lax.ppermute(jnp.where(high == 0, kv2, kv4_far), ALL, [(d, (d - 2 - 4 * p...  7.87 us
  transfers between devices with their start and end apart: 12, of which 3 were waited for; matrix products, arithmetic and copies ran while one was open for 4% of the time, Pallas kernels for 11%

profile of v2, /device:TPU:29, one launch (start us, length us, event | category | flops | bytes accessed | tf_op | source)
XLA Modules:
  0.0 287.2 jit_solution(7608056969162182951)
XLA Ops:
  0.7 1.1 constant_dynamic-slice_fusion.4
  1.8 1.4 constant_dynamic-slice_fusion.2
  3.2 1.0 pad_maximum_fusion.2
  4.2 2.6 collective-permute-start
  6.7 15.4 %collective-permute-start.3 = (bf16[256,1024]{1,0:T(8,128)(2,1)}, bf16[256,1024]{1,0:T(8,128)(2,1)}, u32[]{:S(2)}, u32[]{:S(2)}) collective-permute-start(bf16[256,1024]{1,0:T(8,128)(2,1)} %q_ref.1), channel_id=1, source_target_pairs={{0,8},{4,12},{8,0},{12,4},{16,24},{20,28},{24,16},{28,20},{32,40},... | collective-permute-start | bytes 1572872 | tf_op jit(solution)/shard_map/ppermute | solution.py:33
  22.3 0.1 broadcast_remainder_fusion
  22.6 0.1 copy.27
  22.8 0.1 reduce
  22.9 0.1 select_reduce_fusion
  23.0 0.6 fusion
  23.6 0.1 copy.28
  23.7 0.1 copy.31
  23.9 0.1 copy.30
  24.1 0.1 copy.33
  24.3 0.1 copy.29
  24.4 0.1 ne.103
  24.5 0.1 copy.32
  26.0 0.1 stack.78.meta
  26.3 1.3 pad_maximum_fusion.refs_0_
  27.6 1.9 slice_bitcast_fusion.1
  29.5 1.1 pad_maximum_fusion.1.refs_1_.refs_2_
  30.6 2.6 collective-permute-start.2
  33.2 1.3 collective-permute-start.7
  34.5 1.9 collective-permute-start.1
  36.5 2.5 collective-permute-start.4
  39.0 1.0 pad_maximum_fusion.3.refs_0_
  40.0 0.1 broadcast_in_dim.24.refs_1_
  40.1 4.7 %shard_map.96 = (f32[512,512]{1,0:T(8,128)S(1)}, f32[4,512,128]{2,1,0:T(8,128)S(1)}, f32[4,512,128]{2,1,0:T(8,128)S(1)}) custom-call(s32[7]{0:T(128)S(1)} %stack.78.meta, bf16[512,512]{1,0:T(8,128)(2,1)S(1)} %pad_maximum_fusion.3.refs_0_, s32[512,128]{1,0:T(8,128)S(1)} %broadcast_in_dim.24.refs_1_, bf16[2,512,512]{2,1,0:T(8,128)(2,1)} %pad_maximum_fusion.1.refs_1_.refs_2_), custom_call_target="tpu_custom_call" | custom-call | flops 99999997952 | bytes 100000000 | tf_op jit(solution)/shard_map/pallas_call | solution.py:155
  44.8 4.6 %shard_map.97 = (f32[256,1024]{1,0:T(8,128)S(1)}, f32[16,256]{1,0:T(8,128)S(1)}) custom-call(s32[24]{0:T(128)S(1)} %pad_add_fusion.2.meta, bf16[256,1024]{1,0:T(8,128)(2,1)} %q_ref.1, bf16[3,128,1024]{2,1,0:T(8,128)(2,1)S(1)} %copy-done.2, bf16[3,128,1024]{2,1,0:T(8,128)(2,1)S(1)} %copy-done.3, bf16[2,3,128,1024]{3,2,1,0:T(8,128)(2,1)S(1)} %collective-permute-done.4.side, ...), custom_call_target="tpu_custom_call" | custom-call | flops 1 | bytes 1 | tf_op jit(solution)/shard_map/pallas_call | solution.py:246
  49.5 5.5 %shard_map.98.refs_8_ = bf16[272,1024]{1,0:T(8,128)(2,1)} custom-call(s32[24]{0:T(128)S(1)} %pad_add_fusion.1.meta, bf16[256,1024]{1,0:T(8,128)(2,1)} %collective-permute-done.3.q_ref, bf16[3,128,1024]{2,1,0:T(8,128)(2,1)S(1)} %copy-done.2, bf16[3,128,1024]{2,1,0:T(8,128)(2,1)S(1)} %copy-done.3, bf16[2,3,128,1024]{3,2,1,0:T(8,128)(2,1)S(1)} %collective-permute-done.4.side, ...), custom_call_target="tpu_custom_call" | custom-call | flops 1 | bytes 1 | tf_op jit(solution)/shard_map/pallas_call | solution.py:246
  55.0 18.9 %collective-permute-start.5 = (bf16[272,1024]{1,0:T(8,128)(2,1)}, bf16[272,1024]{1,0:T(8,128)(2,1)}, u32[]{:S(2)}, u32[]{:S(2)}) collective-permute-start(bf16[272,1024]{1,0:T(8,128)(2,1)} %shard_map.98.refs_8_), channel_id=1, source_target_pairs={{0,112},{4,116},{8,120},{12,124},{16,8},{20,12},{24,0},{28,4},{32,... | collective-permute-start | bytes 1671176 | tf_op jit(solution)/shard_map/ppermute | solution.py:44
  73.9 113.9 %collective-permute-done.2.refs_0_ = bf16[2,512,512]{2,1,0:T(8,128)(2,1)S(1)} collective-permute-done((bf16[2,512,512]{2,1,0:T(8,128)(2,1)}, bf16[2,512,512]{2,1,0:T(8,128)(2,1)S(1)}, u32[]{:S(2)}, u32[]{:S(2)}) %collective-permute-start.2) | collective-permute-done | bytes 1048608 | tf_op jit(solution)/shard_map/ppermute | solution.py:28
  187.8 1.0 copy-done
  188.8 6.3 %collective-permute-start.9 = (bf16[2,512,512]{2,1,0:T(8,128)(2,1)}, bf16[2,512,512]{2,1,0:T(8,128)(2,1)}, u32[]{:S(2)}, u32[]{:S(2)}) collective-permute-start(bf16[2,512,512]{2,1,0:T(8,128)(2,1)} %shard_map.99.refs_1_.refs_2_), channel_id=1, source_target_pairs={{0,16},{4,20},{8,24},{12,28},{16,32},{20,36},{24,40},{28,44},{32,4... | collective-permute-start | bytes 3145736 | tf_op jit(solution)/shard_map/ppermute | solution.py:28
  195.1 2.3 broadcast_select_fusion
  197.4 2.5 collective-permute-start.8
  199.9 1.3 collective-permute-start.6
  201.2 52.4 %collective-permute-start.11 = (bf16[272,1024]{1,0:T(8,128)(2,1)}, bf16[272,1024]{1,0:T(8,128)(2,1)}, u32[]{:S(2)}, u32[]{:S(2)}) collective-permute-start(bf16[272,1024]{1,0:T(8,128)(2,1)} %collective-permute-done.5.refs_1_), channel_id=1, source_target_pairs={{0,16},{4,20},{8,24},{12,28},{16,32},{20,36},{24,40},{28,44},{32,4... | collective-permute-start | bytes 1671176 | tf_op jit(solution)/shard_map/ppermute | solution.py:44
  253.6 1.2 copy-done.9
  254.8 1.2 copy-done.11
  256.0 5.6 %shard_map.101 = (f32[512,512]{1,0:T(8,128)S(1)}, f32[4,512,128]{2,1,0:T(8,128)S(1)}, f32[4,512,128]{2,1,0:T(8,128)S(1)}) custom-call(s32[7]{0:T(128)S(1)} %stack.78.meta, bf16[512,512]{1,0:T(8,128)(2,1)S(1)} %pad_maximum_fusion.3.refs_0_, s32[512,128]{1,0:T(8,128)S(1)} %broadcast_in_dim.24.refs_1_, bf16[2,512,512]{2,1,0:T(8,128)(2,1)S(1)} %copy-done.1, ...), custom_call_target="tpu_custom_call" | custom-call | flops 1 | bytes 1 | tf_op jit(solution)/shard_map/pallas_call | solution.py:155
  261.6 2.4 shard_map.102
  264.0 7.9 %collective-permute-done.8.refs_3_ = bf16[2,512,512]{2,1,0:T(8,128)(2,1)} collective-permute-done((bf16[2,512,512]{2,1,0:T(8,128)(2,1)}, bf16[2,512,512]{2,1,0:T(8,128)(2,1)}, u32[]{:S(2)}, u32[]{:S(2)}) %collective-permute-start.8) | collective-permute-done | bytes 1048608 | tf_op jit(solution)/shard_map/ppermute | solution.py:363
  271.8 2.5 collective-permute-done.6.refs_2_
  274.4 5.6 %shard_map.103 = (bf16[256,512]{1,0:T(8,128)(2,1)S(1)}, bf16[256,512]{1,0:T(8,128)(2,1)S(1)}) custom-call(s32[7]{0:T(128)S(1)} %stack.78.meta, bf16[512,512]{1,0:T(8,128)(2,1)S(1)} %pad_maximum_fusion.3.refs_0_, s32[512,128]{1,0:T(8,128)S(1)} %broadcast_in_dim.24.refs_1_, bf16[2,512,512]{2,1,0:T(8,128)(2,1)S(1)} %collective-permute-done.6.refs_2_, ...), custom_call_target="tpu_custom_call" | custom-call | flops 1 | bytes 1 | tf_op jit(solution)/shard_map/pallas_call | solution.py:155
  280.0 3.3 %collective-permute-start.10 = (bf16[256,512]{1,0:T(8,128)(2,1)S(1)}, bf16[256,512]{1,0:T(8,128)(2,1)S(1)}, u32[]{:S(2)}, u32[]{:S(2)}) collective-permute-start(bf16[256,512]{1,0:T(8,128)(2,1)S(1)} %get-tuple-element.26), channel_id=1, source_target_pairs={{0,4},{4,0},{8,12},{12,8},{16,20},{20,16},{24,28},{28,24},{32,36},... | collective-permute-start | bytes 786440 | tf_op jit(solution)/shard_map/ppermute | solution.py:33
  283.3 2.9 %shard_map.104 = bf16[256,1024]{1,0:T(8,128)(2,1)} custom-call(f32[256,1024]{1,0:T(8,128)S(1)} %copy-done.7, bf16[272,1024]{1,0:T(8,128)(2,1)} %collective-permute-done.11.ob_ref, f32[16,256]{1,0:T(8,128)S(1)} %get-tuple-element.16.refs_0_.sa_ref), custom_call_target="tpu_custom_call" | custom-call | flops 1 | bytes 1 | tf_op jit(solution)/shard_map/pallas_call | solution.py:284
  286.3 0.9 maximum_select_fusion
  (56 shorter events, 1.1 us)
Async XLA Ops:
  1.7 20.5 %copy-start.12 = (s32[512,2]{0,1:T(2,128)S(1)}, s32[512,2]{0,1:T(2,128)}, u32[]{:S(2)}) copy-start(s32[512,2]{0,1:T(2,128)} %param.14) | copy-start | bytes 12292
  1.7 20.9 %copy-start.13 = (s32[33]{0:T(128)S(1)}, s32[33]{0:T(128)}, u32[]{:S(2)}) copy-start(s32[33]{0:T(128)} %param.15) | copy-start | bytes 400
  1.8 24.5 %copy-start.2 = (bf16[3,128,1024]{2,1,0:T(8,128)(2,1)S(1)}, bf16[3,128,1024]{2,1,0:T(8,128)(2,1)}, u32[]{:S(2)}) copy-start(bf16[3,128,1024]{2,1,0:T(8,128)(2,1)} %k_here.3) | copy-start | bytes 2359300
  1.8 24.5 %copy-start.3 = (bf16[3,128,1024]{2,1,0:T(8,128)(2,1)S(1)}, bf16[3,128,1024]{2,1,0:T(8,128)(2,1)}, u32[]{:S(2)}) copy-start(bf16[3,128,1024]{2,1,0:T(8,128)(2,1)} %v_here.3) | copy-start | bytes 2359300
  4.2 23.4 %collective-permute-start = (bf16[3,256,512]{2,1,0:T(8,128)(2,1)}, bf16[3,256,512]{2,1,0:T(8,128)(2,1)}, u32[]{:S(2)}, u32[]{:S(2)}) collective-permute-start(bf16[3,256,512]{2,1,0:T(8,128)(2,1)} %pad_maximum_fusion.2), channel_id=1, source_target_pairs={{0,4},{4,0},{8,12},{12,8},{16,20},{20,16},{24,28},{28,24},{32,36},... | collective-permute-start | bytes 2359304 | tf_op jit(solution)/shard_map/ppermute | solution.py:33
  6.7 42.8 %collective-permute-start.3 = (bf16[256,1024]{1,0:T(8,128)(2,1)}, bf16[256,1024]{1,0:T(8,128)(2,1)}, u32[]{:S(2)}, u32[]{:S(2)}) collective-permute-start(bf16[256,1024]{1,0:T(8,128)(2,1)} %q_ref.1), channel_id=1, source_target_pairs={{0,8},{4,12},{8,0},{12,4},{16,24},{20,28},{24,16},{28,20},{32,40},... | collective-permute-start | bytes 1572872 | tf_op jit(solution)/shard_map/ppermute | solution.py:33
  30.6 157.2 %collective-permute-start.2 = (bf16[2,512,512]{2,1,0:T(8,128)(2,1)}, bf16[2,512,512]{2,1,0:T(8,128)(2,1)S(1)}, u32[]{:S(2)}, u32[]{:S(2)}) collective-permute-start(bf16[2,512,512]{2,1,0:T(8,128)(2,1)} %pad_maximum_fusion.1.refs_1_.refs_2_), channel_id=1, source_target_pairs={{0,16},{4,20},{8,24},{12,28},{16,32},{20,36},{24,40},{28,44},{32,4... | collective-permute-start | bytes 3145736 | tf_op jit(solution)/shard_map/ppermute | solution.py:28
  33.2 161.8 %collective-permute-start.7 = (bf16[2,512,512]{2,1,0:T(8,128)(2,1)}, bf16[2,512,512]{2,1,0:T(8,128)(2,1)}, u32[]{:S(2)}, u32[]{:S(2)}) collective-permute-start(bf16[2,512,512]{2,1,0:T(8,128)(2,1)} %pad_maximum_fusion.1.refs_1_.refs_2_), channel_id=1, source_target_pairs={{96,128},{100,132},{104,136},{108,140},{224,256},{228,260},{232,26... | collective-permute-start | bytes 3145736 | tf_op jit(solution)/shard_map/ppermute | solution.py:28
  34.5 165.3 %collective-permute-start.1 = (bf16[2,512,512]{2,1,0:T(8,128)(2,1)}, bf16[2,512,512]{2,1,0:T(8,128)(2,1)}, u32[]{:S(2)}, u32[]{:S(2)}) collective-permute-start(bf16[2,512,512]{2,1,0:T(8,128)(2,1)} %pad_maximum_fusion.1.refs_1_.refs_2_), channel_id=1, source_target_pairs={{0,24},{4,28},{8,32},{12,36},{16,40},{20,44},{24,48},{28,52},{32,5... | collective-permute-start | bytes 3145736 | tf_op jit(solution)/shard_map/ppermute | solution.py:28
  36.5 8.4 %collective-permute-start.4 = (bf16[2,3,128,1024]{3,2,1,0:T(8,128)(2,1)}, bf16[2,3,128,1024]{3,2,1,0:T(8,128)(2,1)S(1)}, u32[]{:S(2)}, u32[]{:S(2)}) collective-permute-start(bf16[2,3,128,1024]{3,2,1,0:T(8,128)(2,1)} %shard_map.95), channel_id=1, source_target_pairs={{0,4},{4,0},{8,12},{12,8},{16,20},{20,16},{24,28},{28,24},{32,36},... | collective-permute-start | bytes 4718600 | tf_op jit(solution)/shard_map/ppermute | solution.py:33
  44.8 4.7 %copy-start.4 = (f32[512,512]{1,0:T(8,128)}, f32[512,512]{1,0:T(8,128)S(1)}, u32[]{:S(2)}) copy-start(f32[512,512]{1,0:T(8,128)S(1)} %get-tuple-element.15.refs_0_.refs_5_) | copy-start | bytes 3145732
  44.8 4.7 %copy-start.8 = (f32[4,512,128]{2,1,0:T(8,128)}, f32[4,512,128]{2,1,0:T(8,128)S(1)}, u32[]{:S(2)}) copy-start(f32[4,512,128]{2,1,0:T(8,128)S(1)} %get-tuple-element.17.refs_6_) | copy-start | bytes 3145732
  44.8 4.7 %copy-start.10 = (f32[4,512,128]{2,1,0:T(8,128)}, f32[4,512,128]{2,1,0:T(8,128)S(1)}, u32[]{:S(2)}) copy-start(f32[4,512,128]{2,1,0:T(8,128)S(1)} %get-tuple-element.18.refs_7_) | copy-start | bytes 3145732
  49.5 5.5 %copy-start.6 = (f32[256,1024]{1,0:T(8,128)}, f32[256,1024]{1,0:T(8,128)S(1)}, u32[]{:S(2)}) copy-start(f32[256,1024]{1,0:T(8,128)S(1)} %get-tuple-element.27.oa_ref) | copy-start | bytes 3145732
  55.0 132.8 %collective-permute-start.5 = (bf16[272,1024]{1,0:T(8,128)(2,1)}, bf16[272,1024]{1,0:T(8,128)(2,1)}, u32[]{:S(2)}, u32[]{:S(2)}) collective-permute-start(bf16[272,1024]{1,0:T(8,128)(2,1)} %shard_map.98.refs_8_), channel_id=1, source_target_pairs={{0,112},{4,116},{8,120},{12,124},{16,8},{20,12},{24,0},{28,4},{32,... | collective-permute-start | bytes 1671176 | tf_op jit(solution)/shard_map/ppermute | solution.py:44
  187.8 1.0 copy-start
  188.8 64.8 %collective-permute-start.9 = (bf16[2,512,512]{2,1,0:T(8,128)(2,1)}, bf16[2,512,512]{2,1,0:T(8,128)(2,1)}, u32[]{:S(2)}, u32[]{:S(2)}) collective-permute-start(bf16[2,512,512]{2,1,0:T(8,128)(2,1)} %shard_map.99.refs_1_.refs_2_), channel_id=1, source_target_pairs={{0,16},{4,20},{8,24},{12,28},{16,32},{20,36},{24,40},{28,44},{32,4... | collective-permute-start | bytes 3145736 | tf_op jit(solution)/shard_map/ppermute | solution.py:28
  197.4 56.2 %copy-start.1 = (bf16[2,512,512]{2,1,0:T(8,128)(2,1)S(1)}, bf16[2,512,512]{2,1,0:T(8,128)(2,1)}, u32[]{:S(2)}) copy-start(bf16[2,512,512]{2,1,0:T(8,128)(2,1)} %shard_map.99.refs_1_.refs_2_) | copy-start | bytes 3145732
  197.4 56.2 %copy-start.5 = (f32[512,512]{1,0:T(8,128)S(1)}, f32[512,512]{1,0:T(8,128)}, u32[]{:S(2)}) copy-start(f32[512,512]{1,0:T(8,128)} %copy-done.4) | copy-start | bytes 3145732
  197.4 74.5 %collective-permute-start.8 = (bf16[2,512,512]{2,1,0:T(8,128)(2,1)}, bf16[2,512,512]{2,1,0:T(8,128)(2,1)}, u32[]{:S(2)}, u32[]{:S(2)}) collective-permute-start(bf16[2,512,512]{2,1,0:T(8,128)(2,1)} %broadcast_select_fusion), channel_id=1, source_target_pairs={{0,504},{4,508},{8,496},{12,500},{128,120},{132,124},{136,112},{14... | collective-permute-start | bytes 3145736 | tf_op jit(solution)/shard_map/ppermute | solution.py:363
  199.9 74.5 %collective-permute-start.6 = (bf16[2,512,512]{2,1,0:T(8,128)(2,1)}, bf16[2,512,512]{2,1,0:T(8,128)(2,1)S(1)}, u32[]{:S(2)}, u32[]{:S(2)}) collective-permute-start(bf16[2,512,512]{2,1,0:T(8,128)(2,1)} %shard_map.100.refs_2_), channel_id=1, source_target_pairs={{16,0},{20,4},{24,8},{28,12},{32,16},{36,20},{40,24},{44,28},{48,3... | collective-permute-start | bytes 3145736 | tf_op jit(solution)/shard_map/ppermute | solution.py:28
  201.2 82.2 %collective-permute-start.11 = (bf16[272,1024]{1,0:T(8,128)(2,1)}, bf16[272,1024]{1,0:T(8,128)(2,1)}, u32[]{:S(2)}, u32[]{:S(2)}) collective-permute-start(bf16[272,1024]{1,0:T(8,128)(2,1)} %collective-permute-done.5.refs_1_), channel_id=1, source_target_pairs={{0,16},{4,20},{8,24},{12,28},{16,32},{20,36},{24,40},{28,44},{32,4... | collective-permute-start | bytes 1671176 | tf_op jit(solution)/shard_map/ppermute | solution.py:44
  253.6 1.2 copy-start.9
  254.8 1.2 copy-start.11
  274.4 9.0 %copy-start.7 = (f32[256,1024]{1,0:T(8,128)S(1)}, f32[256,1024]{1,0:T(8,128)}, u32[]{:S(2)}) copy-start(f32[256,1024]{1,0:T(8,128)} %copy-done.6) | copy-start | bytes 3145732
  280.0 6.2 %collective-permute-start.10 = (bf16[256,512]{1,0:T(8,128)(2,1)S(1)}, bf16[256,512]{1,0:T(8,128)(2,1)S(1)}, u32[]{:S(2)}, u32[]{:S(2)}) collective-permute-start(bf16[256,512]{1,0:T(8,128)(2,1)S(1)} %get-tuple-element.26), channel_id=1, source_target_pairs={{0,4},{4,0},{8,12},{12,8},{16,20},{20,16},{24,28},{28,24},{32,36},... | collective-permute-start | bytes 786440 | tf_op jit(solution)/shard_map/ppermute | solution.py:33

commit v3 on v2

--- a/solution.py
+++ b/solution.py
@@ -14,6 +14,7 @@
 FLOOR = -1e29
 ALL = ("ctx", "nbr")
 RUN = 8
+MEDIUM = pl.CostEstimate(flops=1, bytes_accessed=10**7, transcendentals=0)
 SMALL = pl.CostEstimate(flops=1, bytes_accessed=1, transcendentals=0)
 LARGE = pl.CostEstimate(flops=10**11, bytes_accessed=10**8, transcendentals=0)
 
@@ -26,6 +27,12 @@
     count = lax.axis_size(ALL)
     pairs = [(d, (d + by) % count) for d in range(count)]
     return lax.ppermute(value, ALL, [(a, b) for a, b in pairs if to(*place(b))])
+
+
+def route(value, by):
+    count = lax.axis_size(ALL)
+    steps = [(d, by(*place(d))) for d in range(count)]
+    return lax.ppermute(value, ALL, [(d, (d + n) % count) for d, n in steps if n is not None])
 
 
 def swap(value, bit):
@@ -60,7 +67,8 @@
     refs = list(refs)
     q_ref = refs.pop(0)
     start_ref = refs.pop(0)
-    pairs = [refs.pop(0) for _ in blocks]
+    keys = [refs.pop(0) for _ in blocks]
+    values = [refs.pop(0) for _ in blocks]
     if not first:
         acc_in, top_in, total_in = refs.pop(0), refs.pop(0), refs.pop(0)
     refs = refs[skip:]
@@ -90,7 +98,7 @@
                 mine = pl.ds(qi * half, half)
                 scores = lax.dot_general(
                     q_ref[mine, :],
-                    pairs[bi][0],
+                    keys[bi][...],
                     (((1,), (1,)), ((), ())),
                     preferred_element_type=jnp.float32,
                 )
@@ -109,7 +117,7 @@
                     weights, axis=1, keepdims=True
                 )
                 acc[mine, :] = acc[mine, :] * factor + jnp.dot(
-                    weights.astype(jnp.bfloat16), pairs[bi][1], preferred_element_type=jnp.float32
+                    weights.astype(jnp.bfloat16), values[bi][...], preferred_element_type=jnp.float32
                 )
 
     if last:
@@ -122,15 +130,16 @@
     rows, width = queries.shape
     heads = width // HD
     column = pl.BlockSpec((rows, HD), lambda h: (0, h))
-    pair = pl.BlockSpec((2, rows, HD), lambda h: (0, 0, h))
+    layer = [pl.BlockSpec((None, rows, HD), lambda h, i=i: (i, 0, h)) for i in range(2)]
     stat = pl.BlockSpec((1, rows, HD), lambda h: (h, 0, 0))
     first = state is None
+    operands = [k for k, _ in pairs] + [v for _, v in pairs]
     in_specs = [
         pl.BlockSpec(memory_space=pltpu.SMEM),
         column,
         pl.BlockSpec((rows, HD), lambda h: (0, 0)),
-    ] + [pair] * len(blocks)
-    args = [meta, queries, starts, *pairs]
+    ] + [column if at is None else layer[at] for _, at in operands]
+    args = [meta, queries, starts] + [x for x, _ in operands]
     if not first:
         in_specs += [column, stat, stat]
         args += list(state)
@@ -256,7 +265,8 @@
     )(meta, queries, *pool, *after)
 
 
-def merge_kernel(oa_ref, ob_ref, sa_ref, out_ref):
+def merge_kernel(oa_ref, ob_ref, sa_ref, *refs):
+    out_ref = refs[-1]
     rows, width = oa_ref.shape
     heads = width // HD
     pieces = ob_ref[rows : rows + 2 * heads, : 3 * rows].astype(jnp.float32)
@@ -278,17 +288,17 @@
         ).astype(out_ref.dtype)
 
 
-def merge(oa, ob, sa):
+def merge(oa, ob, sa, after):
     rows, width = oa.shape
     vmem = pl.BlockSpec(memory_space=pltpu.VMEM)
     return pl.pallas_call(
         merge_kernel,
-        in_specs=[vmem] * 3,
+        in_specs=[vmem] * 3 + [pl.BlockSpec(memory_space=pl.ANY)] * len(after),
         out_specs=vmem,
         out_shape=jax.ShapeDtypeStruct((rows, width), jnp.bfloat16),
         compiler_params=pltpu.CompilerParams(vmem_limit_bytes=32 * 1024 * 1024),
         cost_estimate=SMALL,
-    )(oa, ob, sa)
+    )(oa, ob, sa, *after)
 
 
 def shards(
@@ -308,7 +318,7 @@
     zhi = (device // 2) % 2
     chip = device // 2
 
-    far_queries = swap(cross_queries, 2)
+    near_by = around(cross_queries, 1)
 
     def mine(x):
         return lax.dynamic_slice_in_dim(x, core * part, part, 1)
@@ -318,32 +328,49 @@
 
     trio = (self_keys, self_values, self_queries)
     beside = swap(jnp.stack([other(x) for x in trio]), 1)
-    kv0 = jnp.stack([jnp.concatenate([mine(x), beside[i]]) for i, x in enumerate(trio[:2])])
-    q0 = jnp.concatenate([mine(self_queries), beside[2]])
-    pool = held_back(jnp.stack([neighbour_keys, neighbour_values]), (kv0,))
-    pool_beside = swap(pool, 1)
+    k0, v0, q0 = (jnp.concatenate([mine(x), beside[i]]) for i, x in enumerate(trio))
+    pool_beside = swap(jnp.stack([neighbour_keys, neighbour_values]), 1)
+    kv0 = held_back(jnp.stack([k0, v0]), (pool_beside,))
 
     base = jnp.stack([chip * 2 * tokens + core * tokens, chip * 2 * tokens + (1 - core) * tokens])
     positions = (base[:, None] + jnp.arange(tokens, dtype=jnp.int32)[None, :]).reshape(-1)
     ends = jnp.cumsum(doc_lengths)
     starts = jnp.sum(jnp.where(ends[None, :] <= positions[:, None], doc_lengths[None, :], 0), axis=1)
     low, high = place(device)
-    flags = [low > 0, low == 0, low < RUN - 1, low == RUN - 1]
+    top = RUN - 1
+    flags = [
+        low > 0,
+        low == 0,
+        high == 0,
+        (high == 0) & (low < top),
+        (high == 1) & (low < top),
+        low == top,
+        (high == 1) & (low > 0),
+        (high == 1) & (low == 0),
+    ]
     self_meta = jnp.stack(
         [base[0], base[1], jnp.minimum(starts[0], starts[tokens]), *flags], dtype=jnp.int32
     )
     starts_wide = jnp.broadcast_to(starts[:, None], (2 * tokens, HD)).astype(jnp.int32)
 
     def attend(blocks, pairs, state, last=False, after=(), cost=SMALL):
-        return self_part(
-            self_meta, q0, starts_wide, blocks, pairs, state, last, after, cost
-        )
-
-    kv3 = shift(kv0, 6)
+        return self_part(self_meta, q0, starts_wide, blocks, pairs, state, last, after, cost)
+
+    def both(x):
+        return (x, 0), (x, 1)
+
+    k3 = shift(k0, 6)
+    v13 = route(
+        v0,
+        lambda low, high: None if (low, high) == (top, 0) else 2 if high == 0 else 6,
+    )
     kv2 = shift(kv0, 4)
     kv4_far = shift(kv0, 8, lambda low, high: low == 0)
 
-    state = attend(((0, 0),), (kv0,), None, cost=LARGE)
+    state = attend(((0, 0),), (both(kv0),), None, cost=LARGE)
+    far_queries = around(held_back(near_by, state[:1]), 7)
+    k3, v13 = (held_back(x, state[:1]) for x in (k3, v13))
+
     def pool_meta(owner):
         per = tokens // STRETCH
         ids = lax.dynamic_slice_in_dim(neighbour_table, owner * per, per, 0).reshape(-1)
@@ -352,41 +379,47 @@
 
     pool = (neighbour_keys, neighbour_values, pool_beside)
     near_sum, near_stat = cross_part(
-        pool_meta(device), cross_queries, pool, False, state[:1], SMALL
-    )
-    far_sum = cross_part(
-        pool_meta(device ^ 2), far_queries, pool, True, (near_stat,), SMALL
-    )
-    nearly = around(far_sum, 7)
-    kv2 = held_back(kv2, (nearly,))
+        pool_meta(device), cross_queries, pool, False, (state[0], k3, v13), MEDIUM
+    )
+    far_sum = cross_part(pool_meta(device ^ 2), far_queries, pool, True, (near_stat,), SMALL)
+    back_sum = swap(far_sum, 2)
+
+    kv2 = held_back(kv2, (far_sum,))
     kv4 = shift(kv2, 4, lambda low, high: low > 0)
-    kv1_edge = lax.ppermute(
-        jnp.where(high == 0, kv2, kv4_far),
-        ALL,
-        [
-            (d, (d - 2 - 4 * place(d)[1]) % lax.axis_size(ALL))
-            for d in range(lax.axis_size(ALL))
-            if place(d)[0] == 0
-        ],
+    edge = route(
+        jnp.where(low == top, kv0, jnp.where(high == 0, kv2, kv4_far)),
+        lambda low, high: 6 if (low, high) == (top, 0) else None if low else -2 - 4 * high,
+    )
+    k1 = shift(k3, -4, lambda low, high: low < top)
+    v31 = route(
+        v13,
+        lambda low, high: (4 if low < top else None) if high else (-4 if low > 0 else None),
     )
     state = attend(
         ((2, 0), (4, 1), (4, 2)),
-        (kv2, kv4, kv4_far),
+        (both(kv2), both(kv4), both(kv4_far)),
         state,
-        after=(far_sum,),
-    )
-    kv3 = held_back(kv3, (kv2,))
-    kv1 = shift(kv3, -4, lambda low, high: low < RUN - 1)
-    back_sum = around(nearly, 1)
-    state = attend(((3, 0),), (kv3,), state)
-    kept, sent = attend(((1, 3), (1, 4)), (kv1, kv1_edge), state, True)
+    )
+    state = attend(((3, 3),), (((k3, None), (v13, None)),), state)
+    cross_out = merge(near_sum, back_sum, near_stat, ())
+    kept, sent = attend(
+        ((1, 4), (1, 5), (1, 6), (3, 7), (3, 8)),
+        (
+            ((k1, None), (v31, None)),
+            ((k1, None), (v13, None)),
+            both(edge),
+            ((k3, None), (v31, None)),
+            ((k3, None), (edge, 1)),
+        ),
+        state,
+        True,
+    )
     returned = swap(sent, 1)
     self_out = jnp.where(
         core == 0,
         jnp.concatenate([kept, returned], axis=1),
         jnp.concatenate([returned, kept], axis=1),
     )
-    cross_out = merge(near_sum, back_sum, near_stat)
     return self_out, cross_out
 
 

time: 288 us -> 320 us (1.11)
  the two profiles are of different devices: /device:TPU:29 before, /device:TPU:125 now
where the time goes in v3:
time: 320 us; the launch traced here: 319 us
  starting transfers between devices  151 us (47%)
  waiting for transfers between devices  102 us (32%)
  Pallas kernels  37.5 us (12%)
  local copies, waits for them, and re-layouts  18.5 us (6%)
  other arithmetic  8.4 us (3%)
    ppermute x5, starting transfers between devices, shift(): return lax.ppermute(value, ALL, [(a, b) for a, b in pairs if to(*place(b))])  117 us
    ppermute x5, waiting for transfers between devices, shift(): return lax.ppermute(value, ALL, [(a, b) for a, b in pairs if to(*place(b))])  88.9 us
    pallas_call x4, Pallas kernels, self_part(): pl.pallas_call(functools.partial(self_kernel, tuple(blocks), first, last,...  24.8 us
    unnamed x59, local copies, waits for them, and re-layouts  14 us
    ppermute x3, starting transfers between devices, route(): lax.ppermute(value, ALL, [(d, (d + n) % count) for d, n in steps if n is...  13.3 us
    ppermute x3, waiting for transfers between devices, route(): lax.ppermute(value, ALL, [(d, (d + n) % count) for d, n in steps if n is...  12.7 us
    ppermute x4, starting transfers between devices, swap(): return lax.ppermute(value, ALL, [(d, d ^ bit) for d in range(count)])  11.4 us
    pallas_call x2, Pallas kernels, cross_part(): pl.pallas_call(functools.partial(cross_kernel, rows // STRETCH, travels),...  9.82 us
  transfers between devices with their start and end apart: 14, of which 3 were waited for; matrix products, arithmetic and copies ran while one was open for 3% of the time, Pallas kernels for 12%

profile of v3, /device:TPU:125, one launch (start us, length us, event | category | flops | bytes accessed | tf_op | source)
XLA Modules:
  0.0 319.4 jit_solution(8756241032486417128)
XLA Ops:
  0.7 1.1 constant_dynamic-slice_fusion.4
  1.8 1.4 constant_dynamic-slice_fusion.2
  3.1 1.0 pad_maximum_fusion.2
  4.1 2.6 collective-permute-start
  6.7 1.3 pad_maximum_fusion
  8.1 1.9 collective-permute-start.2
  10.0 4.8 %collective-permute-start.5 = (bf16[256,1024]{1,0:T(8,128)(2,1)}, bf16[256,1024]{1,0:T(8,128)(2,1)}, u32[]{:S(2)}, u32[]{:S(2)}) collective-permute-start(bf16[256,1024]{1,0:T(8,128)(2,1)} %q_ref.1), channel_id=1, source_target_pairs={{0,16},{4,20},{8,24},{12,28},{16,32},{20,36},{24,40},{28,44},{32,4... | collective-permute-start | bytes 1572872 | tf_op jit(solution)/shard_map/ppermute | solution.py:51
  15.3 0.6 fusion.2
  18.8 0.9 pad_maximum_fusion.5
  19.7 10.6 %collective-permute-start.7 = (bf16[512,512]{1,0:T(8,128)(2,1)}, bf16[512,512]{1,0:T(8,128)(2,1)S(1)}, u32[]{:S(2)}, u32[]{:S(2)}) collective-permute-start(bf16[512,512]{1,0:T(8,128)(2,1)} %get-tuple-element.35), channel_id=1, source_target_pairs={{0,8},{4,12},{8,32},{12,36},{16,24},{20,28},{24,48},{28,52},{32,40... | collective-permute-start | bytes 1572872 | tf_op jit(solution)/shard_map/ppermute | solution.py:35
  30.3 0.9 fusion.1
  31.2 3.5 %collective-permute-start.1 = (bf16[512,512]{1,0:T(8,128)(2,1)}, bf16[512,512]{1,0:T(8,128)(2,1)S(1)}, u32[]{:S(2)}, u32[]{:S(2)}) collective-permute-start(bf16[512,512]{1,0:T(8,128)(2,1)} %get-tuple-element.38), channel_id=1, source_target_pairs={{0,24},{4,28},{8,32},{12,36},{16,40},{20,44},{24,48},{28,52},{32,5... | collective-permute-start | bytes 1572872 | tf_op jit(solution)/shard_map/ppermute | solution.py:29
  34.8 1.2 pad_maximum_fusion.1.refs_0_
  35.9 1.2 copy-done.4
  37.1 6.0 %collective-permute-start.4 = (bf16[2,512,512]{2,1,0:T(8,128)(2,1)}, bf16[2,512,512]{2,1,0:T(8,128)(2,1)S(1)}, u32[]{:S(2)}, u32[]{:S(2)}) collective-permute-start(bf16[2,512,512]{2,1,0:T(8,128)(2,1)} %shard_map.95.refs_2_.refs_3_), channel_id=1, source_target_pairs={{0,16},{4,20},{8,24},{12,28},{16,32},{20,36},{24,40},{28,44},{32,4... | collective-permute-start | bytes 3145736 | tf_op jit(solution)/shard_map/ppermute | solution.py:29
  43.1 1.6 collective-permute-start.8
  44.7 0.1 broadcast_in_dim.24.refs_1_
  44.9 1.2 copy-done.9
  46.1 4.4 %shard_map.96 = (f32[512,512]{1,0:T(8,128)S(1)}, f32[4,512,128]{2,1,0:T(8,128)S(1)}, f32[4,512,128]{2,1,0:T(8,128)S(1)}) custom-call(s32[11]{0:T(128)S(1)} %stack.110.meta, bf16[512,512]{1,0:T(8,128)(2,1)S(1)} %pad_maximum_fusion.3.refs_0_, s32[512,128]{1,0:T(8,128)S(1)} %broadcast_in_dim.24.refs_1_, bf16[2,512,512]{2,1,0:T(8,128)(2,1)S(1)} %copy-done.9, ...), custom_call_target="tpu_custom_call" | custom-call | flops 99999997952 | bytes 100000000 | tf_op jit(solution)/shard_map/pallas_call | solution.py:164
  50.5 1.0 copy-done
  51.5 1.0 copy-done.21
  52.5 1.0 copy-done.23
  53.5 4.6 %collective-permute-start.6 = (bf16[256,1024]{1,0:T(8,128)(2,1)}, bf16[256,1024]{1,0:T(8,128)(2,1)}, u32[]{:S(2)}, u32[]{:S(2)}) collective-permute-start(bf16[256,1024]{1,0:T(8,128)(2,1)} %shard_map.98), channel_id=1, source_target_pairs={{0,112},{4,116},{8,120},{12,124},{16,8},{20,12},{24,0},{28,4},{32,... | collective-permute-start | bytes 1572872 | tf_op jit(solution)/shard_map/ppermute | solution.py:51
  58.1 12.7 %collective-permute-done.7.refs_0_ = bf16[512,512]{1,0:T(8,128)(2,1)S(1)} collective-permute-done((bf16[512,512]{1,0:T(8,128)(2,1)}, bf16[512,512]{1,0:T(8,128)(2,1)S(1)}, u32[]{:S(2)}, u32[]{:S(2)}) %collective-permute-start.7) | collective-permute-done | bytes 524320 | tf_op jit(solution)/shard_map/ppermute | solution.py:35
  70.8 0.8 copy-done.12
  71.6 28.5 %collective-permute-done.1.refs_0_ = bf16[512,512]{1,0:T(8,128)(2,1)S(1)} collective-permute-done((bf16[512,512]{1,0:T(8,128)(2,1)}, bf16[512,512]{1,0:T(8,128)(2,1)S(1)}, u32[]{:S(2)}, u32[]{:S(2)}) %collective-permute-start.1) | collective-permute-done | bytes 524320 | tf_op jit(solution)/shard_map/ppermute | solution.py:29
  100.2 0.8 copy-done.6
  101.0 1.4 copy-done.5
  102.4 1.0 copy-done.7
  103.5 1.1 copy-done.16
  104.6 1.1 copy-done.19
  105.7 4.4 %shard_map.100 = (f32[256,1024]{1,0:T(8,128)S(1)}, f32[16,256]{1,0:T(8,128)S(1)}) custom-call(s32[24]{0:T(128)S(1)} %pad_add_fusion.2.meta, bf16[256,1024]{1,0:T(8,128)(2,1)} %q_ref.1, bf16[3,128,1024]{2,1,0:T(8,128)(2,1)S(1)} %copy-done.19, bf16[3,128,1024]{2,1,0:T(8,128)(2,1)S(1)} %copy-done.16, bf16[2,3,128,1024]{3,2,1,0:T(8,128)(2,1)S(1)} %copy-done.5, ...), custom_call_target="tpu_custom_call" | custom-call | flops 1 | bytes 10000000 | tf_op jit(solution)/shard_map/pallas_call | solution.py:255
  110.1 5.5 %shard_map.101.refs_1_ = bf16[272,1024]{1,0:T(8,128)(2,1)} custom-call(s32[24]{0:T(128)S(1)} %pad_add_fusion.1.meta, bf16[256,1024]{1,0:T(8,128)(2,1)} %collective-permute-done.6.q_ref, bf16[3,128,1024]{2,1,0:T(8,128)(2,1)S(1)} %copy-done.20, bf16[3,128,1024]{2,1,0:T(8,128)(2,1)S(1)} %copy-done.17, bf16[2,3,128,1024]{3,2,1,0:T(8,128)(2,1)S(1)} %copy-done.5, ...), custom_call_target="tpu_custom_call" | custom-call | flops 1 | bytes 1 | tf_op jit(solution)/shard_map/pallas_call | solution.py:255
  115.6 1.0 copy-done.2
  116.6 103.8 %collective-permute-start.11 = (bf16[2,512,512]{2,1,0:T(8,128)(2,1)}, bf16[2,512,512]{2,1,0:T(8,128)(2,1)S(1)}, u32[]{:S(2)}, u32[]{:S(2)}) collective-permute-start(bf16[2,512,512]{2,1,0:T(8,128)(2,1)} %shard_map.102.refs_2_.refs_5_), channel_id=1, source_target_pairs={{0,16},{4,20},{8,24},{12,28},{16,32},{20,36},{24,40},{28,44},{32,4... | collective-permute-start | bytes 3145736 | tf_op jit(solution)/shard_map/ppermute | solution.py:29
  220.5 1.4 select_select_fusion
  221.9 0.7 collective-permute-start.9
  222.6 1.9 collective-permute-start.10
  224.6 1.9 collective-permute-start.3
  226.5 2.3 collective-permute-start.13
  228.8 60.3 %collective-permute-done.11.refs_3_.refs_6_ = bf16[2,512,512]{2,1,0:T(8,128)(2,1)S(1)} collective-permute-done((bf16[2,512,512]{2,1,0:T(8,128)(2,1)}, bf16[2,512,512]{2,1,0:T(8,128)(2,1)S(1)}, u32[]{:S(2)}, u32[]{:S(2)}) %collective-permute-start.11) | collective-permute-done | bytes 1048608 | tf_op jit(solution)/shard_map/ppermute | solution.py:29
  289.2 1.2 copy-done.24
  290.4 9.3 %shard_map.103 = (f32[512,512]{1,0:T(8,128)S(1)}, f32[4,512,128]{2,1,0:T(8,128)S(1)}, f32[4,512,128]{2,1,0:T(8,128)S(1)}) custom-call(s32[11]{0:T(128)S(1)} %stack.110.meta, bf16[512,512]{1,0:T(8,128)(2,1)S(1)} %copy-done.11, s32[512,128]{1,0:T(8,128)S(1)} %broadcast_in_dim.24.refs_1_, bf16[2,512,512]{2,1,0:T(8,128)(2,1)S(1)} %copy-done.3, ...), custom_call_target="tpu_custom_call" | custom-call | flops 1 | bytes 1 | tf_op jit(solution)/shard_map/pallas_call | solution.py:164
  299.7 5.0 %shard_map.104 = (f32[512,512]{1,0:T(8,128)S(1)}, f32[4,512,128]{2,1,0:T(8,128)S(1)}, f32[4,512,128]{2,1,0:T(8,128)S(1)}) custom-call(s32[11]{0:T(128)S(1)} %stack.110.meta, bf16[512,512]{1,0:T(8,128)(2,1)S(1)} %copy-done.11, s32[512,128]{1,0:T(8,128)S(1)} %broadcast_in_dim.24.refs_1_, bf16[512,512]{1,0:T(8,128)(2,1)S(1)} %copy-done.8, ...), custom_call_target="tpu_custom_call" | custom-call | flops 1 | bytes 1 | tf_op jit(solution)/shard_map/pallas_call | solution.py:164
  304.8 6.0 %shard_map.105 = (bf16[256,512]{1,0:T(8,128)(2,1)S(1)}, bf16[256,512]{1,0:T(8,128)(2,1)S(1)}) custom-call(s32[11]{0:T(128)S(1)} %stack.110.meta, bf16[512,512]{1,0:T(8,128)(2,1)S(1)} %copy-done.11, s32[512,128]{1,0:T(8,128)S(1)} %broadcast_in_dim.24.refs_1_, bf16[512,512]{1,0:T(8,128)(2,1)S(1)} %collective-permute-done.3.refs_2_.refs_3_, ...), custom_call_target="tpu_custom_call" | custom-call | flops 1 | bytes 1 | tf_op jit(solution)/shard_map/pallas_call | solution.py:164
  310.9 4.6 %collective-permute-start.12 = (bf16[256,512]{1,0:T(8,128)(2,1)S(1)}, bf16[256,512]{1,0:T(8,128)(2,1)S(1)}, u32[]{:S(2)}, u32[]{:S(2)}) collective-permute-start(bf16[256,512]{1,0:T(8,128)(2,1)S(1)} %get-tuple-element.26), channel_id=1, source_target_pairs={{0,4},{4,0},{8,12},{12,8},{16,20},{20,16},{24,28},{28,24},{32,36},... | collective-permute-start | bytes 786440 | tf_op jit(solution)/shard_map/ppermute | solution.py:40
  315.5 2.9 shard_map.106
  318.4 0.9 maximum_select_fusion
  (92 shorter events, 2.3 us)
Async XLA Ops:
  1.7 5.0 %copy-start.15 = (bf16[3,128,1024]{2,1,0:T(8,128)(2,1)S(1)}, bf16[3,128,1024]{2,1,0:T(8,128)(2,1)}, u32[]{:S(2)}) copy-start(bf16[3,128,1024]{2,1,0:T(8,128)(2,1)} %v_here.3) | copy-start | bytes 2359300
  1.7 5.0 %copy-start.18 = (bf16[3,128,1024]{2,1,0:T(8,128)(2,1)S(1)}, bf16[3,128,1024]{2,1,0:T(8,128)(2,1)}, u32[]{:S(2)}) copy-start(bf16[3,128,1024]{2,1,0:T(8,128)(2,1)} %k_here.3) | copy-start | bytes 2359300
  4.1 14.6 %collective-permute-start = (bf16[3,256,512]{2,1,0:T(8,128)(2,1)}, bf16[3,256,512]{2,1,0:T(8,128)(2,1)S(1)}, u32[]{:S(2)}, u32[]{:S(2)}) collective-permute-start(bf16[3,256,512]{2,1,0:T(8,128)(2,1)} %pad_maximum_fusion.2), channel_id=1, source_target_pairs={{0,4},{4,0},{8,12},{12,8},{16,20},{20,16},{24,28},{28,24},{32,36},... | collective-permute-start | bytes 2359304 | tf_op jit(solution)/shard_map/ppermute | solution.py:40
  6.7 8.2 %copy-start.28 = (s32[33]{0:T(128)S(1)}, s32[33]{0:T(128)}, u32[]{:S(2)}) copy-start(s32[33]{0:T(128)} %param.15) | copy-start | bytes 400
  6.7 9.2 %copy-start.27 = (s32[512,2]{0,1:T(2,128)S(1)}, s32[512,2]{0,1:T(2,128)}, u32[]{:S(2)}) copy-start(s32[512,2]{0,1:T(2,128)} %param.14) | copy-start | bytes 12292
  8.1 27.9 %collective-permute-start.2 = (bf16[2,3,128,1024]{3,2,1,0:T(8,128)(2,1)}, bf16[2,3,128,1024]{3,2,1,0:T(8,128)(2,1)S(1)}, u32[]{:S(2)}, u32[]{:S(2)}) collective-permute-start(bf16[2,3,128,1024]{3,2,1,0:T(8,128)(2,1)} %pad_maximum_fusion), channel_id=1, source_target_pairs={{0,4},{4,0},{8,12},{12,8},{16,20},{20,16},{24,28},{28,24},{32,36},... | collective-permute-start | bytes 4718600 | tf_op jit(solution)/shard_map/ppermute | solution.py:40
  10.0 43.5 %collective-permute-start.5 = (bf16[256,1024]{1,0:T(8,128)(2,1)}, bf16[256,1024]{1,0:T(8,128)(2,1)}, u32[]{:S(2)}, u32[]{:S(2)}) collective-permute-start(bf16[256,1024]{1,0:T(8,128)(2,1)} %q_ref.1), channel_id=1, source_target_pairs={{0,16},{4,20},{8,24},{12,28},{16,32},{20,36},{24,40},{28,44},{32,4... | collective-permute-start | bytes 1572872 | tf_op jit(solution)/shard_map/ppermute | solution.py:51
  19.7 51.1 %collective-permute-start.7 = (bf16[512,512]{1,0:T(8,128)(2,1)}, bf16[512,512]{1,0:T(8,128)(2,1)S(1)}, u32[]{:S(2)}, u32[]{:S(2)}) collective-permute-start(bf16[512,512]{1,0:T(8,128)(2,1)} %get-tuple-element.35), channel_id=1, source_target_pairs={{0,8},{4,12},{8,32},{12,36},{16,24},{20,28},{24,48},{28,52},{32,40... | collective-permute-start | bytes 1572872 | tf_op jit(solution)/shard_map/ppermute | solution.py:35
  31.2 68.9 %collective-permute-start.1 = (bf16[512,512]{1,0:T(8,128)(2,1)}, bf16[512,512]{1,0:T(8,128)(2,1)S(1)}, u32[]{:S(2)}, u32[]{:S(2)}) collective-permute-start(bf16[512,512]{1,0:T(8,128)(2,1)} %get-tuple-element.38), channel_id=1, source_target_pairs={{0,24},{4,28},{8,32},{12,36},{16,40},{20,44},{24,48},{28,52},{32,5... | collective-permute-start | bytes 1572872 | tf_op jit(solution)/shard_map/ppermute | solution.py:29
  34.8 10.1 %copy-start.10 = (bf16[512,512]{1,0:T(8,128)(2,1)}, bf16[512,512]{1,0:T(8,128)(2,1)S(1)}, u32[]{:S(2)}) copy-start(bf16[512,512]{1,0:T(8,128)(2,1)S(1)} %pad_maximum_fusion.3.refs_0_) | copy-start | bytes 1572868
  35.9 1.2 copy-start.4
  37.1 78.5 %collective-permute-start.4 = (bf16[2,512,512]{2,1,0:T(8,128)(2,1)}, bf16[2,512,512]{2,1,0:T(8,128)(2,1)S(1)}, u32[]{:S(2)}, u32[]{:S(2)}) collective-permute-start(bf16[2,512,512]{2,1,0:T(8,128)(2,1)} %shard_map.95.refs_2_.refs_3_), channel_id=1, source_target_pairs={{0,16},{4,20},{8,24},{12,28},{16,32},{20,36},{24,40},{28,44},{32,4... | collective-permute-start | bytes 3145736 | tf_op jit(solution)/shard_map/ppermute | solution.py:29
  43.1 177.4 %collective-permute-start.8 = (bf16[2,512,512]{2,1,0:T(8,128)(2,1)}, bf16[2,512,512]{2,1,0:T(8,128)(2,1)}, u32[]{:S(2)}, u32[]{:S(2)}) collective-permute-start(bf16[2,512,512]{2,1,0:T(8,128)(2,1)} %shard_map.95.refs_2_.refs_3_), channel_id=1, source_target_pairs={{96,128},{100,132},{104,136},{108,140},{224,256},{228,260},{232,26... | collective-permute-start | bytes 3145736 | tf_op jit(solution)/shard_map/ppermute | solution.py:29
  44.8 1.2 copy-start.9
  50.5 1.0 copy-start
  51.5 1.0 copy-start.21
  52.5 1.0 copy-start.23
  53.5 56.6 %collective-permute-start.6 = (bf16[256,1024]{1,0:T(8,128)(2,1)}, bf16[256,1024]{1,0:T(8,128)(2,1)}, u32[]{:S(2)}, u32[]{:S(2)}) collective-permute-start(bf16[256,1024]{1,0:T(8,128)(2,1)} %shard_map.98), channel_id=1, source_target_pairs={{0,112},{4,116},{8,120},{12,124},{16,8},{20,12},{24,0},{28,4},{32,... | collective-permute-start | bytes 1572872 | tf_op jit(solution)/shard_map/ppermute | solution.py:51
  70.8 0.8 copy-start.12
  71.6 29.4 %copy-start.1 = (f32[512,512]{1,0:T(8,128)S(1)}, f32[512,512]{1,0:T(8,128)}, u32[]{:S(2)}) copy-start(f32[512,512]{1,0:T(8,128)} %copy-done) | copy-start | bytes 3145732
  71.6 29.4 %copy-start.13 = (bf16[512,512]{1,0:T(8,128)(2,1)S(1)}, bf16[512,512]{1,0:T(8,128)(2,1)}, u32[]{:S(2)}) copy-start(bf16[512,512]{1,0:T(8,128)(2,1)} %shard_map.99.refs_2_.refs_3_.refs_8_) | copy-start | bytes 1572868
  100.1 0.8 copy-start.6
  101.0 1.4 copy-start.5
  102.4 1.0 copy-start.7
  103.5 1.1 copy-start.16
  104.6 1.1 copy-start.19
  105.7 4.4 %copy-start.17 = (bf16[3,128,1024]{2,1,0:T(8,128)(2,1)S(1)}, bf16[3,128,1024]{2,1,0:T(8,128)(2,1)}, u32[]{:S(2)}) copy-start(bf16[3,128,1024]{2,1,0:T(8,128)(2,1)} %v_here.3) | copy-start | bytes 2359300
  105.7 4.4 %copy-start.20 = (bf16[3,128,1024]{2,1,0:T(8,128)(2,1)S(1)}, bf16[3,128,1024]{2,1,0:T(8,128)(2,1)}, u32[]{:S(2)}) copy-start(bf16[3,128,1024]{2,1,0:T(8,128)(2,1)} %k_here.3) | copy-start | bytes 2359300
  110.1 5.5 %copy-start.25 = (f32[256,1024]{1,0:T(8,128)}, f32[256,1024]{1,0:T(8,128)S(1)}, u32[]{:S(2)}) copy-start(f32[256,1024]{1,0:T(8,128)S(1)} %get-tuple-element.27.oa_ref) | copy-start | bytes 3145732
  115.6 1.0 copy-start.2
  116.6 106.0 %copy-start.14 = (bf16[512,512]{1,0:T(8,128)(2,1)S(1)}, bf16[512,512]{1,0:T(8,128)(2,1)}, u32[]{:S(2)}) copy-start(bf16[512,512]{1,0:T(8,128)(2,1)} %shard_map.99.refs_2_.refs_3_.refs_8_) | copy-start | bytes 1572868
  116.6 107.9 %copy-start.8 = (bf16[512,512]{1,0:T(8,128)(2,1)S(1)}, bf16[512,512]{1,0:T(8,128)(2,1)}, u32[]{:S(2)}) copy-start(bf16[512,512]{1,0:T(8,128)(2,1)} %shard_map.97.refs_1_.refs_2_.refs_5_.refs_6_) | copy-start | bytes 1572868
  116.6 172.6 %copy-start.3 = (bf16[2,512,512]{2,1,0:T(8,128)(2,1)S(1)}, bf16[2,512,512]{2,1,0:T(8,128)(2,1)}, u32[]{:S(2)}) copy-start(bf16[2,512,512]{2,1,0:T(8,128)(2,1)} %shard_map.102.refs_2_.refs_5_) | copy-start | bytes 3145732
  116.6 172.6 %copy-start.11 = (bf16[512,512]{1,0:T(8,128)(2,1)S(1)}, bf16[512,512]{1,0:T(8,128)(2,1)}, u32[]{:S(2)}) copy-start(bf16[512,512]{1,0:T(8,128)(2,1)} %copy-done.10) | copy-start | bytes 1572868
  116.6 172.6 %copy-start.22 = (f32[4,512,128]{2,1,0:T(8,128)S(1)}, f32[4,512,128]{2,1,0:T(8,128)}, u32[]{:S(2)}) copy-start(f32[4,512,128]{2,1,0:T(8,128)} %copy-done.21) | copy-start | bytes 3145732
  116.6 172.5 %collective-permute-start.11 = (bf16[2,512,512]{2,1,0:T(8,128)(2,1)}, bf16[2,512,512]{2,1,0:T(8,128)(2,1)S(1)}, u32[]{:S(2)}, u32[]{:S(2)}) collective-permute-start(bf16[2,512,512]{2,1,0:T(8,128)(2,1)} %shard_map.102.refs_2_.refs_5_), channel_id=1, source_target_pairs={{0,16},{4,20},{8,24},{12,28},{16,32},{20,36},{24,40},{28,44},{32,4... | collective-permute-start | bytes 3145736 | tf_op jit(solution)/shard_map/ppermute | solution.py:29
  221.9 82.9 %collective-permute-start.9 = (bf16[2,512,512]{2,1,0:T(8,128)(2,1)S(1)}, bf16[2,512,512]{2,1,0:T(8,128)(2,1)S(1)}, u32[]{:S(2)}, u32[]{:S(2)}) collective-permute-start(bf16[2,512,512]{2,1,0:T(8,128)(2,1)S(1)} %select_select_fusion), channel_id=1, source_target_pairs={{0,504},{4,508},{8,496},{12,500},{112,136},{116,140},{128,120},{13... | collective-permute-start | bytes 3145736 | tf_op jit(solution)/shard_map/ppermute | solution.py:35
  222.6 82.1 %collective-permute-start.10 = (bf16[512,512]{1,0:T(8,128)(2,1)S(1)}, bf16[512,512]{1,0:T(8,128)(2,1)S(1)}, u32[]{:S(2)}, u32[]{:S(2)}) collective-permute-start(bf16[512,512]{1,0:T(8,128)(2,1)S(1)} %copy-done.14), channel_id=1, source_target_pairs={{8,24},{12,28},{16,0},{20,4},{24,40},{28,44},{32,16},{36,20},{40,5... | collective-permute-start | bytes 1572872 | tf_op jit(solution)/shard_map/ppermute | solution.py:35
  224.6 80.2 %collective-permute-start.3 = (bf16[512,512]{1,0:T(8,128)(2,1)S(1)}, bf16[512,512]{1,0:T(8,128)(2,1)S(1)}, u32[]{:S(2)}, u32[]{:S(2)}) collective-permute-start(bf16[512,512]{1,0:T(8,128)(2,1)S(1)} %copy-done.8), channel_id=1, source_target_pairs={{16,0},{20,4},{24,8},{28,12},{32,16},{36,20},{40,24},{44,28},{48,3... | collective-permute-start | bytes 1572872 | tf_op jit(solution)/shard_map/ppermute | solution.py:29
  226.5 89.0 %collective-permute-start.13 = (bf16[272,1024]{1,0:T(8,128)(2,1)}, bf16[272,1024]{1,0:T(8,128)(2,1)}, u32[]{:S(2)}, u32[]{:S(2)}) collective-permute-start(bf16[272,1024]{1,0:T(8,128)(2,1)} %shard_map.101.refs_1_), channel_id=1, source_target_pairs={{0,8},{4,12},{8,0},{12,4},{16,24},{20,28},{24,16},{28,20},{32,40},... | collective-permute-start | bytes 1671176 | tf_op jit(solution)/shard_map/ppermute | solution.py:40
  289.2 1.2 copy-start.24
  304.8 10.7 %copy-start.26 = (f32[256,1024]{1,0:T(8,128)S(1)}, f32[256,1024]{1,0:T(8,128)}, u32[]{:S(2)}) copy-start(f32[256,1024]{1,0:T(8,128)} %copy-done.25) | copy-start | bytes 3145732
  310.9 7.6 %collective-permute-start.12 = (bf16[256,512]{1,0:T(8,128)(2,1)S(1)}, bf16[256,512]{1,0:T(8,128)(2,1)S(1)}, u32[]{:S(2)}, u32[]{:S(2)}) collective-permute-start(bf16[256,512]{1,0:T(8,128)(2,1)S(1)} %get-tuple-element.26), channel_id=1, source_target_pairs={{0,4},{4,0},{8,12},{12,8},{16,20},{20,16},{24,28},{28,24},{32,36},... | collective-permute-start | bytes 786440 | tf_op jit(solution)/shard_map/ppermute | solution.py:40

commit v4 on v2

--- a/solution.py
+++ b/solution.py
@@ -308,7 +308,6 @@
     zhi = (device // 2) % 2
     chip = device // 2
 
-    far_queries = swap(cross_queries, 2)
 
     def mine(x):
         return lax.dynamic_slice_in_dim(x, core * part, part, 1)
@@ -328,7 +327,8 @@
     ends = jnp.cumsum(doc_lengths)
     starts = jnp.sum(jnp.where(ends[None, :] <= positions[:, None], doc_lengths[None, :], 0), axis=1)
     low, high = place(device)
-    flags = [low > 0, low == 0, low < RUN - 1, low == RUN - 1]
+    first_a, first_b = (low == 0) & (high == 0), (low == 0) & (high == 1)
+    flags = [low > 0, first_b, first_a, low < RUN - 1, low == RUN - 1]
     self_meta = jnp.stack(
         [base[0], base[1], jnp.minimum(starts[0], starts[tokens]), *flags], dtype=jnp.int32
     )
@@ -339,11 +339,14 @@
             self_meta, q0, starts_wide, blocks, pairs, state, last, after, cost
         )
 
+    far_queries = around(cross_queries, 1)
+
     kv3 = shift(kv0, 6)
     kv2 = shift(kv0, 4)
-    kv4_far = shift(kv0, 8, lambda low, high: low == 0)
+    kv4_far = shift(kv0, 8, lambda low, high: low == 0 and high == 1)
 
     state = attend(((0, 0),), (kv0,), None, cost=LARGE)
+    far_queries = around(held_back(far_queries, state[:1]), 7)
     def pool_meta(owner):
         per = tokens // STRETCH
         ids = lax.dynamic_slice_in_dim(neighbour_table, owner * per, per, 0).reshape(-1)
@@ -357,8 +360,8 @@
     far_sum = cross_part(
         pool_meta(device ^ 2), far_queries, pool, True, (near_stat,), SMALL
     )
-    nearly = around(far_sum, 7)
-    kv2 = held_back(kv2, (nearly,))
+    back_sum = swap(far_sum, 2)
+    kv2 = held_back(kv2, (far_sum,))
     kv4 = shift(kv2, 4, lambda low, high: low > 0)
     kv1_edge = lax.ppermute(
         jnp.where(high == 0, kv2, kv4_far),
@@ -377,9 +380,9 @@
     )
     kv3 = held_back(kv3, (kv2,))
     kv1 = shift(kv3, -4, lambda low, high: low < RUN - 1)
-    back_sum = around(nearly, 1)
+    kv4_last = shift(kv3, 2, lambda low, high: low == 0 and high == 0)
     state = attend(((3, 0),), (kv3,), state)
-    kept, sent = attend(((1, 3), (1, 4)), (kv1, kv1_edge), state, True)
+    kept, sent = attend(((4, 3), (1, 4), (1, 5)), (kv4_last, kv1, kv1_edge), state, True)
     returned = swap(sent, 1)
     self_out = jnp.where(
         core == 0,

time: 288 us -> 288 us (level)
  the two profiles are of different devices: /device:TPU:29 before, /device:TPU:32 now
where the time goes in v4:
time: 288 us; the launch traced here: 287 us
  waiting for transfers between devices  165 us (57%)
  starting transfers between devices  65.4 us (23%)
  Pallas kernels  27.9 us (10%)
  local copies, waits for them, and re-layouts  18.2 us (6%)
  other arithmetic  7.69 us (3%)
    ppermute x6, waiting for transfers between devices, shift(): return lax.ppermute(value, ALL, [(a, b) for a, b in pairs if to(*place(b))])  108 us
    ppermute x2, waiting for transfers between devices, around(): return lax.ppermute(value, ALL, [(d, target(d)) for d in range(count)])  45.7 us
    ppermute x6, starting transfers between devices, shift(): return lax.ppermute(value, ALL, [(a, b) for a, b in pairs if to(*place(b))])  39.9 us
    ppermute x4, starting transfers between devices, swap(): return lax.ppermute(value, ALL, [(d, d ^ bit) for d in range(count)])  17 us
    pallas_call x4, Pallas kernels, self_part(): pl.pallas_call(functools.partial(self_kernel, tuple(blocks), first, last,...  15.7 us
    ppermute x4, waiting for transfers between devices, swap(): return lax.ppermute(value, ALL, [(d, d ^ bit) for d in range(count)])  11.5 us
    unnamed x49, local copies, waits for them, and re-layouts  10.4 us
    pallas_call x2, Pallas kernels, cross_part(): pl.pallas_call(functools.partial(cross_kernel, rows // STRETCH, travels),...  9.21 us
  transfers between devices with their start and end apart: 13, of which 4 were waited for; matrix products, arithmetic and copies ran while one was open for 3% of the time, Pallas kernels for 10%

profile of v4, /device:TPU:32, one launch (start us, length us, event | category | flops | bytes accessed | tf_op | source)
XLA Modules:
  0.0 286.5 jit_solution(15504696777649974510)
XLA Ops:
  0.7 1.8 constant_dynamic-slice_fusion.4
  2.5 2.1 constant_dynamic-slice_fusion.2
  4.6 1.0 pad_maximum_fusion.2
  5.6 1.9 collective-permute-start
  7.5 3.8 %collective-permute-start.3 = (bf16[256,1024]{1,0:T(8,128)(2,1)S(1)}, bf16[256,1024]{1,0:T(8,128)(2,1)}, u32[]{:S(2)}, u32[]{:S(2)}) collective-permute-start(bf16[256,1024]{1,0:T(8,128)(2,1)S(1)} %copy-done.17), channel_id=1, source_target_pairs={{0,16},{4,20},{8,24},{12,28},{16,32},{20,36},{24,40},{28,44},{32,4... | collective-permute-start | bytes 1572872 | tf_op jit(solution)/shard_map/ppermute | solution.py:44
  11.8 0.1 copy.28
  11.9 0.1 reduce
  12.8 0.1 copy.30
  13.0 0.1 copy.33
  13.3 0.6 fusion
  15.3 1.4 pad_maximum_fusion.refs_0_
  16.7 1.9 slice_bitcast_fusion.1
  18.7 1.1 pad_maximum_fusion.1.refs_2_.refs_1_
  19.7 3.9 %collective-permute-start.2 = (bf16[2,512,512]{2,1,0:T(8,128)(2,1)}, bf16[2,512,512]{2,1,0:T(8,128)(2,1)S(1)}, u32[]{:S(2)}, u32[]{:S(2)}) collective-permute-start(bf16[2,512,512]{2,1,0:T(8,128)(2,1)} %pad_maximum_fusion.1.refs_2_.refs_1_), channel_id=1, source_target_pairs={{0,16},{4,20},{8,24},{12,28},{16,32},{20,36},{24,40},{28,44},{32,4... | collective-permute-start | bytes 3145736 | tf_op jit(solution)/shard_map/ppermute | solution.py:28
  23.7 1.7 collective-permute-start.8
  25.4 12.6 %collective-permute-start.1 = (bf16[2,512,512]{2,1,0:T(8,128)(2,1)}, bf16[2,512,512]{2,1,0:T(8,128)(2,1)}, u32[]{:S(2)}, u32[]{:S(2)}) collective-permute-start(bf16[2,512,512]{2,1,0:T(8,128)(2,1)} %pad_maximum_fusion.1.refs_2_.refs_1_), channel_id=1, source_target_pairs={{0,24},{4,28},{8,32},{12,36},{16,40},{20,44},{24,48},{28,52},{32,5... | collective-permute-start | bytes 3145736 | tf_op jit(solution)/shard_map/ppermute | solution.py:28
  37.9 1.9 collective-permute-start.5
  39.9 0.1 broadcast_in_dim.24.refs_1_
  40.1 4.8 %shard_map.95 = (f32[512,512]{1,0:T(8,128)S(1)}, f32[4,512,128]{2,1,0:T(8,128)S(1)}, f32[4,512,128]{2,1,0:T(8,128)S(1)}) custom-call(s32[8]{0:T(128)S(1)} %stack.86.meta, bf16[512,512]{1,0:T(8,128)(2,1)S(1)} %pad_maximum_fusion.3.refs_0_, s32[512,128]{1,0:T(8,128)S(1)} %broadcast_in_dim.24.refs_1_, bf16[2,512,512]{2,1,0:T(8,128)(2,1)} %pad_maximum_fusion.1.refs_2_.refs_1_), custom_call_target="tpu_custom_call" | custom-call | flops 99999997952 | bytes 100000000 | tf_op jit(solution)/shard_map/pallas_call | solution.py:155
  44.9 1.0 copy-done.2
  45.8 1.0 copy-done.13
  46.8 1.0 copy-done.15
  47.8 2.9 %collective-permute-start.4 = (bf16[256,1024]{1,0:T(8,128)(2,1)}, bf16[256,1024]{1,0:T(8,128)(2,1)S(1)}, u32[]{:S(2)}, u32[]{:S(2)}) collective-permute-start(bf16[256,1024]{1,0:T(8,128)(2,1)} %shard_map.96), channel_id=1, source_target_pairs={{0,112},{4,116},{8,120},{12,124},{16,8},{20,12},{24,0},{28,4},{32,... | collective-permute-start | bytes 1572872 | tf_op jit(solution)/shard_map/ppermute | solution.py:44
  50.8 1.1 copy-done.6
  52.0 1.0 copy-done.18
  53.0 4.6 %shard_map.98 = (f32[256,1024]{1,0:T(8,128)S(1)}, f32[16,256]{1,0:T(8,128)S(1)}) custom-call(s32[24]{0:T(128)S(1)} %pad_add_fusion.2.meta, bf16[256,1024]{1,0:T(8,128)(2,1)S(1)} %copy-done.18, bf16[3,128,1024]{2,1,0:T(8,128)(2,1)S(1)} %copy-done.4, bf16[3,128,1024]{2,1,0:T(8,128)(2,1)S(1)} %copy-done.6, ...), custom_call_target="tpu_custom_call" | custom-call | flops 1 | bytes 1 | tf_op jit(solution)/shard_map/pallas_call | solution.py:246
  57.6 1.0 copy-done.11
  58.6 45.7 %collective-permute-done.4.q_ref = bf16[256,1024]{1,0:T(8,128)(2,1)S(1)} collective-permute-done((bf16[256,1024]{1,0:T(8,128)(2,1)}, bf16[256,1024]{1,0:T(8,128)(2,1)S(1)}, u32[]{:S(2)}, u32[]{:S(2)}) %collective-permute-start.4) | collective-permute-done | bytes 524320 | tf_op jit(solution)/shard_map/ppermute | solution.py:44
  104.3 4.6 %shard_map.99.refs_1_.refs_8_ = bf16[272,1024]{1,0:T(8,128)(2,1)S(1)} custom-call(s32[24]{0:T(128)S(1)} %pad_add_fusion.1.meta, bf16[256,1024]{1,0:T(8,128)(2,1)S(1)} %collective-permute-done.4.q_ref, bf16[3,128,1024]{2,1,0:T(8,128)(2,1)S(1)} %copy-done.4, bf16[3,128,1024]{2,1,0:T(8,128)(2,1)S(1)} %copy-done.6, ...), custom_call_target="tpu_custom_call" | custom-call | flops 1 | bytes 1 | tf_op jit(solution)/shard_map/pallas_call | solution.py:246
  108.9 0.8 copy-done.7
  109.7 1.0 copy-done
  110.7 9.5 %collective-permute-start.10 = (bf16[2,512,512]{2,1,0:T(8,128)(2,1)}, bf16[2,512,512]{2,1,0:T(8,128)(2,1)}, u32[]{:S(2)}, u32[]{:S(2)}) collective-permute-start(bf16[2,512,512]{2,1,0:T(8,128)(2,1)} %shard_map.100.refs_1_.refs_2_), channel_id=1, source_target_pairs={{0,16},{4,20},{8,24},{12,28},{16,32},{20,36},{24,40},{28,44},{32,4... | collective-permute-start | bytes 3145736 | tf_op jit(solution)/shard_map/ppermute | solution.py:28
  120.2 2.4 broadcast_select_fusion
  122.7 1.8 collective-permute-start.9
  124.5 67.0 %collective-permute-done.1.refs_0_ = bf16[2,512,512]{2,1,0:T(8,128)(2,1)} collective-permute-done((bf16[2,512,512]{2,1,0:T(8,128)(2,1)}, bf16[2,512,512]{2,1,0:T(8,128)(2,1)}, u32[]{:S(2)}, u32[]{:S(2)}) %collective-permute-start.1) | collective-permute-done | bytes 1048608 | tf_op jit(solution)/shard_map/ppermute | solution.py:28
  191.5 0.7 collective-permute-start.6
  192.2 11.4 %collective-permute-start.7 = (bf16[2,512,512]{2,1,0:T(8,128)(2,1)}, bf16[2,512,512]{2,1,0:T(8,128)(2,1)S(1)}, u32[]{:S(2)}, u32[]{:S(2)}) collective-permute-start(bf16[2,512,512]{2,1,0:T(8,128)(2,1)} %shard_map.101.refs_2_), channel_id=1, source_target_pairs={{16,0},{20,4},{24,8},{28,12},{32,16},{36,20},{40,24},{44,28},{48,3... | collective-permute-start | bytes 3145736 | tf_op jit(solution)/shard_map/ppermute | solution.py:28
  203.7 11.3 %collective-permute-start.12 = (bf16[272,1024]{1,0:T(8,128)(2,1)S(1)}, bf16[272,1024]{1,0:T(8,128)(2,1)}, u32[]{:S(2)}, u32[]{:S(2)}) collective-permute-start(bf16[272,1024]{1,0:T(8,128)(2,1)S(1)} %copy-done.8), channel_id=1, source_target_pairs={{0,8},{4,12},{8,0},{12,4},{16,24},{20,28},{24,16},{28,20},{32,40},... | collective-permute-start | bytes 1671176 | tf_op jit(solution)/shard_map/ppermute | solution.py:33
  215.0 1.2 copy-done.14
  216.2 1.2 copy-done.16
  217.4 2.8 shard_map.102
  220.2 2.4 shard_map.103
  222.6 40.8 %collective-permute-done.7.refs_3_ = bf16[2,512,512]{2,1,0:T(8,128)(2,1)S(1)} collective-permute-done((bf16[2,512,512]{2,1,0:T(8,128)(2,1)}, bf16[2,512,512]{2,1,0:T(8,128)(2,1)S(1)}, u32[]{:S(2)}, u32[]{:S(2)}) %collective-permute-start.7) | collective-permute-done | bytes 1048608 | tf_op jit(solution)/shard_map/ppermute | solution.py:28
  263.4 5.8 %shard_map.104 = (bf16[256,512]{1,0:T(8,128)(2,1)S(1)}, bf16[256,512]{1,0:T(8,128)(2,1)S(1)}) custom-call(s32[8]{0:T(128)S(1)} %stack.86.meta, bf16[512,512]{1,0:T(8,128)(2,1)S(1)} %pad_maximum_fusion.3.refs_0_, s32[512,128]{1,0:T(8,128)S(1)} %copy-done.10, bf16[2,512,512]{2,1,0:T(8,128)(2,1)S(1)} %collective-permute-done.6.refs_2_, ...), custom_call_target="tpu_custom_call" | custom-call | flops 1 | bytes 1 | tf_op jit(solution)/shard_map/pallas_call | solution.py:155
  269.2 1.9 collective-permute-start.11
  271.1 11.5 %collective-permute-done.12.ob_ref = bf16[272,1024]{1,0:T(8,128)(2,1)} collective-permute-done((bf16[272,1024]{1,0:T(8,128)(2,1)S(1)}, bf16[272,1024]{1,0:T(8,128)(2,1)}, u32[]{:S(2)}, u32[]{:S(2)}) %collective-permute-start.12) | collective-permute-done | bytes 557088 | tf_op jit(solution)/shard_map/ppermute | solution.py:33
  282.7 2.9 %shard_map.105 = bf16[256,1024]{1,0:T(8,128)(2,1)} custom-call(f32[256,1024]{1,0:T(8,128)S(1)} %copy-done.12, bf16[272,1024]{1,0:T(8,128)(2,1)} %collective-permute-done.12.ob_ref, f32[16,256]{1,0:T(8,128)S(1)} %get-tuple-element.16.refs_0_.sa_ref), custom_call_target="tpu_custom_call" | custom-call | flops 1 | bytes 1 | tf_op jit(solution)/shard_map/pallas_call | solution.py:284
  285.6 0.9 maximum_select_fusion
  (79 shorter events, 1.9 us)
Async XLA Ops:
  2.4 5.1 %copy-start.17 = (bf16[256,1024]{1,0:T(8,128)(2,1)S(1)}, bf16[256,1024]{1,0:T(8,128)(2,1)}, u32[]{:S(2)}) copy-start(bf16[256,1024]{1,0:T(8,128)(2,1)} %q_ref.1) | copy-start | bytes 1572868
  2.4 9.0 %copy-start.22 = (s32[512,2]{0,1:T(2,128)S(1)}, s32[512,2]{0,1:T(2,128)}, u32[]{:S(2)}) copy-start(s32[512,2]{0,1:T(2,128)} %param.14) | copy-start | bytes 12292
  2.4 9.3 %copy-start.23 = (s32[33]{0:T(128)S(1)}, s32[33]{0:T(128)}, u32[]{:S(2)}) copy-start(s32[33]{0:T(128)} %param.15) | copy-start | bytes 400
  2.4 12.8 %copy-start.4 = (bf16[3,128,1024]{2,1,0:T(8,128)(2,1)S(1)}, bf16[3,128,1024]{2,1,0:T(8,128)(2,1)}, u32[]{:S(2)}) copy-start(bf16[3,128,1024]{2,1,0:T(8,128)(2,1)} %k_here.3) | copy-start | bytes 2359300
  2.4 12.8 %copy-start.5 = (bf16[3,128,1024]{2,1,0:T(8,128)(2,1)S(1)}, bf16[3,128,1024]{2,1,0:T(8,128)(2,1)}, u32[]{:S(2)}) copy-start(bf16[3,128,1024]{2,1,0:T(8,128)(2,1)} %v_here.3) | copy-start | bytes 2359300
  5.6 11.1 %collective-permute-start = (bf16[3,256,512]{2,1,0:T(8,128)(2,1)}, bf16[3,256,512]{2,1,0:T(8,128)(2,1)}, u32[]{:S(2)}, u32[]{:S(2)}) collective-permute-start(bf16[3,256,512]{2,1,0:T(8,128)(2,1)} %pad_maximum_fusion.2), channel_id=1, source_target_pairs={{0,4},{4,0},{8,12},{12,8},{16,20},{20,16},{24,28},{28,24},{32,36},... | collective-permute-start | bytes 2359304 | tf_op jit(solution)/shard_map/ppermute | solution.py:33
  7.5 40.3 %collective-permute-start.3 = (bf16[256,1024]{1,0:T(8,128)(2,1)S(1)}, bf16[256,1024]{1,0:T(8,128)(2,1)}, u32[]{:S(2)}, u32[]{:S(2)}) collective-permute-start(bf16[256,1024]{1,0:T(8,128)(2,1)S(1)} %copy-done.17), channel_id=1, source_target_pairs={{0,16},{4,20},{8,24},{12,28},{16,32},{20,36},{24,40},{28,44},{32,4... | collective-permute-start | bytes 1572872 | tf_op jit(solution)/shard_map/ppermute | solution.py:44
  16.7 1.9 copy-start.21
  19.7 20.1 %copy-start.19 = (bf16[256,512]{1,0:T(8,128)(2,1)S(1)}, bf16[256,512]{1,0:T(8,128)(2,1)}, u32[]{:S(2)}) copy-start(bf16[256,512]{1,0:T(8,128)(2,1)} %get-tuple-element.39) | copy-start | bytes 786436
  19.7 20.1 %copy-start.20 = (bf16[256,512]{1,0:T(8,128)(2,1)S(1)}, bf16[256,512]{1,0:T(8,128)(2,1)}, u32[]{:S(2)}) copy-start(bf16[256,512]{1,0:T(8,128)(2,1)} %get-tuple-element.34) | copy-start | bytes 786436
  19.7 89.9 %collective-permute-start.2 = (bf16[2,512,512]{2,1,0:T(8,128)(2,1)}, bf16[2,512,512]{2,1,0:T(8,128)(2,1)S(1)}, u32[]{:S(2)}, u32[]{:S(2)}) collective-permute-start(bf16[2,512,512]{2,1,0:T(8,128)(2,1)} %pad_maximum_fusion.1.refs_2_.refs_1_), channel_id=1, source_target_pairs={{0,16},{4,20},{8,24},{12,28},{16,32},{20,36},{24,40},{28,44},{32,4... | collective-permute-start | bytes 3145736 | tf_op jit(solution)/shard_map/ppermute | solution.py:28
  23.7 96.5 %collective-permute-start.8 = (bf16[2,512,512]{2,1,0:T(8,128)(2,1)}, bf16[2,512,512]{2,1,0:T(8,128)(2,1)}, u32[]{:S(2)}, u32[]{:S(2)}) collective-permute-start(bf16[2,512,512]{2,1,0:T(8,128)(2,1)} %pad_maximum_fusion.1.refs_2_.refs_1_), channel_id=1, source_target_pairs={{104,136},{108,140},{232,264},{236,268},{360,392},{364,396},{488,8... | collective-permute-start | bytes 3145736 | tf_op jit(solution)/shard_map/ppermute | solution.py:28
  25.4 166.1 %collective-permute-start.1 = (bf16[2,512,512]{2,1,0:T(8,128)(2,1)}, bf16[2,512,512]{2,1,0:T(8,128)(2,1)}, u32[]{:S(2)}, u32[]{:S(2)}) collective-permute-start(bf16[2,512,512]{2,1,0:T(8,128)(2,1)} %pad_maximum_fusion.1.refs_2_.refs_1_), channel_id=1, source_target_pairs={{0,24},{4,28},{8,32},{12,36},{16,40},{20,44},{24,48},{28,52},{32,5... | collective-permute-start | bytes 3145736 | tf_op jit(solution)/shard_map/ppermute | solution.py:28
  37.9 12.9 %collective-permute-start.5 = (bf16[2,3,128,1024]{3,2,1,0:T(8,128)(2,1)}, bf16[2,3,128,1024]{3,2,1,0:T(8,128)(2,1)}, u32[]{:S(2)}, u32[]{:S(2)}) collective-permute-start(bf16[2,3,128,1024]{3,2,1,0:T(8,128)(2,1)} %shard_map.97), channel_id=1, source_target_pairs={{0,4},{4,0},{8,12},{12,8},{16,20},{20,16},{24,28},{28,24},{32,36},... | collective-permute-start | bytes 4718600 | tf_op jit(solution)/shard_map/ppermute | solution.py:33
  40.1 4.8 %copy-start.9 = (s32[512,128]{1,0:T(8,128)}, s32[512,128]{1,0:T(8,128)S(1)}, u32[]{:S(2)}) copy-start(s32[512,128]{1,0:T(8,128)S(1)} %broadcast_in_dim.24.refs_1_) | copy-start | bytes 786436
  44.9 1.0 copy-start.2
  45.8 1.0 copy-start.13
  46.8 1.0 copy-start.15
  47.8 3.0 %copy-start.3 = (f32[512,512]{1,0:T(8,128)S(1)}, f32[512,512]{1,0:T(8,128)}, u32[]{:S(2)}) copy-start(f32[512,512]{1,0:T(8,128)} %copy-done.2) | copy-start | bytes 3145732
  47.8 56.4 %collective-permute-start.4 = (bf16[256,1024]{1,0:T(8,128)(2,1)}, bf16[256,1024]{1,0:T(8,128)(2,1)S(1)}, u32[]{:S(2)}, u32[]{:S(2)}) collective-permute-start(bf16[256,1024]{1,0:T(8,128)(2,1)} %shard_map.96), channel_id=1, source_target_pairs={{0,112},{4,116},{8,120},{12,124},{16,8},{20,12},{24,0},{28,4},{32,... | collective-permute-start | bytes 1572872 | tf_op jit(solution)/shard_map/ppermute | solution.py:44
  50.8 1.1 copy-start.6
  52.0 1.0 copy-start.18
  57.6 1.0 copy-start.11
  108.9 0.8 copy-start.7
  109.7 1.0 copy-start
  110.7 104.3 %collective-permute-start.10 = (bf16[2,512,512]{2,1,0:T(8,128)(2,1)}, bf16[2,512,512]{2,1,0:T(8,128)(2,1)}, u32[]{:S(2)}, u32[]{:S(2)}) collective-permute-start(bf16[2,512,512]{2,1,0:T(8,128)(2,1)} %shard_map.100.refs_1_.refs_2_), channel_id=1, source_target_pairs={{0,16},{4,20},{8,24},{12,28},{16,32},{20,36},{24,40},{28,44},{32,4... | collective-permute-start | bytes 3145736 | tf_op jit(solution)/shard_map/ppermute | solution.py:28
  122.7 81.0 %copy-start.8 = (bf16[272,1024]{1,0:T(8,128)(2,1)S(1)}, bf16[272,1024]{1,0:T(8,128)(2,1)}, u32[]{:S(2)}) copy-start(bf16[272,1024]{1,0:T(8,128)(2,1)} %copy-done.7) | copy-start | bytes 1671172
  122.7 92.3 %copy-start.1 = (bf16[2,512,512]{2,1,0:T(8,128)(2,1)S(1)}, bf16[2,512,512]{2,1,0:T(8,128)(2,1)}, u32[]{:S(2)}) copy-start(bf16[2,512,512]{2,1,0:T(8,128)(2,1)} %shard_map.100.refs_1_.refs_2_) | copy-start | bytes 3145732
  122.7 92.3 %copy-start.10 = (s32[512,128]{1,0:T(8,128)S(1)}, s32[512,128]{1,0:T(8,128)}, u32[]{:S(2)}) copy-start(s32[512,128]{1,0:T(8,128)} %copy-done.9) | copy-start | bytes 786436
  122.7 99.9 %collective-permute-start.9 = (bf16[2,512,512]{2,1,0:T(8,128)(2,1)}, bf16[2,512,512]{2,1,0:T(8,128)(2,1)}, u32[]{:S(2)}, u32[]{:S(2)}) collective-permute-start(bf16[2,512,512]{2,1,0:T(8,128)(2,1)} %broadcast_select_fusion), channel_id=1, source_target_pairs={{0,504},{4,508},{8,496},{12,500},{128,120},{132,124},{136,112},{14... | collective-permute-start | bytes 3145736 | tf_op jit(solution)/shard_map/ppermute | solution.py:366
  191.5 31.1 %collective-permute-start.6 = (bf16[2,512,512]{2,1,0:T(8,128)(2,1)}, bf16[2,512,512]{2,1,0:T(8,128)(2,1)S(1)}, u32[]{:S(2)}, u32[]{:S(2)}) collective-permute-start(bf16[2,512,512]{2,1,0:T(8,128)(2,1)} %shard_map.101.refs_2_), channel_id=1, source_target_pairs={{120,128},{124,132},{248,256},{252,260},{376,384},{380,388},{504,0... | collective-permute-start | bytes 3145736 | tf_op jit(solution)/shard_map/ppermute | solution.py:28
  192.2 71.2 %collective-permute-start.7 = (bf16[2,512,512]{2,1,0:T(8,128)(2,1)}, bf16[2,512,512]{2,1,0:T(8,128)(2,1)S(1)}, u32[]{:S(2)}, u32[]{:S(2)}) collective-permute-start(bf16[2,512,512]{2,1,0:T(8,128)(2,1)} %shard_map.101.refs_2_), channel_id=1, source_target_pairs={{16,0},{20,4},{24,8},{28,12},{32,16},{36,20},{40,24},{44,28},{48,3... | collective-permute-start | bytes 3145736 | tf_op jit(solution)/shard_map/ppermute | solution.py:28
  203.7 79.0 %collective-permute-start.12 = (bf16[272,1024]{1,0:T(8,128)(2,1)S(1)}, bf16[272,1024]{1,0:T(8,128)(2,1)}, u32[]{:S(2)}, u32[]{:S(2)}) collective-permute-start(bf16[272,1024]{1,0:T(8,128)(2,1)S(1)} %copy-done.8), channel_id=1, source_target_pairs={{0,8},{4,12},{8,0},{12,4},{16,24},{20,28},{24,16},{28,20},{32,40},... | collective-permute-start | bytes 1671176 | tf_op jit(solution)/shard_map/ppermute | solution.py:33
  215.0 1.2 copy-start.14
  216.2 1.2 copy-start.16
  263.4 19.3 %copy-start.12 = (f32[256,1024]{1,0:T(8,128)S(1)}, f32[256,1024]{1,0:T(8,128)}, u32[]{:S(2)}) copy-start(f32[256,1024]{1,0:T(8,128)} %copy-done.11) | copy-start | bytes 3145732
  269.2 16.4 %collective-permute-start.11 = (bf16[256,512]{1,0:T(8,128)(2,1)S(1)}, bf16[256,512]{1,0:T(8,128)(2,1)S(1)}, u32[]{:S(2)}, u32[]{:S(2)}) collective-permute-start(bf16[256,512]{1,0:T(8,128)(2,1)S(1)} %get-tuple-element.26), channel_id=1, source_target_pairs={{0,4},{4,0},{8,12},{12,8},{16,20},{20,16},{24,28},{28,24},{32,36},... | collective-permute-start | bytes 786440 | tf_op jit(solution)/shard_map/ppermute | solution.py:33

commit v5 on v2

--- a/solution.py
+++ b/solution.py
@@ -54,6 +54,62 @@
         input_output_aliases={0: 0},
         cost_estimate=SMALL,
     )(value, *after)
+
+
+def cut_kernel(core, a_ref, b_ref, c_ref, out_ref):
+    out_ref[0] = a_ref[...]
+    out_ref[1] = b_ref[...]
+    out_ref[2] = c_ref[...]
+
+
+def cut(core, arrays):
+    rows, width = arrays[0].shape
+    part = width // 2
+    return pl.pallas_call(
+        cut_kernel,
+        grid_spec=pltpu.PrefetchScalarGridSpec(
+            num_scalar_prefetch=1,
+            grid=(1,),
+            in_specs=[pl.BlockSpec((rows, part), lambda i, c: (0, 1 - c[0]))] * 3,
+            out_specs=pl.BlockSpec((3, rows, part), lambda i, c: (0, 0, 0)),
+        ),
+        out_shape=jax.ShapeDtypeStruct((3, rows, part), arrays[0].dtype),
+        cost_estimate=SMALL,
+    )(core, *arrays)
+
+
+def join_kernel(core, a_ref, b_ref, c_ref, beside_ref, pair_ref, single_ref):
+    rows = a_ref.shape[0]
+    for i, ref in enumerate((a_ref, b_ref)):
+        pair_ref[i, :rows] = ref[...]
+        pair_ref[i, rows:] = beside_ref[i]
+    single_ref[:rows] = c_ref[...]
+    single_ref[rows:] = beside_ref[2]
+
+
+def join(core, arrays, beside):
+    rows, width = arrays[0].shape
+    part = width // 2
+    dtype = arrays[0].dtype
+    return pl.pallas_call(
+        join_kernel,
+        grid_spec=pltpu.PrefetchScalarGridSpec(
+            num_scalar_prefetch=1,
+            grid=(1,),
+            in_specs=[pl.BlockSpec((rows, part), lambda i, c: (0, c[0]))] * 3
+            + [pl.BlockSpec((3, rows, part), lambda i, c: (0, 0, 0))],
+            out_specs=(
+                pl.BlockSpec((2, 2 * rows, part), lambda i, c: (0, 0, 0)),
+                pl.BlockSpec((2 * rows, part), lambda i, c: (0, 0)),
+            ),
+        ),
+        out_shape=(
+            jax.ShapeDtypeStruct((2, 2 * rows, part), dtype),
+            jax.ShapeDtypeStruct((2 * rows, part), dtype),
+        ),
+        compiler_params=pltpu.CompilerParams(vmem_limit_bytes=32 * 1024 * 1024),
+        cost_estimate=SMALL,
+    )(core, *arrays, beside)
 
 
 def self_kernel(blocks, first, last, skip, meta, *refs):
@@ -310,16 +366,10 @@
 
     far_queries = swap(cross_queries, 2)
 
-    def mine(x):
-        return lax.dynamic_slice_in_dim(x, core * part, part, 1)
-
-    def other(x):
-        return lax.dynamic_slice_in_dim(x, (1 - core) * part, part, 1)
-
+    which = core.astype(jnp.int32).reshape(1)
     trio = (self_keys, self_values, self_queries)
-    beside = swap(jnp.stack([other(x) for x in trio]), 1)
-    kv0 = jnp.stack([jnp.concatenate([mine(x), beside[i]]) for i, x in enumerate(trio[:2])])
-    q0 = jnp.concatenate([mine(self_queries), beside[2]])
+    beside = swap(cut(which, trio), 1)
+    kv0, q0 = join(which, trio, beside)
     pool = held_back(jnp.stack([neighbour_keys, neighbour_values]), (kv0,))
     pool_beside = swap(pool, 1)
 
@@ -328,7 +378,13 @@
     ends = jnp.cumsum(doc_lengths)
     starts = jnp.sum(jnp.where(ends[None, :] <= positions[:, None], doc_lengths[None, :], 0), axis=1)
     low, high = place(device)
-    flags = [low > 0, low == 0, low < RUN - 1, low == RUN - 1]
+    flags = [
+        low > 0,
+        (low == 0) & (high == 1),
+        (low == 0) & (high == 0),
+        low < RUN - 1,
+        low == RUN - 1,
+    ]
     self_meta = jnp.stack(
         [base[0], base[1], jnp.minimum(starts[0], starts[tokens]), *flags], dtype=jnp.int32
     )
@@ -341,7 +397,7 @@
 
     kv3 = shift(kv0, 6)
     kv2 = shift(kv0, 4)
-    kv4_far = shift(kv0, 8, lambda low, high: low == 0)
+    kv4_far = shift(kv0, 8, lambda low, high: low == 0 and high == 1)
 
     state = attend(((0, 0),), (kv0,), None, cost=LARGE)
     def pool_meta(owner):
@@ -369,17 +425,13 @@
             if place(d)[0] == 0
         ],
     )
-    state = attend(
-        ((2, 0), (4, 1), (4, 2)),
-        (kv2, kv4, kv4_far),
-        state,
-        after=(far_sum,),
-    )
-    kv3 = held_back(kv3, (kv2,))
+    state = attend(((2, 0),), (kv2,), state)
+    kv3 = held_back(kv3, (kv2, state[0]))
     kv1 = shift(kv3, -4, lambda low, high: low < RUN - 1)
+    kv4_last = shift(kv3, 2, lambda low, high: low == 0 and high == 0)
     back_sum = around(nearly, 1)
-    state = attend(((3, 0),), (kv3,), state)
-    kept, sent = attend(((1, 3), (1, 4)), (kv1, kv1_edge), state, True)
+    state = attend(((4, 1), (4, 2), (3, 0)), (kv4, kv4_far, kv3), state)
+    kept, sent = attend(((4, 3), (1, 4), (1, 5)), (kv4_last, kv1, kv1_edge), state, True)
     returned = swap(sent, 1)
     self_out = jnp.where(
         core == 0,

time: 288 us -> 267 us (0.927)
  the two profiles are of different devices: /device:TPU:29 before, /device:TPU:101 now
where the time goes in v5:
time: 267 us; the launch traced here: 265 us
  waiting for transfers between devices  133 us (50%)
  starting transfers between devices  76.7 us (29%)
  Pallas kernels  35.8 us (13%)
  local copies, waits for them, and re-layouts  11.3 us (4%)
  other arithmetic  5.41 us (2%)
    ppermute x6, waiting for transfers between devices, shift(): return lax.ppermute(value, ALL, [(a, b) for a, b in pairs if to(*place(b))])  74.6 us
    ppermute x2, waiting for transfers between devices, around(): return lax.ppermute(value, ALL, [(d, target(d)) for d in range(count)])  52.2 us
    ppermute x2, starting transfers between devices, around(): return lax.ppermute(value, ALL, [(d, target(d)) for d in range(count)])  36.3 us
    ppermute x4, starting transfers between devices, swap(): return lax.ppermute(value, ALL, [(d, d ^ bit) for d in range(count)])  21.3 us
    pallas_call x4, Pallas kernels, self_part(): pl.pallas_call(functools.partial(self_kernel, tuple(blocks), first, last,...  20.7 us
    ppermute x6, starting transfers between devices, shift(): return lax.ppermute(value, ALL, [(a, b) for a, b in pairs if to(*place(b))])  18.3 us
    unnamed x47, local copies, waits for them, and re-layouts  9.34 us
    pallas_call x2, Pallas kernels, cross_part(): pl.pallas_call(functools.partial(cross_kernel, rows // STRETCH, travels),...  8.92 us
  transfers between devices with their start and end apart: 13, of which 5 were waited for; matrix products, arithmetic and copies ran while one was open for 2% of the time, Pallas kernels for 13%

profile of v5, /device:TPU:101, one launch (start us, length us, event | category | flops | bytes accessed | tf_op | source)
XLA Modules:
  0.0 265.0 jit_solution(7873860467172928170)
XLA Ops:
  0.7 2.2 shard_map.95
  2.9 2.6 collective-permute-start
  5.4 12.7 %collective-permute-start.3 = (bf16[256,1024]{1,0:T(8,128)(2,1)}, bf16[256,1024]{1,0:T(8,128)(2,1)}, u32[]{:S(2)}, u32[]{:S(2)}) collective-permute-start(bf16[256,1024]{1,0:T(8,128)(2,1)} %q_ref.1), channel_id=1, source_target_pairs={{0,8},{4,12},{8,0},{12,4},{16,24},{20,28},{24,16},{28,20},{32,40},... | collective-permute-start | bytes 1572872 | tf_op jit(solution)/shard_map/ppermute | solution.py:33
  18.6 0.1 copy.27
  18.8 0.1 reduce
  19.0 0.6 fusion
  19.9 0.1 copy.30
  20.1 0.1 copy.33
  20.2 0.1 copy.29
  20.4 0.1 copy.32
  22.2 1.3 pad_maximum_fusion.refs_0_
  23.6 0.2 copy-done.9
  23.7 0.4 copy-done.10
  24.1 1.1 shard_map.96
  25.2 2.6 collective-permute-start.2
  27.9 2.6 collective-permute-start.1
  30.5 1.7 collective-permute-start.8
  32.1 2.7 %collective-permute-start.4 = (bf16[2,3,128,1024]{3,2,1,0:T(8,128)(2,1)}, bf16[2,3,128,1024]{3,2,1,0:T(8,128)(2,1)S(1)}, u32[]{:S(2)}, u32[]{:S(2)}) collective-permute-start(bf16[2,3,128,1024]{3,2,1,0:T(8,128)(2,1)} %shard_map.97), channel_id=1, source_target_pairs={{0,4},{4,0},{8,12},{12,8},{16,20},{20,16},{24,28},{28,24},{32,36},... | collective-permute-start | bytes 4718600 | tf_op jit(solution)/shard_map/ppermute | solution.py:33
  34.9 0.1 broadcast_in_dim.24.refs_1_
  35.0 4.7 %shard_map.98 = (f32[512,512]{1,0:T(8,128)S(1)}, f32[4,512,128]{2,1,0:T(8,128)S(1)}, f32[4,512,128]{2,1,0:T(8,128)S(1)}) custom-call(s32[8]{0:T(128)S(1)} %stack.65.meta, bf16[512,512]{1,0:T(8,128)(2,1)S(1)} %get-tuple-element.17.refs_0_, s32[512,128]{1,0:T(8,128)S(1)} %broadcast_in_dim.24.refs_1_, bf16[2,512,512]{2,1,0:T(8,128)(2,1)} %get-tuple-element.18.refs_1_.refs_2_), custom_call_target="tpu_custom_call" | custom-call | flops 99999997952 | bytes 100000000 | tf_op jit(solution)/shard_map/pallas_call | solution.py:211
  39.7 1.0 copy-done.11
  40.7 1.0 copy-done.13
  41.8 4.6 %shard_map.99 = (f32[256,1024]{1,0:T(8,128)S(1)}, f32[16,256]{1,0:T(8,128)S(1)}) custom-call(s32[24]{0:T(128)S(1)} %pad_add_fusion.2.meta, bf16[256,1024]{1,0:T(8,128)(2,1)} %q_ref.1, bf16[3,128,1024]{2,1,0:T(8,128)(2,1)S(1)} %copy-done.2, bf16[3,128,1024]{2,1,0:T(8,128)(2,1)S(1)} %copy-done.3, bf16[2,3,128,1024]{3,2,1,0:T(8,128)(2,1)S(1)} %collective-permute-done.4.side, ...), custom_call_target="tpu_custom_call" | custom-call | flops 1 | bytes 1 | tf_op jit(solution)/shard_map/pallas_call | solution.py:302
  46.4 6.7 %collective-permute-done.3.q_ref = bf16[256,1024]{1,0:T(8,128)(2,1)} collective-permute-done((bf16[256,1024]{1,0:T(8,128)(2,1)}, bf16[256,1024]{1,0:T(8,128)(2,1)}, u32[]{:S(2)}, u32[]{:S(2)}) %collective-permute-start.3) | collective-permute-done | bytes 524320 | tf_op jit(solution)/shard_map/ppermute | solution.py:33
  53.1 4.3 %shard_map.100 = bf16[272,1024]{1,0:T(8,128)(2,1)S(1)} custom-call(s32[24]{0:T(128)S(1)} %pad_add_fusion.1.meta, bf16[256,1024]{1,0:T(8,128)(2,1)} %collective-permute-done.3.q_ref, bf16[3,128,1024]{2,1,0:T(8,128)(2,1)S(1)} %copy-done.2, bf16[3,128,1024]{2,1,0:T(8,128)(2,1)S(1)} %copy-done.3, bf16[2,3,128,1024]{3,2,1,0:T(8,128)(2,1)S(1)} %collective-permute-done.4.side, ...), custom_call_target="tpu_custom_call" | custom-call | flops 1 | bytes 1 | tf_op jit(solution)/shard_map/pallas_call | solution.py:302
  57.4 10.8 %collective-permute-start.5 = (bf16[272,1024]{1,0:T(8,128)(2,1)S(1)}, bf16[272,1024]{1,0:T(8,128)(2,1)}, u32[]{:S(2)}, u32[]{:S(2)}) collective-permute-start(bf16[272,1024]{1,0:T(8,128)(2,1)S(1)} %shard_map.100), channel_id=1, source_target_pairs={{0,112},{4,116},{8,120},{12,124},{16,8},{20,12},{24,0},{28,4},{32,... | collective-permute-start | bytes 1671176 | tf_op jit(solution)/shard_map/ppermute | solution.py:44
  68.2 18.7 %collective-permute-done.2.refs_0_ = bf16[2,512,512]{2,1,0:T(8,128)(2,1)S(1)} collective-permute-done((bf16[2,512,512]{2,1,0:T(8,128)(2,1)}, bf16[2,512,512]{2,1,0:T(8,128)(2,1)S(1)}, u32[]{:S(2)}, u32[]{:S(2)}) %collective-permute-start.2) | collective-permute-done | bytes 1048608 | tf_op jit(solution)/shard_map/ppermute | solution.py:28
  86.9 52.1 %collective-permute-done.5.refs_1_ = bf16[272,1024]{1,0:T(8,128)(2,1)} collective-permute-done((bf16[272,1024]{1,0:T(8,128)(2,1)S(1)}, bf16[272,1024]{1,0:T(8,128)(2,1)}, u32[]{:S(2)}, u32[]{:S(2)}) %collective-permute-start.5) | collective-permute-done | bytes 557088 | tf_op jit(solution)/shard_map/ppermute | solution.py:44
  139.1 8.7 %collective-permute-start.10 = (bf16[2,512,512]{2,1,0:T(8,128)(2,1)}, bf16[2,512,512]{2,1,0:T(8,128)(2,1)}, u32[]{:S(2)}, u32[]{:S(2)}) collective-permute-start(bf16[2,512,512]{2,1,0:T(8,128)(2,1)} %shard_map.101.refs_2_.refs_1_), channel_id=1, source_target_pairs={{0,16},{4,20},{8,24},{12,28},{16,32},{20,36},{24,40},{28,44},{32,4... | collective-permute-start | bytes 3145736 | tf_op jit(solution)/shard_map/ppermute | solution.py:28
  147.8 2.4 broadcast_select_fusion
  150.1 0.7 collective-permute-start.9
  150.9 1.2 copy-done.14
  152.1 5.0 %shard_map.102 = (f32[512,512]{1,0:T(8,128)S(1)}, f32[4,512,128]{2,1,0:T(8,128)S(1)}, f32[4,512,128]{2,1,0:T(8,128)S(1)}) custom-call(s32[8]{0:T(128)S(1)} %stack.65.meta, bf16[512,512]{1,0:T(8,128)(2,1)S(1)} %get-tuple-element.17.refs_0_, s32[512,128]{1,0:T(8,128)S(1)} %broadcast_in_dim.24.refs_1_, bf16[2,512,512]{2,1,0:T(8,128)(2,1)S(1)} %copy-done.1, ...), custom_call_target="tpu_custom_call" | custom-call | flops 1 | bytes 1 | tf_op jit(solution)/shard_map/pallas_call | solution.py:211
  157.1 1.0 copy-done.6
  158.1 1.0 copy-done.15
  159.2 1.0 copy-done.17
  160.1 43.0 %collective-permute-done.1.refs_0_ = bf16[2,512,512]{2,1,0:T(8,128)(2,1)} collective-permute-done((bf16[2,512,512]{2,1,0:T(8,128)(2,1)}, bf16[2,512,512]{2,1,0:T(8,128)(2,1)}, u32[]{:S(2)}, u32[]{:S(2)}) %collective-permute-start.1) | collective-permute-done | bytes 1048608 | tf_op jit(solution)/shard_map/ppermute | solution.py:28
  203.2 0.8 collective-permute-start.6
  204.0 1.9 collective-permute-start.7
  206.0 25.5 %collective-permute-start.12 = (bf16[272,1024]{1,0:T(8,128)(2,1)}, bf16[272,1024]{1,0:T(8,128)(2,1)}, u32[]{:S(2)}, u32[]{:S(2)}) collective-permute-start(bf16[272,1024]{1,0:T(8,128)(2,1)} %collective-permute-done.5.refs_1_), channel_id=1, source_target_pairs={{0,16},{4,20},{8,24},{12,28},{16,32},{20,36},{24,40},{28,44},{32,4... | collective-permute-start | bytes 1671176 | tf_op jit(solution)/shard_map/ppermute | solution.py:44
  231.5 1.2 copy-done.16
  232.7 1.2 copy-done.18
  233.9 5.5 %shard_map.104 = (f32[512,512]{1,0:T(8,128)S(1)}, f32[4,512,128]{2,1,0:T(8,128)S(1)}, f32[4,512,128]{2,1,0:T(8,128)S(1)}) custom-call(s32[8]{0:T(128)S(1)} %stack.65.meta, bf16[512,512]{1,0:T(8,128)(2,1)S(1)} %get-tuple-element.17.refs_0_, s32[512,128]{1,0:T(8,128)S(1)} %broadcast_in_dim.24.refs_1_, bf16[2,512,512]{2,1,0:T(8,128)(2,1)} %collective-permute-done.10.refs_2_, ...), custom_call_target="tpu_custom_call" | custom-call | flops 1 | bytes 1 | tf_op jit(solution)/shard_map/pallas_call | solution.py:211
  239.5 12.8 %collective-permute-done.7.refs_3_ = bf16[2,512,512]{2,1,0:T(8,128)(2,1)S(1)} collective-permute-done((bf16[2,512,512]{2,1,0:T(8,128)(2,1)}, bf16[2,512,512]{2,1,0:T(8,128)(2,1)S(1)}, u32[]{:S(2)}, u32[]{:S(2)}) %collective-permute-start.7) | collective-permute-done | bytes 1048608 | tf_op jit(solution)/shard_map/ppermute | solution.py:28
  252.3 5.5 %shard_map.105 = (bf16[256,512]{1,0:T(8,128)(2,1)S(1)}, bf16[256,512]{1,0:T(8,128)(2,1)S(1)}) custom-call(s32[8]{0:T(128)S(1)} %stack.65.meta, bf16[512,512]{1,0:T(8,128)(2,1)S(1)} %get-tuple-element.17.refs_0_, s32[512,128]{1,0:T(8,128)S(1)} %broadcast_in_dim.24.refs_1_, bf16[2,512,512]{2,1,0:T(8,128)(2,1)S(1)} %collective-permute-done.6.refs_2_, ...), custom_call_target="tpu_custom_call" | custom-call | flops 1 | bytes 1 | tf_op jit(solution)/shard_map/pallas_call | solution.py:211
  257.8 3.2 %collective-permute-start.11 = (bf16[256,512]{1,0:T(8,128)(2,1)S(1)}, bf16[256,512]{1,0:T(8,128)(2,1)S(1)}, u32[]{:S(2)}, u32[]{:S(2)}) collective-permute-start(bf16[256,512]{1,0:T(8,128)(2,1)S(1)} %get-tuple-element.30), channel_id=1, source_target_pairs={{0,4},{4,0},{8,12},{12,8},{16,20},{20,16},{24,28},{28,24},{32,36},... | collective-permute-start | bytes 786440 | tf_op jit(solution)/shard_map/ppermute | solution.py:33
  261.1 2.9 %shard_map.106 = bf16[256,1024]{1,0:T(8,128)(2,1)} custom-call(f32[256,1024]{1,0:T(8,128)S(1)} %copy-done.20, bf16[272,1024]{1,0:T(8,128)(2,1)} %collective-permute-done.12.ob_ref, f32[16,256]{1,0:T(8,128)S(1)} %get-tuple-element.20.refs_0_.sa_ref), custom_call_target="tpu_custom_call" | custom-call | flops 1 | bytes 1 | tf_op jit(solution)/shard_map/pallas_call | solution.py:340
  264.0 0.9 maximum_select_fusion
  (70 shorter events, 1.6 us)
Async XLA Ops:
  0.6 17.6 %copy-start.21 = (s32[512,2]{0,1:T(2,128)S(1)}, s32[512,2]{0,1:T(2,128)}, u32[]{:S(2)}) copy-start(s32[512,2]{0,1:T(2,128)} %param.14) | copy-start | bytes 12292
  0.6 18.0 %copy-start.22 = (s32[33]{0:T(128)S(1)}, s32[33]{0:T(128)}, u32[]{:S(2)}) copy-start(s32[33]{0:T(128)} %param.15) | copy-start | bytes 400
  0.7 21.6 %copy-start.3 = (bf16[3,128,1024]{2,1,0:T(8,128)(2,1)S(1)}, bf16[3,128,1024]{2,1,0:T(8,128)(2,1)}, u32[]{:S(2)}) copy-start(bf16[3,128,1024]{2,1,0:T(8,128)(2,1)} %v_here.3) | copy-start | bytes 2359300
  0.7 21.5 %copy-start.2 = (bf16[3,128,1024]{2,1,0:T(8,128)(2,1)S(1)}, bf16[3,128,1024]{2,1,0:T(8,128)(2,1)}, u32[]{:S(2)}) copy-start(bf16[3,128,1024]{2,1,0:T(8,128)(2,1)} %k_here.3) | copy-start | bytes 2359300
  2.9 20.7 %collective-permute-start = (bf16[3,256,512]{2,1,0:T(8,128)(2,1)}, bf16[3,256,512]{2,1,0:T(8,128)(2,1)S(1)}, u32[]{:S(2)}, u32[]{:S(2)}) collective-permute-start(bf16[3,256,512]{2,1,0:T(8,128)(2,1)} %shard_map.95), channel_id=1, source_target_pairs={{0,4},{4,0},{8,12},{12,8},{16,20},{20,16},{24,28},{28,24},{32,36},... | collective-permute-start | bytes 2359304 | tf_op jit(solution)/shard_map/ppermute | solution.py:33
  5.4 47.7 %collective-permute-start.3 = (bf16[256,1024]{1,0:T(8,128)(2,1)}, bf16[256,1024]{1,0:T(8,128)(2,1)}, u32[]{:S(2)}, u32[]{:S(2)}) collective-permute-start(bf16[256,1024]{1,0:T(8,128)(2,1)} %q_ref.1), channel_id=1, source_target_pairs={{0,8},{4,12},{8,0},{12,4},{16,24},{20,28},{24,16},{28,20},{32,40},... | collective-permute-start | bytes 1572872 | tf_op jit(solution)/shard_map/ppermute | solution.py:33
  22.2 1.4 copy-start.8
  22.2 1.5 copy-start.9
  22.2 1.9 copy-start.10
  25.2 61.7 %collective-permute-start.2 = (bf16[2,512,512]{2,1,0:T(8,128)(2,1)}, bf16[2,512,512]{2,1,0:T(8,128)(2,1)S(1)}, u32[]{:S(2)}, u32[]{:S(2)}) collective-permute-start(bf16[2,512,512]{2,1,0:T(8,128)(2,1)} %get-tuple-element.18.refs_1_.refs_2_), channel_id=1, source_target_pairs={{0,16},{4,20},{8,24},{12,28},{16,32},{20,36},{24,40},{28,44},{32,4... | collective-permute-start | bytes 3145736 | tf_op jit(solution)/shard_map/ppermute | solution.py:28
  27.9 175.3 %collective-permute-start.1 = (bf16[2,512,512]{2,1,0:T(8,128)(2,1)}, bf16[2,512,512]{2,1,0:T(8,128)(2,1)}, u32[]{:S(2)}, u32[]{:S(2)}) collective-permute-start(bf16[2,512,512]{2,1,0:T(8,128)(2,1)} %get-tuple-element.18.refs_1_.refs_2_), channel_id=1, source_target_pairs={{0,24},{4,28},{8,32},{12,36},{16,40},{20,44},{24,48},{28,52},{32,5... | collective-permute-start | bytes 3145736 | tf_op jit(solution)/shard_map/ppermute | solution.py:28
  30.5 117.3 %collective-permute-start.8 = (bf16[2,512,512]{2,1,0:T(8,128)(2,1)}, bf16[2,512,512]{2,1,0:T(8,128)(2,1)}, u32[]{:S(2)}, u32[]{:S(2)}) collective-permute-start(bf16[2,512,512]{2,1,0:T(8,128)(2,1)} %get-tuple-element.18.refs_1_.refs_2_), channel_id=1, source_target_pairs={{104,136},{108,140},{232,264},{236,268},{360,392},{364,396},{488,8... | collective-permute-start | bytes 3145736 | tf_op jit(solution)/shard_map/ppermute | solution.py:28
  32.1 9.6 %collective-permute-start.4 = (bf16[2,3,128,1024]{3,2,1,0:T(8,128)(2,1)}, bf16[2,3,128,1024]{3,2,1,0:T(8,128)(2,1)S(1)}, u32[]{:S(2)}, u32[]{:S(2)}) collective-permute-start(bf16[2,3,128,1024]{3,2,1,0:T(8,128)(2,1)} %shard_map.97), channel_id=1, source_target_pairs={{0,4},{4,0},{8,12},{12,8},{16,20},{20,16},{24,28},{28,24},{32,36},... | collective-permute-start | bytes 4718600 | tf_op jit(solution)/shard_map/ppermute | solution.py:33
  39.7 1.0 copy-start.11
  40.7 1.0 copy-start.13
  41.8 4.7 %copy-start.4 = (f32[512,512]{1,0:T(8,128)}, f32[512,512]{1,0:T(8,128)S(1)}, u32[]{:S(2)}) copy-start(f32[512,512]{1,0:T(8,128)S(1)} %get-tuple-element.19.refs_0_.refs_3_) | copy-start | bytes 3145732
  46.4 10.9 %copy-start.19 = (f32[256,1024]{1,0:T(8,128)}, f32[256,1024]{1,0:T(8,128)S(1)}, u32[]{:S(2)}) copy-start(f32[256,1024]{1,0:T(8,128)S(1)} %get-tuple-element.31.oa_ref) | copy-start | bytes 3145732
  57.4 81.7 %collective-permute-start.5 = (bf16[272,1024]{1,0:T(8,128)(2,1)S(1)}, bf16[272,1024]{1,0:T(8,128)(2,1)}, u32[]{:S(2)}, u32[]{:S(2)}) collective-permute-start(bf16[272,1024]{1,0:T(8,128)(2,1)S(1)} %shard_map.100), channel_id=1, source_target_pairs={{0,112},{4,116},{8,120},{12,124},{16,8},{20,12},{24,0},{28,4},{32,... | collective-permute-start | bytes 1671176 | tf_op jit(solution)/shard_map/ppermute | solution.py:44
  86.9 52.2 %copy-start = (bf16[2,512,512]{2,1,0:T(8,128)(2,1)}, bf16[2,512,512]{2,1,0:T(8,128)(2,1)S(1)}, u32[]{:S(2)}) copy-start(bf16[2,512,512]{2,1,0:T(8,128)(2,1)S(1)} %collective-permute-done.2.refs_0_) | copy-start | bytes 3145732
  139.0 11.8 %copy-start.1 = (bf16[2,512,512]{2,1,0:T(8,128)(2,1)S(1)}, bf16[2,512,512]{2,1,0:T(8,128)(2,1)}, u32[]{:S(2)}) copy-start(bf16[2,512,512]{2,1,0:T(8,128)(2,1)} %shard_map.101.refs_2_.refs_1_) | copy-start | bytes 3145732
  139.1 11.8 %copy-start.5 = (f32[512,512]{1,0:T(8,128)S(1)}, f32[512,512]{1,0:T(8,128)}, u32[]{:S(2)}) copy-start(f32[512,512]{1,0:T(8,128)} %copy-done.4) | copy-start | bytes 3145732
  139.1 11.8 %copy-start.12 = (f32[4,512,128]{2,1,0:T(8,128)S(1)}, f32[4,512,128]{2,1,0:T(8,128)}, u32[]{:S(2)}) copy-start(f32[4,512,128]{2,1,0:T(8,128)} %copy-done.11) | copy-start | bytes 3145732
  139.1 92.4 %collective-permute-start.10 = (bf16[2,512,512]{2,1,0:T(8,128)(2,1)}, bf16[2,512,512]{2,1,0:T(8,128)(2,1)}, u32[]{:S(2)}, u32[]{:S(2)}) collective-permute-start(bf16[2,512,512]{2,1,0:T(8,128)(2,1)} %shard_map.101.refs_2_.refs_1_), channel_id=1, source_target_pairs={{0,16},{4,20},{8,24},{12,28},{16,32},{20,36},{24,40},{28,44},{32,4... | collective-permute-start | bytes 3145736 | tf_op jit(solution)/shard_map/ppermute | solution.py:28
  150.1 89.3 %collective-permute-start.9 = (bf16[2,512,512]{2,1,0:T(8,128)(2,1)}, bf16[2,512,512]{2,1,0:T(8,128)(2,1)S(1)}, u32[]{:S(2)}, u32[]{:S(2)}) collective-permute-start(bf16[2,512,512]{2,1,0:T(8,128)(2,1)} %broadcast_select_fusion), channel_id=1, source_target_pairs={{0,504},{4,508},{8,496},{12,500},{128,120},{132,124},{136,112},{14... | collective-permute-start | bytes 3145736 | tf_op jit(solution)/shard_map/ppermute | solution.py:419
  150.9 1.2 copy-start.14
  157.1 1.0 copy-start.6
  158.1 1.0 copy-start.15
  159.2 1.0 copy-start.17
  203.2 28.3 %copy-start.7 = (f32[512,512]{1,0:T(8,128)S(1)}, f32[512,512]{1,0:T(8,128)}, u32[]{:S(2)}) copy-start(f32[512,512]{1,0:T(8,128)} %copy-done.6) | copy-start | bytes 3145732
  203.2 36.3 %collective-permute-start.6 = (bf16[2,512,512]{2,1,0:T(8,128)(2,1)}, bf16[2,512,512]{2,1,0:T(8,128)(2,1)S(1)}, u32[]{:S(2)}, u32[]{:S(2)}) collective-permute-start(bf16[2,512,512]{2,1,0:T(8,128)(2,1)} %shard_map.103.refs_4_), channel_id=1, source_target_pairs={{120,128},{124,132},{248,256},{252,260},{376,384},{380,388},{504,0... | collective-permute-start | bytes 3145736 | tf_op jit(solution)/shard_map/ppermute | solution.py:28
  204.0 48.3 %collective-permute-start.7 = (bf16[2,512,512]{2,1,0:T(8,128)(2,1)}, bf16[2,512,512]{2,1,0:T(8,128)(2,1)S(1)}, u32[]{:S(2)}, u32[]{:S(2)}) collective-permute-start(bf16[2,512,512]{2,1,0:T(8,128)(2,1)} %shard_map.103.refs_4_), channel_id=1, source_target_pairs={{16,0},{20,4},{24,8},{28,12},{32,16},{36,20},{40,24},{44,28},{48,3... | collective-permute-start | bytes 3145736 | tf_op jit(solution)/shard_map/ppermute | solution.py:28
  206.0 55.1 %collective-permute-start.12 = (bf16[272,1024]{1,0:T(8,128)(2,1)}, bf16[272,1024]{1,0:T(8,128)(2,1)}, u32[]{:S(2)}, u32[]{:S(2)}) collective-permute-start(bf16[272,1024]{1,0:T(8,128)(2,1)} %collective-permute-done.5.refs_1_), channel_id=1, source_target_pairs={{0,16},{4,20},{8,24},{12,28},{16,32},{20,36},{24,40},{28,44},{32,4... | collective-permute-start | bytes 1671176 | tf_op jit(solution)/shard_map/ppermute | solution.py:44
  231.5 1.2 copy-start.16
  232.7 1.2 copy-start.18
  252.3 8.8 %copy-start.20 = (f32[256,1024]{1,0:T(8,128)S(1)}, f32[256,1024]{1,0:T(8,128)}, u32[]{:S(2)}) copy-start(f32[256,1024]{1,0:T(8,128)} %copy-done.19) | copy-start | bytes 3145732
  257.8 6.2 %collective-permute-start.11 = (bf16[256,512]{1,0:T(8,128)(2,1)S(1)}, bf16[256,512]{1,0:T(8,128)(2,1)S(1)}, u32[]{:S(2)}, u32[]{:S(2)}) collective-permute-start(bf16[256,512]{1,0:T(8,128)(2,1)S(1)} %get-tuple-element.30), channel_id=1, source_target_pairs={{0,4},{4,0},{8,12},{12,8},{16,20},{20,16},{24,28},{28,24},{32,36},... | collective-permute-start | bytes 786440 | tf_op jit(solution)/shard_map/ppermute | solution.py:33

commit v6 on v5

--- a/solution.py
+++ b/solution.py
@@ -414,10 +414,12 @@
         pool_meta(device ^ 2), far_queries, pool, True, (near_stat,), SMALL
     )
     nearly = around(far_sum, 7)
-    kv2 = held_back(kv2, (nearly,))
+    from_first = jnp.where(high == 0, kv2, kv4_far)
+    state = attend(((2, 0),), (kv2,), state, after=(far_sum, from_first))
+    kv2 = held_back(kv2, state[:1])
     kv4 = shift(kv2, 4, lambda low, high: low > 0)
     kv1_edge = lax.ppermute(
-        jnp.where(high == 0, kv2, kv4_far),
+        from_first,
         ALL,
         [
             (d, (d - 2 - 4 * place(d)[1]) % lax.axis_size(ALL))
@@ -425,8 +427,7 @@
             if place(d)[0] == 0
         ],
     )
-    state = attend(((2, 0),), (kv2,), state)
-    kv3 = held_back(kv3, (kv2, state[0]))
+    kv3 = held_back(kv3, (kv2, nearly))
     kv1 = shift(kv3, -4, lambda low, high: low < RUN - 1)
     kv4_last = shift(kv3, 2, lambda low, high: low == 0 and high == 0)
     back_sum = around(nearly, 1)

time: 267 us -> 270 us (1.011)
  the two profiles are of different devices: /device:TPU:101 before, /device:TPU:97 now
where the time goes in v6:
time: 270 us; the launch traced here: 269 us
  waiting for transfers between devices  151 us (56%)
  starting transfers between devices  73.1 us (27%)
  Pallas kernels  30.2 us (11%)
  local copies, waits for them, and re-layouts  8.95 us (3%)
  other arithmetic  3.16 us (1%)
    ppermute x6, waiting for transfers between devices, shift(): return lax.ppermute(value, ALL, [(a, b) for a, b in pairs if to(*place(b))])  139 us
    ppermute x2, starting transfers between devices, around(): return lax.ppermute(value, ALL, [(d, target(d)) for d in range(count)])  36.1 us
    ppermute x4, starting transfers between devices, swap(): return lax.ppermute(value, ALL, [(d, d ^ bit) for d in range(count)])  21.3 us
    pallas_call x4, Pallas kernels, self_part(): pl.pallas_call(functools.partial(self_kernel, tuple(blocks), first, last,...  14.7 us
    ppermute x6, starting transfers between devices, shift(): return lax.ppermute(value, ALL, [(a, b) for a, b in pairs if to(*place(b))])  14 us
    ppermute x4, waiting for transfers between devices, swap(): return lax.ppermute(value, ALL, [(d, d ^ bit) for d in range(count)])  12.1 us
    pallas_call x2, Pallas kernels, cross_part(): pl.pallas_call(functools.partial(cross_kernel, rows // STRETCH, travels),...  9.36 us
    unnamed x33, local copies, waits for them, and re-layouts  6.95 us
  transfers between devices with their start and end apart: 13, of which 4 were waited for; matrix products, arithmetic and copies ran while one was open for 2% of the time, Pallas kernels for 10%

profile of v6, /device:TPU:97, one launch (start us, length us, event | category | flops | bytes accessed | tf_op | source)
XLA Modules:
  0.0 268.8 jit_solution(13345102439560508801)
XLA Ops:
  0.7 2.2 shard_map.95
  2.9 2.6 collective-permute-start
  5.4 12.7 %collective-permute-start.3 = (bf16[256,1024]{1,0:T(8,128)(2,1)}, bf16[256,1024]{1,0:T(8,128)(2,1)}, u32[]{:S(2)}, u32[]{:S(2)}) collective-permute-start(bf16[256,1024]{1,0:T(8,128)(2,1)} %q_ref.1), channel_id=1, source_target_pairs={{0,8},{4,12},{8,0},{12,4},{16,24},{20,28},{24,16},{28,20},{32,40},... | collective-permute-start | bytes 1572872 | tf_op jit(solution)/shard_map/ppermute | solution.py:33
  18.6 0.1 copy.27
  18.8 0.1 reduce
  18.9 0.1 select_reduce_fusion
  19.0 0.6 fusion
  19.6 0.1 copy.28
  19.8 0.1 copy.31
  19.9 0.1 copy.30
  20.1 0.1 copy.33
  20.3 0.1 copy.29
  20.5 0.1 copy.32
  22.4 1.3 pad_maximum_fusion.refs_0_
  23.7 0.2 copy-done.6
  23.9 0.4 copy-done.7
  24.3 1.1 shard_map.96
  25.4 2.6 collective-permute-start.2
  28.0 1.7 collective-permute-start.5
  29.7 2.6 collective-permute-start.1
  32.3 2.8 %collective-permute-start.4 = (bf16[2,3,128,1024]{3,2,1,0:T(8,128)(2,1)}, bf16[2,3,128,1024]{3,2,1,0:T(8,128)(2,1)S(1)}, u32[]{:S(2)}, u32[]{:S(2)}) collective-permute-start(bf16[2,3,128,1024]{3,2,1,0:T(8,128)(2,1)} %shard_map.98), channel_id=1, source_target_pairs={{0,4},{4,0},{8,12},{12,8},{16,20},{20,16},{24,28},{28,24},{32,36},... | collective-permute-start | bytes 4718600 | tf_op jit(solution)/shard_map/ppermute | solution.py:33
  35.0 0.1 broadcast_in_dim.24.refs_1_
  35.2 4.7 %shard_map.97 = (f32[512,512]{1,0:T(8,128)S(1)}, f32[4,512,128]{2,1,0:T(8,128)S(1)}, f32[4,512,128]{2,1,0:T(8,128)S(1)}) custom-call(s32[8]{0:T(128)S(1)} %stack.65.meta, bf16[512,512]{1,0:T(8,128)(2,1)S(1)} %get-tuple-element.17.refs_0_, s32[512,128]{1,0:T(8,128)S(1)} %broadcast_in_dim.24.refs_1_, bf16[2,512,512]{2,1,0:T(8,128)(2,1)} %get-tuple-element.18.refs_2_.refs_1_), custom_call_target="tpu_custom_call" | custom-call | flops 99999997952 | bytes 100000000 | tf_op jit(solution)/shard_map/pallas_call | solution.py:211
  39.9 4.3 %shard_map.99 = (f32[256,1024]{1,0:T(8,128)S(1)}, f32[16,256]{1,0:T(8,128)S(1)}) custom-call(s32[24]{0:T(128)S(1)} %pad_add_fusion.2.meta, bf16[256,1024]{1,0:T(8,128)(2,1)} %q_ref.1, bf16[3,128,1024]{2,1,0:T(8,128)(2,1)S(1)} %copy-done.1, bf16[3,128,1024]{2,1,0:T(8,128)(2,1)S(1)} %copy-done.2, bf16[2,3,128,1024]{3,2,1,0:T(8,128)(2,1)S(1)} %collective-permute-done.4.side, ...), custom_call_target="tpu_custom_call" | custom-call | flops 1 | bytes 1 | tf_op jit(solution)/shard_map/pallas_call | solution.py:302
  44.2 12.1 %collective-permute-done.3.q_ref = bf16[256,1024]{1,0:T(8,128)(2,1)} collective-permute-done((bf16[256,1024]{1,0:T(8,128)(2,1)}, bf16[256,1024]{1,0:T(8,128)(2,1)}, u32[]{:S(2)}, u32[]{:S(2)}) %collective-permute-start.3) | collective-permute-done | bytes 524320 | tf_op jit(solution)/shard_map/ppermute | solution.py:33
  56.3 5.1 %shard_map.100.refs_6_ = bf16[272,1024]{1,0:T(8,128)(2,1)} custom-call(s32[24]{0:T(128)S(1)} %pad_add_fusion.1.meta, bf16[256,1024]{1,0:T(8,128)(2,1)} %collective-permute-done.3.q_ref, bf16[3,128,1024]{2,1,0:T(8,128)(2,1)S(1)} %copy-done.1, bf16[3,128,1024]{2,1,0:T(8,128)(2,1)S(1)} %copy-done.2, bf16[2,3,128,1024]{3,2,1,0:T(8,128)(2,1)S(1)} %collective-permute-done.4.side, ...), custom_call_target="tpu_custom_call" | custom-call | flops 1 | bytes 1 | tf_op jit(solution)/shard_map/pallas_call | solution.py:302
  61.4 7.7 %collective-permute-start.6 = (bf16[272,1024]{1,0:T(8,128)(2,1)}, bf16[272,1024]{1,0:T(8,128)(2,1)}, u32[]{:S(2)}, u32[]{:S(2)}) collective-permute-start(bf16[272,1024]{1,0:T(8,128)(2,1)} %shard_map.100.refs_6_), channel_id=1, source_target_pairs={{0,112},{4,116},{8,120},{12,124},{16,8},{20,12},{24,0},{28,4},{32,... | collective-permute-start | bytes 1671176 | tf_op jit(solution)/shard_map/ppermute | solution.py:44
  69.1 17.8 %collective-permute-done.2.refs_2_.refs_0_ = bf16[2,512,512]{2,1,0:T(8,128)(2,1)S(1)} collective-permute-done((bf16[2,512,512]{2,1,0:T(8,128)(2,1)}, bf16[2,512,512]{2,1,0:T(8,128)(2,1)S(1)}, u32[]{:S(2)}, u32[]{:S(2)}) %collective-permute-start.2) | collective-permute-done | bytes 1048608 | tf_op jit(solution)/shard_map/ppermute | solution.py:28
  86.9 0.1 broadcast_select_fusion.refs_7_
  87.0 0.9 copy-done
  87.8 1.3 shard_map.101
  89.1 1.0 copy-done.3
  90.1 1.0 copy-done.8
  91.1 1.1 copy-done.10
  92.2 4.5 %collective-permute-start.10 = (bf16[2,512,512]{2,1,0:T(8,128)(2,1)}, bf16[2,512,512]{2,1,0:T(8,128)(2,1)}, u32[]{:S(2)}, u32[]{:S(2)}) collective-permute-start(bf16[2,512,512]{2,1,0:T(8,128)(2,1)} %shard_map.102.refs_1_), channel_id=1, source_target_pairs={{0,16},{4,20},{8,24},{12,28},{16,32},{20,36},{24,40},{28,44},{32,4... | collective-permute-start | bytes 3145736 | tf_op jit(solution)/shard_map/ppermute | solution.py:28
  96.7 1.7 collective-permute-start.9
  98.3 105.5 %collective-permute-done.1.refs_0_ = bf16[2,512,512]{2,1,0:T(8,128)(2,1)} collective-permute-done((bf16[2,512,512]{2,1,0:T(8,128)(2,1)}, bf16[2,512,512]{2,1,0:T(8,128)(2,1)}, u32[]{:S(2)}, u32[]{:S(2)}) %collective-permute-start.1) | collective-permute-done | bytes 1048608 | tf_op jit(solution)/shard_map/ppermute | solution.py:28
  203.9 0.7 collective-permute-start.7
  204.6 1.9 collective-permute-start.8
  206.5 28.5 %collective-permute-start.12 = (bf16[272,1024]{1,0:T(8,128)(2,1)}, bf16[272,1024]{1,0:T(8,128)(2,1)}, u32[]{:S(2)}, u32[]{:S(2)}) collective-permute-start(bf16[272,1024]{1,0:T(8,128)(2,1)} %collective-permute-done.6.refs_2_), channel_id=1, source_target_pairs={{0,16},{4,20},{8,24},{12,28},{16,32},{20,36},{24,40},{28,44},{32,4... | collective-permute-start | bytes 1671176 | tf_op jit(solution)/shard_map/ppermute | solution.py:44
  235.0 1.2 copy-done.9
  236.2 1.2 copy-done.11
  237.5 2.9 %shard_map.104 = (f32[512,512]{1,0:T(8,128)S(1)}, f32[4,512,128]{2,1,0:T(8,128)S(1)}, f32[4,512,128]{2,1,0:T(8,128)S(1)}) custom-call(s32[8]{0:T(128)S(1)} %stack.65.meta, bf16[512,512]{1,0:T(8,128)(2,1)S(1)} %get-tuple-element.17.refs_0_, s32[512,128]{1,0:T(8,128)S(1)} %broadcast_in_dim.24.refs_1_, bf16[2,512,512]{2,1,0:T(8,128)(2,1)} %collective-permute-done.10.refs_2_, ...), custom_call_target="tpu_custom_call" | custom-call | flops 1 | bytes 1 | tf_op jit(solution)/shard_map/pallas_call | solution.py:211
  240.4 15.5 %collective-permute-done.8.refs_3_ = bf16[2,512,512]{2,1,0:T(8,128)(2,1)S(1)} collective-permute-done((bf16[2,512,512]{2,1,0:T(8,128)(2,1)}, bf16[2,512,512]{2,1,0:T(8,128)(2,1)S(1)}, u32[]{:S(2)}, u32[]{:S(2)}) %collective-permute-start.8) | collective-permute-done | bytes 1048608 | tf_op jit(solution)/shard_map/ppermute | solution.py:28
  255.9 5.8 %shard_map.105 = (bf16[256,512]{1,0:T(8,128)(2,1)S(1)}, bf16[256,512]{1,0:T(8,128)(2,1)S(1)}) custom-call(s32[8]{0:T(128)S(1)} %stack.65.meta, bf16[512,512]{1,0:T(8,128)(2,1)S(1)} %get-tuple-element.17.refs_0_, s32[512,128]{1,0:T(8,128)S(1)} %broadcast_in_dim.24.refs_1_, bf16[2,512,512]{2,1,0:T(8,128)(2,1)S(1)} %collective-permute-done.7.refs_2_, ...), custom_call_target="tpu_custom_call" | custom-call | flops 1 | bytes 1 | tf_op jit(solution)/shard_map/pallas_call | solution.py:211
  261.7 3.2 %collective-permute-start.11 = (bf16[256,512]{1,0:T(8,128)(2,1)S(1)}, bf16[256,512]{1,0:T(8,128)(2,1)S(1)}, u32[]{:S(2)}, u32[]{:S(2)}) collective-permute-start(bf16[256,512]{1,0:T(8,128)(2,1)S(1)} %get-tuple-element.30), channel_id=1, source_target_pairs={{0,4},{4,0},{8,12},{12,8},{16,20},{20,16},{24,28},{28,24},{32,36},... | collective-permute-start | bytes 786440 | tf_op jit(solution)/shard_map/ppermute | solution.py:33
  265.0 2.9 %shard_map.106 = bf16[256,1024]{1,0:T(8,128)(2,1)} custom-call(f32[256,1024]{1,0:T(8,128)S(1)} %copy-done.13, bf16[272,1024]{1,0:T(8,128)(2,1)} %collective-permute-done.12.ob_ref, f32[16,256]{1,0:T(8,128)S(1)} %get-tuple-element.22.refs_0_.sa_ref), custom_call_target="tpu_custom_call" | custom-call | flops 1 | bytes 1 | tf_op jit(solution)/shard_map/pallas_call | solution.py:340
  267.9 0.9 maximum_select_fusion
  (56 shorter events, 1.3 us)
Async XLA Ops:
  0.6 17.6 %copy-start.14 = (s32[512,2]{0,1:T(2,128)S(1)}, s32[512,2]{0,1:T(2,128)}, u32[]{:S(2)}) copy-start(s32[512,2]{0,1:T(2,128)} %param.14) | copy-start | bytes 12292
  0.6 18.0 %copy-start.15 = (s32[33]{0:T(128)S(1)}, s32[33]{0:T(128)}, u32[]{:S(2)}) copy-start(s32[33]{0:T(128)} %param.15) | copy-start | bytes 400
  0.7 21.7 %copy-start.2 = (bf16[3,128,1024]{2,1,0:T(8,128)(2,1)S(1)}, bf16[3,128,1024]{2,1,0:T(8,128)(2,1)}, u32[]{:S(2)}) copy-start(bf16[3,128,1024]{2,1,0:T(8,128)(2,1)} %v_here.3) | copy-start | bytes 2359300
  0.7 21.7 %copy-start.1 = (bf16[3,128,1024]{2,1,0:T(8,128)(2,1)S(1)}, bf16[3,128,1024]{2,1,0:T(8,128)(2,1)}, u32[]{:S(2)}) copy-start(bf16[3,128,1024]{2,1,0:T(8,128)(2,1)} %k_here.3) | copy-start | bytes 2359300
  2.9 20.9 %collective-permute-start = (bf16[3,256,512]{2,1,0:T(8,128)(2,1)}, bf16[3,256,512]{2,1,0:T(8,128)(2,1)S(1)}, u32[]{:S(2)}, u32[]{:S(2)}) collective-permute-start(bf16[3,256,512]{2,1,0:T(8,128)(2,1)} %shard_map.95), channel_id=1, source_target_pairs={{0,4},{4,0},{8,12},{12,8},{16,20},{20,16},{24,28},{28,24},{32,36},... | collective-permute-start | bytes 2359304 | tf_op jit(solution)/shard_map/ppermute | solution.py:33
  5.4 50.9 %collective-permute-start.3 = (bf16[256,1024]{1,0:T(8,128)(2,1)}, bf16[256,1024]{1,0:T(8,128)(2,1)}, u32[]{:S(2)}, u32[]{:S(2)}) collective-permute-start(bf16[256,1024]{1,0:T(8,128)(2,1)} %q_ref.1), channel_id=1, source_target_pairs={{0,8},{4,12},{8,0},{12,4},{16,24},{20,28},{24,16},{28,20},{32,40},... | collective-permute-start | bytes 1572872 | tf_op jit(solution)/shard_map/ppermute | solution.py:33
  22.4 1.4 copy-start.5
  22.4 1.5 copy-start.6
  22.4 1.9 copy-start.7
  25.4 61.5 %collective-permute-start.2 = (bf16[2,512,512]{2,1,0:T(8,128)(2,1)}, bf16[2,512,512]{2,1,0:T(8,128)(2,1)S(1)}, u32[]{:S(2)}, u32[]{:S(2)}) collective-permute-start(bf16[2,512,512]{2,1,0:T(8,128)(2,1)} %get-tuple-element.18.refs_2_.refs_1_), channel_id=1, source_target_pairs={{0,16},{4,20},{8,24},{12,28},{16,32},{20,36},{24,40},{28,44},{32,4... | collective-permute-start | bytes 3145736 | tf_op jit(solution)/shard_map/ppermute | solution.py:28
  28.0 58.9 %collective-permute-start.5 = (bf16[2,512,512]{2,1,0:T(8,128)(2,1)}, bf16[2,512,512]{2,1,0:T(8,128)(2,1)}, u32[]{:S(2)}, u32[]{:S(2)}) collective-permute-start(bf16[2,512,512]{2,1,0:T(8,128)(2,1)} %get-tuple-element.18.refs_2_.refs_1_), channel_id=1, source_target_pairs={{104,136},{108,140},{232,264},{236,268},{360,392},{364,396},{488,8... | collective-permute-start | bytes 3145736 | tf_op jit(solution)/shard_map/ppermute | solution.py:28
  29.7 174.2 %collective-permute-start.1 = (bf16[2,512,512]{2,1,0:T(8,128)(2,1)}, bf16[2,512,512]{2,1,0:T(8,128)(2,1)}, u32[]{:S(2)}, u32[]{:S(2)}) collective-permute-start(bf16[2,512,512]{2,1,0:T(8,128)(2,1)} %get-tuple-element.18.refs_2_.refs_1_), channel_id=1, source_target_pairs={{0,24},{4,28},{8,32},{12,36},{16,40},{20,44},{24,48},{28,52},{32,5... | collective-permute-start | bytes 3145736 | tf_op jit(solution)/shard_map/ppermute | solution.py:28
  32.3 7.6 %collective-permute-start.4 = (bf16[2,3,128,1024]{3,2,1,0:T(8,128)(2,1)}, bf16[2,3,128,1024]{3,2,1,0:T(8,128)(2,1)S(1)}, u32[]{:S(2)}, u32[]{:S(2)}) collective-permute-start(bf16[2,3,128,1024]{3,2,1,0:T(8,128)(2,1)} %shard_map.98), channel_id=1, source_target_pairs={{0,4},{4,0},{8,12},{12,8},{16,20},{20,16},{24,28},{28,24},{32,36},... | collective-permute-start | bytes 4718600 | tf_op jit(solution)/shard_map/ppermute | solution.py:33
  44.2 17.2 %copy-start.12 = (f32[256,1024]{1,0:T(8,128)}, f32[256,1024]{1,0:T(8,128)S(1)}, u32[]{:S(2)}) copy-start(f32[256,1024]{1,0:T(8,128)S(1)} %get-tuple-element.31.oa_ref) | copy-start | bytes 3145732
  61.4 142.5 %collective-permute-start.6 = (bf16[272,1024]{1,0:T(8,128)(2,1)}, bf16[272,1024]{1,0:T(8,128)(2,1)}, u32[]{:S(2)}, u32[]{:S(2)}) collective-permute-start(bf16[272,1024]{1,0:T(8,128)(2,1)} %shard_map.100.refs_6_), channel_id=1, source_target_pairs={{0,112},{4,116},{8,120},{12,124},{16,8},{20,12},{24,0},{28,4},{32,... | collective-permute-start | bytes 1671176 | tf_op jit(solution)/shard_map/ppermute | solution.py:44
  86.9 1.0 copy-start
  89.1 1.0 copy-start.3
  90.1 1.0 copy-start.8
  91.1 1.1 copy-start.10
  92.2 142.8 %copy-start.4 = (f32[512,512]{1,0:T(8,128)S(1)}, f32[512,512]{1,0:T(8,128)}, u32[]{:S(2)}) copy-start(f32[512,512]{1,0:T(8,128)} %copy-done.3) | copy-start | bytes 3145732
  92.2 142.8 %collective-permute-start.10 = (bf16[2,512,512]{2,1,0:T(8,128)(2,1)}, bf16[2,512,512]{2,1,0:T(8,128)(2,1)}, u32[]{:S(2)}, u32[]{:S(2)}) collective-permute-start(bf16[2,512,512]{2,1,0:T(8,128)(2,1)} %shard_map.102.refs_1_), channel_id=1, source_target_pairs={{0,16},{4,20},{8,24},{12,28},{16,32},{20,36},{24,40},{28,44},{32,4... | collective-permute-start | bytes 3145736 | tf_op jit(solution)/shard_map/ppermute | solution.py:28
  96.7 143.7 %collective-permute-start.9 = (bf16[2,512,512]{2,1,0:T(8,128)(2,1)S(1)}, bf16[2,512,512]{2,1,0:T(8,128)(2,1)}, u32[]{:S(2)}, u32[]{:S(2)}) collective-permute-start(bf16[2,512,512]{2,1,0:T(8,128)(2,1)S(1)} %broadcast_select_fusion.refs_7_), channel_id=1, source_target_pairs={{0,504},{4,508},{8,496},{12,500},{128,120},{132,124},{136,112},{14... | collective-permute-start | bytes 3145736 | tf_op jit(solution)/shard_map/ppermute | solution.py:421
  203.9 36.5 %collective-permute-start.7 = (bf16[2,512,512]{2,1,0:T(8,128)(2,1)}, bf16[2,512,512]{2,1,0:T(8,128)(2,1)S(1)}, u32[]{:S(2)}, u32[]{:S(2)}) collective-permute-start(bf16[2,512,512]{2,1,0:T(8,128)(2,1)} %shard_map.103.refs_4_), channel_id=1, source_target_pairs={{120,128},{124,132},{248,256},{252,260},{376,384},{380,388},{504,0... | collective-permute-start | bytes 3145736 | tf_op jit(solution)/shard_map/ppermute | solution.py:28
  204.6 51.3 %collective-permute-start.8 = (bf16[2,512,512]{2,1,0:T(8,128)(2,1)}, bf16[2,512,512]{2,1,0:T(8,128)(2,1)S(1)}, u32[]{:S(2)}, u32[]{:S(2)}) collective-permute-start(bf16[2,512,512]{2,1,0:T(8,128)(2,1)} %shard_map.103.refs_4_), channel_id=1, source_target_pairs={{16,0},{20,4},{24,8},{28,12},{32,16},{36,20},{40,24},{44,28},{48,3... | collective-permute-start | bytes 3145736 | tf_op jit(solution)/shard_map/ppermute | solution.py:28
  206.5 58.4 %collective-permute-start.12 = (bf16[272,1024]{1,0:T(8,128)(2,1)}, bf16[272,1024]{1,0:T(8,128)(2,1)}, u32[]{:S(2)}, u32[]{:S(2)}) collective-permute-start(bf16[272,1024]{1,0:T(8,128)(2,1)} %collective-permute-done.6.refs_2_), channel_id=1, source_target_pairs={{0,16},{4,20},{8,24},{12,28},{16,32},{20,36},{24,40},{28,44},{32,4... | collective-permute-start | bytes 1671176 | tf_op jit(solution)/shard_map/ppermute | solution.py:44
  235.0 1.2 copy-start.9
  236.2 1.2 copy-start.11
  255.9 9.0 %copy-start.13 = (f32[256,1024]{1,0:T(8,128)S(1)}, f32[256,1024]{1,0:T(8,128)}, u32[]{:S(2)}) copy-start(f32[256,1024]{1,0:T(8,128)} %copy-done.12) | copy-start | bytes 3145732
  261.7 6.1 %collective-permute-start.11 = (bf16[256,512]{1,0:T(8,128)(2,1)S(1)}, bf16[256,512]{1,0:T(8,128)(2,1)S(1)}, u32[]{:S(2)}, u32[]{:S(2)}) collective-permute-start(bf16[256,512]{1,0:T(8,128)(2,1)S(1)} %get-tuple-element.30), channel_id=1, source_target_pairs={{0,4},{4,0},{8,12},{12,8},{16,20},{20,16},{24,28},{28,24},{32,36},... | collective-permute-start | bytes 786440 | tf_op jit(solution)/shard_map/ppermute | solution.py:33

commit v7 on v5

--- a/solution.py
+++ b/solution.py
@@ -139,10 +139,9 @@
         seen = (chip_first - away + rows - 1 >= meta[2]) & (chip_first >= away)
         if flag:
             seen &= meta[2 + flag] > 0
-        for qi in range(2):
-
-            @pl.when(seen)
-            def _(qi=qi, bi=bi, away=away):
+        @pl.when(seen)
+        def _(bi=bi, away=away):
+            for qi in range(2):
                 mine = pl.ds(qi * half, half)
                 scores = lax.dot_general(
                     q_ref[mine, :],

time: 267 us -> 266 us (level)
  no operation moved by 1% of the time
where the time goes in v7:
time: 266 us; the launch traced here: 265 us
  waiting for transfers between devices  133 us (50%)
  starting transfers between devices  76.7 us (29%)
  Pallas kernels  35.8 us (13%)
  local copies, waits for them, and re-layouts  11.3 us (4%)
  other arithmetic  5.41 us (2%)
    ppermute x6, waiting for transfers between devices, shift(): return lax.ppermute(value, ALL, [(a, b) for a, b in pairs if to(*place(b))])  74.6 us
    ppermute x2, waiting for transfers between devices, around(): return lax.ppermute(value, ALL, [(d, target(d)) for d in range(count)])  52.2 us
    ppermute x2, starting transfers between devices, around(): return lax.ppermute(value, ALL, [(d, target(d)) for d in range(count)])  36.3 us
    ppermute x4, starting transfers between devices, swap(): return lax.ppermute(value, ALL, [(d, d ^ bit) for d in range(count)])  21.3 us
    pallas_call x4, Pallas kernels, self_part(): pl.pallas_call(functools.partial(self_kernel, tuple(blocks), first, last,...  20.7 us
    ppermute x6, starting transfers between devices, shift(): return lax.ppermute(value, ALL, [(a, b) for a, b in pairs if to(*place(b))])  18.3 us
    unnamed x47, local copies, waits for them, and re-layouts  9.34 us
    pallas_call x2, Pallas kernels, cross_part(): pl.pallas_call(functools.partial(cross_kernel, rows // STRETCH, travels),...  8.92 us
  transfers between devices with their start and end apart: 13, of which 5 were waited for; matrix products, arithmetic and copies ran while one was open for 2% of the time, Pallas kernels for 13%

profile of v7, /device:TPU:101, one launch (start us, length us, event | category | flops | bytes accessed | tf_op | source)
XLA Modules:
  0.0 265.0 jit_solution(7873860467172928170)
XLA Ops:
  0.7 2.2 shard_map.95
  2.9 2.6 collective-permute-start
  5.4 12.7 %collective-permute-start.3 = (bf16[256,1024]{1,0:T(8,128)(2,1)}, bf16[256,1024]{1,0:T(8,128)(2,1)}, u32[]{:S(2)}, u32[]{:S(2)}) collective-permute-start(bf16[256,1024]{1,0:T(8,128)(2,1)} %q_ref.1), channel_id=1, source_target_pairs={{0,8},{4,12},{8,0},{12,4},{16,24},{20,28},{24,16},{28,20},{32,40},... | collective-permute-start | bytes 1572872 | tf_op jit(solution)/shard_map/ppermute | solution.py:33
  18.6 0.1 copy.27
  18.8 0.1 reduce
  19.0 0.6 fusion
  19.5 0.1 copy.28
  19.7 0.1 copy.31
  20.2 0.1 copy.29
  20.4 0.1 copy.32
  22.2 1.3 pad_maximum_fusion.refs_0_
  23.6 0.2 copy-done.9
  23.7 0.4 copy-done.10
  24.1 1.1 shard_map.96
  25.2 2.6 collective-permute-start.2
  27.9 2.6 collective-permute-start.1
  30.5 1.7 collective-permute-start.8
  32.1 2.7 %collective-permute-start.4 = (bf16[2,3,128,1024]{3,2,1,0:T(8,128)(2,1)}, bf16[2,3,128,1024]{3,2,1,0:T(8,128)(2,1)S(1)}, u32[]{:S(2)}, u32[]{:S(2)}) collective-permute-start(bf16[2,3,128,1024]{3,2,1,0:T(8,128)(2,1)} %shard_map.97), channel_id=1, source_target_pairs={{0,4},{4,0},{8,12},{12,8},{16,20},{20,16},{24,28},{28,24},{32,36},... | collective-permute-start | bytes 4718600 | tf_op jit(solution)/shard_map/ppermute | solution.py:33
  34.9 0.1 broadcast_in_dim.24.refs_1_
  35.0 4.7 %shard_map.98 = (f32[512,512]{1,0:T(8,128)S(1)}, f32[4,512,128]{2,1,0:T(8,128)S(1)}, f32[4,512,128]{2,1,0:T(8,128)S(1)}) custom-call(s32[8]{0:T(128)S(1)} %stack.65.meta, bf16[512,512]{1,0:T(8,128)(2,1)S(1)} %get-tuple-element.17.refs_0_, s32[512,128]{1,0:T(8,128)S(1)} %broadcast_in_dim.24.refs_1_, bf16[2,512,512]{2,1,0:T(8,128)(2,1)} %get-tuple-element.18.refs_1_.refs_2_), custom_call_target="tpu_custom_call" | custom-call | flops 99999997952 | bytes 100000000 | tf_op jit(solution)/shard_map/pallas_call | solution.py:210
  39.7 1.0 copy-done.11
  40.7 1.0 copy-done.13
  41.8 4.6 %shard_map.99 = (f32[256,1024]{1,0:T(8,128)S(1)}, f32[16,256]{1,0:T(8,128)S(1)}) custom-call(s32[24]{0:T(128)S(1)} %pad_add_fusion.2.meta, bf16[256,1024]{1,0:T(8,128)(2,1)} %q_ref.1, bf16[3,128,1024]{2,1,0:T(8,128)(2,1)S(1)} %copy-done.2, bf16[3,128,1024]{2,1,0:T(8,128)(2,1)S(1)} %copy-done.3, bf16[2,3,128,1024]{3,2,1,0:T(8,128)(2,1)S(1)} %collective-permute-done.4.side, ...), custom_call_target="tpu_custom_call" | custom-call | flops 1 | bytes 1 | tf_op jit(solution)/shard_map/pallas_call | solution.py:301
  46.4 6.7 %collective-permute-done.3.q_ref = bf16[256,1024]{1,0:T(8,128)(2,1)} collective-permute-done((bf16[256,1024]{1,0:T(8,128)(2,1)}, bf16[256,1024]{1,0:T(8,128)(2,1)}, u32[]{:S(2)}, u32[]{:S(2)}) %collective-permute-start.3) | collective-permute-done | bytes 524320 | tf_op jit(solution)/shard_map/ppermute | solution.py:33
  53.1 4.3 %shard_map.100 = bf16[272,1024]{1,0:T(8,128)(2,1)S(1)} custom-call(s32[24]{0:T(128)S(1)} %pad_add_fusion.1.meta, bf16[256,1024]{1,0:T(8,128)(2,1)} %collective-permute-done.3.q_ref, bf16[3,128,1024]{2,1,0:T(8,128)(2,1)S(1)} %copy-done.2, bf16[3,128,1024]{2,1,0:T(8,128)(2,1)S(1)} %copy-done.3, bf16[2,3,128,1024]{3,2,1,0:T(8,128)(2,1)S(1)} %collective-permute-done.4.side, ...), custom_call_target="tpu_custom_call" | custom-call | flops 1 | bytes 1 | tf_op jit(solution)/shard_map/pallas_call | solution.py:301
  57.4 10.8 %collective-permute-start.5 = (bf16[272,1024]{1,0:T(8,128)(2,1)S(1)}, bf16[272,1024]{1,0:T(8,128)(2,1)}, u32[]{:S(2)}, u32[]{:S(2)}) collective-permute-start(bf16[272,1024]{1,0:T(8,128)(2,1)S(1)} %shard_map.100), channel_id=1, source_target_pairs={{0,112},{4,116},{8,120},{12,124},{16,8},{20,12},{24,0},{28,4},{32,... | collective-permute-start | bytes 1671176 | tf_op jit(solution)/shard_map/ppermute | solution.py:44
  68.2 18.7 %collective-permute-done.2.refs_0_ = bf16[2,512,512]{2,1,0:T(8,128)(2,1)S(1)} collective-permute-done((bf16[2,512,512]{2,1,0:T(8,128)(2,1)}, bf16[2,512,512]{2,1,0:T(8,128)(2,1)S(1)}, u32[]{:S(2)}, u32[]{:S(2)}) %collective-permute-start.2) | collective-permute-done | bytes 1048608 | tf_op jit(solution)/shard_map/ppermute | solution.py:28
  86.9 52.1 %collective-permute-done.5.refs_1_ = bf16[272,1024]{1,0:T(8,128)(2,1)} collective-permute-done((bf16[272,1024]{1,0:T(8,128)(2,1)S(1)}, bf16[272,1024]{1,0:T(8,128)(2,1)}, u32[]{:S(2)}, u32[]{:S(2)}) %collective-permute-start.5) | collective-permute-done | bytes 557088 | tf_op jit(solution)/shard_map/ppermute | solution.py:44
  139.1 8.7 %collective-permute-start.10 = (bf16[2,512,512]{2,1,0:T(8,128)(2,1)}, bf16[2,512,512]{2,1,0:T(8,128)(2,1)}, u32[]{:S(2)}, u32[]{:S(2)}) collective-permute-start(bf16[2,512,512]{2,1,0:T(8,128)(2,1)} %shard_map.101.refs_2_.refs_1_), channel_id=1, source_target_pairs={{0,16},{4,20},{8,24},{12,28},{16,32},{20,36},{24,40},{28,44},{32,4... | collective-permute-start | bytes 3145736 | tf_op jit(solution)/shard_map/ppermute | solution.py:28
  147.8 2.4 broadcast_select_fusion
  150.1 0.7 collective-permute-start.9
  150.9 1.2 copy-done.14
  152.1 5.0 %shard_map.102 = (f32[512,512]{1,0:T(8,128)S(1)}, f32[4,512,128]{2,1,0:T(8,128)S(1)}, f32[4,512,128]{2,1,0:T(8,128)S(1)}) custom-call(s32[8]{0:T(128)S(1)} %stack.65.meta, bf16[512,512]{1,0:T(8,128)(2,1)S(1)} %get-tuple-element.17.refs_0_, s32[512,128]{1,0:T(8,128)S(1)} %broadcast_in_dim.24.refs_1_, bf16[2,512,512]{2,1,0:T(8,128)(2,1)S(1)} %copy-done.1, ...), custom_call_target="tpu_custom_call" | custom-call | flops 1 | bytes 1 | tf_op jit(solution)/shard_map/pallas_call | solution.py:210
  157.1 1.0 copy-done.6
  158.1 1.0 copy-done.15
  159.2 1.0 copy-done.17
  160.1 43.0 %collective-permute-done.1.refs_0_ = bf16[2,512,512]{2,1,0:T(8,128)(2,1)} collective-permute-done((bf16[2,512,512]{2,1,0:T(8,128)(2,1)}, bf16[2,512,512]{2,1,0:T(8,128)(2,1)}, u32[]{:S(2)}, u32[]{:S(2)}) %collective-permute-start.1) | collective-permute-done | bytes 1048608 | tf_op jit(solution)/shard_map/ppermute | solution.py:28
  203.2 0.8 collective-permute-start.6
  204.0 1.9 collective-permute-start.7
  206.0 25.5 %collective-permute-start.12 = (bf16[272,1024]{1,0:T(8,128)(2,1)}, bf16[272,1024]{1,0:T(8,128)(2,1)}, u32[]{:S(2)}, u32[]{:S(2)}) collective-permute-start(bf16[272,1024]{1,0:T(8,128)(2,1)} %collective-permute-done.5.refs_1_), channel_id=1, source_target_pairs={{0,16},{4,20},{8,24},{12,28},{16,32},{20,36},{24,40},{28,44},{32,4... | collective-permute-start | bytes 1671176 | tf_op jit(solution)/shard_map/ppermute | solution.py:44
  231.5 1.2 copy-done.16
  232.7 1.2 copy-done.18
  233.9 5.5 %shard_map.104 = (f32[512,512]{1,0:T(8,128)S(1)}, f32[4,512,128]{2,1,0:T(8,128)S(1)}, f32[4,512,128]{2,1,0:T(8,128)S(1)}) custom-call(s32[8]{0:T(128)S(1)} %stack.65.meta, bf16[512,512]{1,0:T(8,128)(2,1)S(1)} %get-tuple-element.17.refs_0_, s32[512,128]{1,0:T(8,128)S(1)} %broadcast_in_dim.24.refs_1_, bf16[2,512,512]{2,1,0:T(8,128)(2,1)} %collective-permute-done.10.refs_2_, ...), custom_call_target="tpu_custom_call" | custom-call | flops 1 | bytes 1 | tf_op jit(solution)/shard_map/pallas_call | solution.py:210
  239.5 12.8 %collective-permute-done.7.refs_3_ = bf16[2,512,512]{2,1,0:T(8,128)(2,1)S(1)} collective-permute-done((bf16[2,512,512]{2,1,0:T(8,128)(2,1)}, bf16[2,512,512]{2,1,0:T(8,128)(2,1)S(1)}, u32[]{:S(2)}, u32[]{:S(2)}) %collective-permute-start.7) | collective-permute-done | bytes 1048608 | tf_op jit(solution)/shard_map/ppermute | solution.py:28
  252.3 5.5 %shard_map.105 = (bf16[256,512]{1,0:T(8,128)(2,1)S(1)}, bf16[256,512]{1,0:T(8,128)(2,1)S(1)}) custom-call(s32[8]{0:T(128)S(1)} %stack.65.meta, bf16[512,512]{1,0:T(8,128)(2,1)S(1)} %get-tuple-element.17.refs_0_, s32[512,128]{1,0:T(8,128)S(1)} %broadcast_in_dim.24.refs_1_, bf16[2,512,512]{2,1,0:T(8,128)(2,1)S(1)} %collective-permute-done.6.refs_2_, ...), custom_call_target="tpu_custom_call" | custom-call | flops 1 | bytes 1 | tf_op jit(solution)/shard_map/pallas_call | solution.py:210
  257.8 3.2 %collective-permute-start.11 = (bf16[256,512]{1,0:T(8,128)(2,1)S(1)}, bf16[256,512]{1,0:T(8,128)(2,1)S(1)}, u32[]{:S(2)}, u32[]{:S(2)}) collective-permute-start(bf16[256,512]{1,0:T(8,128)(2,1)S(1)} %get-tuple-element.30), channel_id=1, source_target_pairs={{0,4},{4,0},{8,12},{12,8},{16,20},{20,16},{24,28},{28,24},{32,36},... | collective-permute-start | bytes 786440 | tf_op jit(solution)/shard_map/ppermute | solution.py:33
  261.1 2.9 %shard_map.106 = bf16[256,1024]{1,0:T(8,128)(2,1)} custom-call(f32[256,1024]{1,0:T(8,128)S(1)} %copy-done.20, bf16[272,1024]{1,0:T(8,128)(2,1)} %collective-permute-done.12.ob_ref, f32[16,256]{1,0:T(8,128)S(1)} %get-tuple-element.20.refs_0_.sa_ref), custom_call_target="tpu_custom_call" | custom-call | flops 1 | bytes 1 | tf_op jit(solution)/shard_map/pallas_call | solution.py:339
  264.0 0.9 maximum_select_fusion
  (70 shorter events, 1.6 us)
Async XLA Ops:
  0.6 17.6 %copy-start.21 = (s32[512,2]{0,1:T(2,128)S(1)}, s32[512,2]{0,1:T(2,128)}, u32[]{:S(2)}) copy-start(s32[512,2]{0,1:T(2,128)} %param.14) | copy-start | bytes 12292
  0.6 18.0 %copy-start.22 = (s32[33]{0:T(128)S(1)}, s32[33]{0:T(128)}, u32[]{:S(2)}) copy-start(s32[33]{0:T(128)} %param.15) | copy-start | bytes 400
  0.7 21.6 %copy-start.3 = (bf16[3,128,1024]{2,1,0:T(8,128)(2,1)S(1)}, bf16[3,128,1024]{2,1,0:T(8,128)(2,1)}, u32[]{:S(2)}) copy-start(bf16[3,128,1024]{2,1,0:T(8,128)(2,1)} %v_here.3) | copy-start | bytes 2359300
  0.7 21.5 %copy-start.2 = (bf16[3,128,1024]{2,1,0:T(8,128)(2,1)S(1)}, bf16[3,128,1024]{2,1,0:T(8,128)(2,1)}, u32[]{:S(2)}) copy-start(bf16[3,128,1024]{2,1,0:T(8,128)(2,1)} %k_here.3) | copy-start | bytes 2359300
  2.9 20.7 %collective-permute-start = (bf16[3,256,512]{2,1,0:T(8,128)(2,1)}, bf16[3,256,512]{2,1,0:T(8,128)(2,1)S(1)}, u32[]{:S(2)}, u32[]{:S(2)}) collective-permute-start(bf16[3,256,512]{2,1,0:T(8,128)(2,1)} %shard_map.95), channel_id=1, source_target_pairs={{0,4},{4,0},{8,12},{12,8},{16,20},{20,16},{24,28},{28,24},{32,36},... | collective-permute-start | bytes 2359304 | tf_op jit(solution)/shard_map/ppermute | solution.py:33
  5.4 47.7 %collective-permute-start.3 = (bf16[256,1024]{1,0:T(8,128)(2,1)}, bf16[256,1024]{1,0:T(8,128)(2,1)}, u32[]{:S(2)}, u32[]{:S(2)}) collective-permute-start(bf16[256,1024]{1,0:T(8,128)(2,1)} %q_ref.1), channel_id=1, source_target_pairs={{0,8},{4,12},{8,0},{12,4},{16,24},{20,28},{24,16},{28,20},{32,40},... | collective-permute-start | bytes 1572872 | tf_op jit(solution)/shard_map/ppermute | solution.py:33
  22.2 1.4 copy-start.8
  22.2 1.5 copy-start.9
  22.2 1.9 copy-start.10
  25.2 61.7 %collective-permute-start.2 = (bf16[2,512,512]{2,1,0:T(8,128)(2,1)}, bf16[2,512,512]{2,1,0:T(8,128)(2,1)S(1)}, u32[]{:S(2)}, u32[]{:S(2)}) collective-permute-start(bf16[2,512,512]{2,1,0:T(8,128)(2,1)} %get-tuple-element.18.refs_1_.refs_2_), channel_id=1, source_target_pairs={{0,16},{4,20},{8,24},{12,28},{16,32},{20,36},{24,40},{28,44},{32,4... | collective-permute-start | bytes 3145736 | tf_op jit(solution)/shard_map/ppermute | solution.py:28
  27.9 175.3 %collective-permute-start.1 = (bf16[2,512,512]{2,1,0:T(8,128)(2,1)}, bf16[2,512,512]{2,1,0:T(8,128)(2,1)}, u32[]{:S(2)}, u32[]{:S(2)}) collective-permute-start(bf16[2,512,512]{2,1,0:T(8,128)(2,1)} %get-tuple-element.18.refs_1_.refs_2_), channel_id=1, source_target_pairs={{0,24},{4,28},{8,32},{12,36},{16,40},{20,44},{24,48},{28,52},{32,5... | collective-permute-start | bytes 3145736 | tf_op jit(solution)/shard_map/ppermute | solution.py:28
  30.5 117.3 %collective-permute-start.8 = (bf16[2,512,512]{2,1,0:T(8,128)(2,1)}, bf16[2,512,512]{2,1,0:T(8,128)(2,1)}, u32[]{:S(2)}, u32[]{:S(2)}) collective-permute-start(bf16[2,512,512]{2,1,0:T(8,128)(2,1)} %get-tuple-element.18.refs_1_.refs_2_), channel_id=1, source_target_pairs={{104,136},{108,140},{232,264},{236,268},{360,392},{364,396},{488,8... | collective-permute-start | bytes 3145736 | tf_op jit(solution)/shard_map/ppermute | solution.py:28
  32.1 9.6 %collective-permute-start.4 = (bf16[2,3,128,1024]{3,2,1,0:T(8,128)(2,1)}, bf16[2,3,128,1024]{3,2,1,0:T(8,128)(2,1)S(1)}, u32[]{:S(2)}, u32[]{:S(2)}) collective-permute-start(bf16[2,3,128,1024]{3,2,1,0:T(8,128)(2,1)} %shard_map.97), channel_id=1, source_target_pairs={{0,4},{4,0},{8,12},{12,8},{16,20},{20,16},{24,28},{28,24},{32,36},... | collective-permute-start | bytes 4718600 | tf_op jit(solution)/shard_map/ppermute | solution.py:33
  39.7 1.0 copy-start.11
  40.7 1.0 copy-start.13
  41.8 4.7 %copy-start.4 = (f32[512,512]{1,0:T(8,128)}, f32[512,512]{1,0:T(8,128)S(1)}, u32[]{:S(2)}) copy-start(f32[512,512]{1,0:T(8,128)S(1)} %get-tuple-element.19.refs_0_.refs_3_) | copy-start | bytes 3145732
  46.4 10.9 %copy-start.19 = (f32[256,1024]{1,0:T(8,128)}, f32[256,1024]{1,0:T(8,128)S(1)}, u32[]{:S(2)}) copy-start(f32[256,1024]{1,0:T(8,128)S(1)} %get-tuple-element.31.oa_ref) | copy-start | bytes 3145732
  57.4 81.7 %collective-permute-start.5 = (bf16[272,1024]{1,0:T(8,128)(2,1)S(1)}, bf16[272,1024]{1,0:T(8,128)(2,1)}, u32[]{:S(2)}, u32[]{:S(2)}) collective-permute-start(bf16[272,1024]{1,0:T(8,128)(2,1)S(1)} %shard_map.100), channel_id=1, source_target_pairs={{0,112},{4,116},{8,120},{12,124},{16,8},{20,12},{24,0},{28,4},{32,... | collective-permute-start | bytes 1671176 | tf_op jit(solution)/shard_map/ppermute | solution.py:44
  86.9 52.2 %copy-start = (bf16[2,512,512]{2,1,0:T(8,128)(2,1)}, bf16[2,512,512]{2,1,0:T(8,128)(2,1)S(1)}, u32[]{:S(2)}) copy-start(bf16[2,512,512]{2,1,0:T(8,128)(2,1)S(1)} %collective-permute-done.2.refs_0_) | copy-start | bytes 3145732
  139.0 11.8 %copy-start.1 = (bf16[2,512,512]{2,1,0:T(8,128)(2,1)S(1)}, bf16[2,512,512]{2,1,0:T(8,128)(2,1)}, u32[]{:S(2)}) copy-start(bf16[2,512,512]{2,1,0:T(8,128)(2,1)} %shard_map.101.refs_2_.refs_1_) | copy-start | bytes 3145732
  139.1 11.8 %copy-start.5 = (f32[512,512]{1,0:T(8,128)S(1)}, f32[512,512]{1,0:T(8,128)}, u32[]{:S(2)}) copy-start(f32[512,512]{1,0:T(8,128)} %copy-done.4) | copy-start | bytes 3145732
  139.1 11.8 %copy-start.12 = (f32[4,512,128]{2,1,0:T(8,128)S(1)}, f32[4,512,128]{2,1,0:T(8,128)}, u32[]{:S(2)}) copy-start(f32[4,512,128]{2,1,0:T(8,128)} %copy-done.11) | copy-start | bytes 3145732
  139.1 92.4 %collective-permute-start.10 = (bf16[2,512,512]{2,1,0:T(8,128)(2,1)}, bf16[2,512,512]{2,1,0:T(8,128)(2,1)}, u32[]{:S(2)}, u32[]{:S(2)}) collective-permute-start(bf16[2,512,512]{2,1,0:T(8,128)(2,1)} %shard_map.101.refs_2_.refs_1_), channel_id=1, source_target_pairs={{0,16},{4,20},{8,24},{12,28},{16,32},{20,36},{24,40},{28,44},{32,4... | collective-permute-start | bytes 3145736 | tf_op jit(solution)/shard_map/ppermute | solution.py:28
  150.1 89.3 %collective-permute-start.9 = (bf16[2,512,512]{2,1,0:T(8,128)(2,1)}, bf16[2,512,512]{2,1,0:T(8,128)(2,1)S(1)}, u32[]{:S(2)}, u32[]{:S(2)}) collective-permute-start(bf16[2,512,512]{2,1,0:T(8,128)(2,1)} %broadcast_select_fusion), channel_id=1, source_target_pairs={{0,504},{4,508},{8,496},{12,500},{128,120},{132,124},{136,112},{14... | collective-permute-start | bytes 3145736 | tf_op jit(solution)/shard_map/ppermute | solution.py:418
  150.9 1.2 copy-start.14
  157.1 1.0 copy-start.6
  158.1 1.0 copy-start.15
  159.2 1.0 copy-start.17
  203.2 28.3 %copy-start.7 = (f32[512,512]{1,0:T(8,128)S(1)}, f32[512,512]{1,0:T(8,128)}, u32[]{:S(2)}) copy-start(f32[512,512]{1,0:T(8,128)} %copy-done.6) | copy-start | bytes 3145732
  203.2 36.3 %collective-permute-start.6 = (bf16[2,512,512]{2,1,0:T(8,128)(2,1)}, bf16[2,512,512]{2,1,0:T(8,128)(2,1)S(1)}, u32[]{:S(2)}, u32[]{:S(2)}) collective-permute-start(bf16[2,512,512]{2,1,0:T(8,128)(2,1)} %shard_map.103.refs_4_), channel_id=1, source_target_pairs={{120,128},{124,132},{248,256},{252,260},{376,384},{380,388},{504,0... | collective-permute-start | bytes 3145736 | tf_op jit(solution)/shard_map/ppermute | solution.py:28
  204.0 48.3 %collective-permute-start.7 = (bf16[2,512,512]{2,1,0:T(8,128)(2,1)}, bf16[2,512,512]{2,1,0:T(8,128)(2,1)S(1)}, u32[]{:S(2)}, u32[]{:S(2)}) collective-permute-start(bf16[2,512,512]{2,1,0:T(8,128)(2,1)} %shard_map.103.refs_4_), channel_id=1, source_target_pairs={{16,0},{20,4},{24,8},{28,12},{32,16},{36,20},{40,24},{44,28},{48,3... | collective-permute-start | bytes 3145736 | tf_op jit(solution)/shard_map/ppermute | solution.py:28
  206.0 55.1 %collective-permute-start.12 = (bf16[272,1024]{1,0:T(8,128)(2,1)}, bf16[272,1024]{1,0:T(8,128)(2,1)}, u32[]{:S(2)}, u32[]{:S(2)}) collective-permute-start(bf16[272,1024]{1,0:T(8,128)(2,1)} %collective-permute-done.5.refs_1_), channel_id=1, source_target_pairs={{0,16},{4,20},{8,24},{12,28},{16,32},{20,36},{24,40},{28,44},{32,4... | collective-permute-start | bytes 1671176 | tf_op jit(solution)/shard_map/ppermute | solution.py:44
  231.5 1.2 copy-start.16
  232.7 1.2 copy-start.18
  252.3 8.8 %copy-start.20 = (f32[256,1024]{1,0:T(8,128)S(1)}, f32[256,1024]{1,0:T(8,128)}, u32[]{:S(2)}) copy-start(f32[256,1024]{1,0:T(8,128)} %copy-done.19) | copy-start | bytes 3145732
  257.8 6.2 %collective-permute-start.11 = (bf16[256,512]{1,0:T(8,128)(2,1)S(1)}, bf16[256,512]{1,0:T(8,128)(2,1)S(1)}, u32[]{:S(2)}, u32[]{:S(2)}) collective-permute-start(bf16[256,512]{1,0:T(8,128)(2,1)S(1)} %get-tuple-element.30), channel_id=1, source_target_pairs={{0,4},{4,0},{8,12},{12,8},{16,20},{20,16},{24,28},{28,24},{32,36},... | collective-permute-start | bytes 786440 | tf_op jit(solution)/shard_map/ppermute | solution.py:33

commit v8 on v7

--- a/solution.py
+++ b/solution.py
@@ -413,10 +413,13 @@
         pool_meta(device ^ 2), far_queries, pool, True, (near_stat,), SMALL
     )
     nearly = around(far_sum, 7)
+    from_first = jnp.where(high == 0, kv2, kv4_far)
+    state = attend(((2, 0),), (kv2,), state, after=(far_sum, from_first))
+    nearly = held_back(nearly, state[:1])
     kv2 = held_back(kv2, (nearly,))
     kv4 = shift(kv2, 4, lambda low, high: low > 0)
     kv1_edge = lax.ppermute(
-        jnp.where(high == 0, kv2, kv4_far),
+        from_first,
         ALL,
         [
             (d, (d - 2 - 4 * place(d)[1]) % lax.axis_size(ALL))
@@ -424,8 +427,7 @@
             if place(d)[0] == 0
         ],
     )
-    state = attend(((2, 0),), (kv2,), state)
-    kv3 = held_back(kv3, (kv2, state[0]))
+    kv3 = held_back(kv3, (kv2,))
     kv1 = shift(kv3, -4, lambda low, high: low < RUN - 1)
     kv4_last = shift(kv3, 2, lambda low, high: low == 0 and high == 0)
     back_sum = around(nearly, 1)

time: 266 us -> 270 us (1.015)
  the two profiles are of different devices: /device:TPU:101 before, /device:TPU:121 now
where the time goes in v8:
time: 270 us; the launch traced here: 269 us
  waiting for transfers between devices  148 us (55%)
  starting transfers between devices  77.2 us (29%)
  Pallas kernels  29.4 us (11%)
  local copies, waits for them, and re-layouts  8.99 us (3%)
  other arithmetic  3.16 us (1%)
    ppermute x6, waiting for transfers between devices, shift(): return lax.ppermute(value, ALL, [(a, b) for a, b in pairs if to(*place(b))])  105 us
    ppermute x2, starting transfers between devices, around(): return lax.ppermute(value, ALL, [(d, target(d)) for d in range(count)])  34.9 us
    ppermute x2, waiting for transfers between devices, around(): return lax.ppermute(value, ALL, [(d, target(d)) for d in range(count)])  31 us
    ppermute x4, starting transfers between devices, swap(): return lax.ppermute(value, ALL, [(d, d ^ bit) for d in range(count)])  21.3 us
    ppermute x6, starting transfers between devices, shift(): return lax.ppermute(value, ALL, [(a, b) for a, b in pairs if to(*place(b))])  19.4 us
    pallas_call x4, Pallas kernels, self_part(): pl.pallas_call(functools.partial(self_kernel, tuple(blocks), first, last,...  14.7 us
    ppermute x4, waiting for transfers between devices, swap(): return lax.ppermute(value, ALL, [(d, d ^ bit) for d in range(count)])  12.7 us
    pallas_call x2, Pallas kernels, cross_part(): pl.pallas_call(functools.partial(cross_kernel, rows // STRETCH, travels),...  8.54 us
  transfers between devices with their start and end apart: 13, of which 5 were waited for; matrix products, arithmetic and copies ran while one was open for 2% of the time, Pallas kernels for 10%

profile of v8, /device:TPU:121, one launch (start us, length us, event | category | flops | bytes accessed | tf_op | source)
XLA Modules:
  0.0 269.3 jit_solution(17858872574301188495)
XLA Ops:
  0.7 2.2 shard_map.95
  2.9 2.6 collective-permute-start
  5.4 12.7 %collective-permute-start.3 = (bf16[256,1024]{1,0:T(8,128)(2,1)}, bf16[256,1024]{1,0:T(8,128)(2,1)}, u32[]{:S(2)}, u32[]{:S(2)}) collective-permute-start(bf16[256,1024]{1,0:T(8,128)(2,1)} %q_ref.1), channel_id=1, source_target_pairs={{0,8},{4,12},{8,0},{12,4},{16,24},{20,28},{24,16},{28,20},{32,40},... | collective-permute-start | bytes 1572872 | tf_op jit(solution)/shard_map/ppermute | solution.py:33
  18.6 0.1 copy.28
  18.8 0.1 reduce
  19.0 0.6 fusion
  19.6 0.1 copy.29
  19.8 0.1 copy.32
  19.9 0.1 copy.31
  20.1 0.1 copy.34
  20.3 0.1 copy.30
  20.5 0.1 copy.33
  22.2 1.3 pad_maximum_fusion.refs_0_
  23.6 0.2 copy-done.6
  23.7 0.4 copy-done.7
  24.1 1.1 shard_map.96
  25.2 2.6 collective-permute-start.2
  27.8 1.6 collective-permute-start.6
  29.5 2.6 collective-permute-start.1
  32.1 2.8 %collective-permute-start.4 = (bf16[2,3,128,1024]{3,2,1,0:T(8,128)(2,1)}, bf16[2,3,128,1024]{3,2,1,0:T(8,128)(2,1)S(1)}, u32[]{:S(2)}, u32[]{:S(2)}) collective-permute-start(bf16[2,3,128,1024]{3,2,1,0:T(8,128)(2,1)} %shard_map.97), channel_id=1, source_target_pairs={{0,4},{4,0},{8,12},{12,8},{16,20},{20,16},{24,28},{28,24},{32,36},... | collective-permute-start | bytes 4718600 | tf_op jit(solution)/shard_map/ppermute | solution.py:33
  34.9 0.1 broadcast_in_dim.24.refs_1_
  35.0 4.7 %shard_map.98 = (f32[512,512]{1,0:T(8,128)S(1)}, f32[4,512,128]{2,1,0:T(8,128)S(1)}, f32[4,512,128]{2,1,0:T(8,128)S(1)}) custom-call(s32[8]{0:T(128)S(1)} %stack.65.meta, bf16[512,512]{1,0:T(8,128)(2,1)S(1)} %get-tuple-element.17.refs_0_, s32[512,128]{1,0:T(8,128)S(1)} %broadcast_in_dim.24.refs_1_, bf16[2,512,512]{2,1,0:T(8,128)(2,1)} %get-tuple-element.18.refs_1_.refs_2_), custom_call_target="tpu_custom_call" | custom-call | flops 99999997952 | bytes 100000000 | tf_op jit(solution)/shard_map/pallas_call | solution.py:210
  39.7 4.3 %shard_map.99 = (f32[256,1024]{1,0:T(8,128)S(1)}, f32[16,256]{1,0:T(8,128)S(1)}) custom-call(s32[24]{0:T(128)S(1)} %pad_add_fusion.2.meta, bf16[256,1024]{1,0:T(8,128)(2,1)} %q_ref.1, bf16[3,128,1024]{2,1,0:T(8,128)(2,1)S(1)} %copy-done.1, bf16[3,128,1024]{2,1,0:T(8,128)(2,1)S(1)} %copy-done.2, bf16[2,3,128,1024]{3,2,1,0:T(8,128)(2,1)S(1)} %collective-permute-done.4.side, ...), custom_call_target="tpu_custom_call" | custom-call | flops 1 | bytes 1 | tf_op jit(solution)/shard_map/pallas_call | solution.py:301
  44.0 12.7 %collective-permute-done.3.q_ref = bf16[256,1024]{1,0:T(8,128)(2,1)} collective-permute-done((bf16[256,1024]{1,0:T(8,128)(2,1)}, bf16[256,1024]{1,0:T(8,128)(2,1)}, u32[]{:S(2)}, u32[]{:S(2)}) %collective-permute-start.3) | collective-permute-done | bytes 524320 | tf_op jit(solution)/shard_map/ppermute | solution.py:33
  56.7 4.3 %shard_map.100.refs_6_ = bf16[272,1024]{1,0:T(8,128)(2,1)S(1)} custom-call(s32[24]{0:T(128)S(1)} %pad_add_fusion.1.meta, bf16[256,1024]{1,0:T(8,128)(2,1)} %collective-permute-done.3.q_ref, bf16[3,128,1024]{2,1,0:T(8,128)(2,1)S(1)} %copy-done.1, bf16[3,128,1024]{2,1,0:T(8,128)(2,1)S(1)} %copy-done.2, ...), custom_call_target="tpu_custom_call" | custom-call | flops 1 | bytes 1 | tf_op jit(solution)/shard_map/pallas_call | solution.py:301
  60.9 7.1 %collective-permute-start.5 = (bf16[272,1024]{1,0:T(8,128)(2,1)S(1)}, bf16[272,1024]{1,0:T(8,128)(2,1)}, u32[]{:S(2)}, u32[]{:S(2)}) collective-permute-start(bf16[272,1024]{1,0:T(8,128)(2,1)S(1)} %shard_map.100.refs_6_), channel_id=1, source_target_pairs={{0,112},{4,116},{8,120},{12,124},{16,8},{20,12},{24,0},{28,4},{32,... | collective-permute-start | bytes 1671176 | tf_op jit(solution)/shard_map/ppermute | solution.py:44
  68.1 18.7 %collective-permute-done.2.refs_2_.refs_0_ = bf16[2,512,512]{2,1,0:T(8,128)(2,1)S(1)} collective-permute-done((bf16[2,512,512]{2,1,0:T(8,128)(2,1)}, bf16[2,512,512]{2,1,0:T(8,128)(2,1)S(1)}, u32[]{:S(2)}, u32[]{:S(2)}) %collective-permute-start.2) | collective-permute-done | bytes 1048608 | tf_op jit(solution)/shard_map/ppermute | solution.py:28
  86.8 0.1 broadcast_select_fusion.refs_7_
  86.9 0.9 copy-done
  87.8 1.3 shard_map.101
  89.1 1.0 copy-done.3
  90.0 1.0 copy-done.8
  91.0 1.1 copy-done.10
  92.1 31.0 %collective-permute-done.5.refs_0_ = bf16[272,1024]{1,0:T(8,128)(2,1)} collective-permute-done((bf16[272,1024]{1,0:T(8,128)(2,1)S(1)}, bf16[272,1024]{1,0:T(8,128)(2,1)}, u32[]{:S(2)}, u32[]{:S(2)}) %collective-permute-start.5) | collective-permute-done | bytes 557088 | tf_op jit(solution)/shard_map/ppermute | solution.py:44
  123.1 9.9 %collective-permute-start.10 = (bf16[2,512,512]{2,1,0:T(8,128)(2,1)}, bf16[2,512,512]{2,1,0:T(8,128)(2,1)}, u32[]{:S(2)}, u32[]{:S(2)}) collective-permute-start(bf16[2,512,512]{2,1,0:T(8,128)(2,1)} %shard_map.103.refs_1_), channel_id=1, source_target_pairs={{0,16},{4,20},{8,24},{12,28},{16,32},{20,36},{24,40},{28,44},{32,4... | collective-permute-start | bytes 3145736 | tf_op jit(solution)/shard_map/ppermute | solution.py:28
  133.0 1.6 collective-permute-start.9
  134.6 70.4 %collective-permute-done.1.refs_0_ = bf16[2,512,512]{2,1,0:T(8,128)(2,1)} collective-permute-done((bf16[2,512,512]{2,1,0:T(8,128)(2,1)}, bf16[2,512,512]{2,1,0:T(8,128)(2,1)}, u32[]{:S(2)}, u32[]{:S(2)}) %collective-permute-start.1) | collective-permute-done | bytes 1048608 | tf_op jit(solution)/shard_map/ppermute | solution.py:28
  205.0 0.7 collective-permute-start.7
  205.8 1.9 collective-permute-start.8
  207.7 27.8 %collective-permute-start.12 = (bf16[272,1024]{1,0:T(8,128)(2,1)}, bf16[272,1024]{1,0:T(8,128)(2,1)}, u32[]{:S(2)}, u32[]{:S(2)}) collective-permute-start(bf16[272,1024]{1,0:T(8,128)(2,1)} %shard_map.102.refs_1_), channel_id=1, source_target_pairs={{0,16},{4,20},{8,24},{12,28},{16,32},{20,36},{24,40},{28,44},{32,4... | collective-permute-start | bytes 1671176 | tf_op jit(solution)/shard_map/ppermute | solution.py:44
  235.5 1.2 copy-done.9
  236.7 1.2 copy-done.11
  238.0 2.9 %shard_map.105 = (f32[512,512]{1,0:T(8,128)S(1)}, f32[4,512,128]{2,1,0:T(8,128)S(1)}, f32[4,512,128]{2,1,0:T(8,128)S(1)}) custom-call(s32[8]{0:T(128)S(1)} %stack.65.meta, bf16[512,512]{1,0:T(8,128)(2,1)S(1)} %get-tuple-element.17.refs_0_, s32[512,128]{1,0:T(8,128)S(1)} %broadcast_in_dim.24.refs_1_, bf16[2,512,512]{2,1,0:T(8,128)(2,1)} %collective-permute-done.10.refs_2_, ...), custom_call_target="tpu_custom_call" | custom-call | flops 1 | bytes 1 | tf_op jit(solution)/shard_map/pallas_call | solution.py:210
  240.9 15.5 %collective-permute-done.8.refs_3_ = bf16[2,512,512]{2,1,0:T(8,128)(2,1)S(1)} collective-permute-done((bf16[2,512,512]{2,1,0:T(8,128)(2,1)}, bf16[2,512,512]{2,1,0:T(8,128)(2,1)S(1)}, u32[]{:S(2)}, u32[]{:S(2)}) %collective-permute-start.8) | collective-permute-done | bytes 1048608 | tf_op jit(solution)/shard_map/ppermute | solution.py:28
  256.4 5.8 %shard_map.106 = (bf16[256,512]{1,0:T(8,128)(2,1)S(1)}, bf16[256,512]{1,0:T(8,128)(2,1)S(1)}) custom-call(s32[8]{0:T(128)S(1)} %stack.65.meta, bf16[512,512]{1,0:T(8,128)(2,1)S(1)} %get-tuple-element.17.refs_0_, s32[512,128]{1,0:T(8,128)S(1)} %broadcast_in_dim.24.refs_1_, bf16[2,512,512]{2,1,0:T(8,128)(2,1)S(1)} %collective-permute-done.7.refs_2_, ...), custom_call_target="tpu_custom_call" | custom-call | flops 1 | bytes 1 | tf_op jit(solution)/shard_map/pallas_call | solution.py:210
  262.2 3.2 %collective-permute-start.11 = (bf16[256,512]{1,0:T(8,128)(2,1)S(1)}, bf16[256,512]{1,0:T(8,128)(2,1)S(1)}, u32[]{:S(2)}, u32[]{:S(2)}) collective-permute-start(bf16[256,512]{1,0:T(8,128)(2,1)S(1)} %get-tuple-element.30), channel_id=1, source_target_pairs={{0,4},{4,0},{8,12},{12,8},{16,20},{20,16},{24,28},{28,24},{32,36},... | collective-permute-start | bytes 786440 | tf_op jit(solution)/shard_map/ppermute | solution.py:33
  265.5 2.9 %shard_map.107 = bf16[256,1024]{1,0:T(8,128)(2,1)} custom-call(f32[256,1024]{1,0:T(8,128)S(1)} %copy-done.13, bf16[272,1024]{1,0:T(8,128)(2,1)} %collective-permute-done.12.ob_ref, f32[16,256]{1,0:T(8,128)S(1)} %get-tuple-element.20.refs_0_.sa_ref), custom_call_target="tpu_custom_call" | custom-call | flops 1 | bytes 1 | tf_op jit(solution)/shard_map/pallas_call | solution.py:339
  268.4 0.9 maximum_select_fusion
  (57 shorter events, 1.3 us)
Async XLA Ops:
  0.6 17.7 %copy-start.14 = (s32[512,2]{0,1:T(2,128)S(1)}, s32[512,2]{0,1:T(2,128)}, u32[]{:S(2)}) copy-start(s32[512,2]{0,1:T(2,128)} %param.14) | copy-start | bytes 12292
  0.6 18.0 %copy-start.15 = (s32[33]{0:T(128)S(1)}, s32[33]{0:T(128)}, u32[]{:S(2)}) copy-start(s32[33]{0:T(128)} %param.15) | copy-start | bytes 400
  0.7 21.5 %copy-start.2 = (bf16[3,128,1024]{2,1,0:T(8,128)(2,1)S(1)}, bf16[3,128,1024]{2,1,0:T(8,128)(2,1)}, u32[]{:S(2)}) copy-start(bf16[3,128,1024]{2,1,0:T(8,128)(2,1)} %v_here.3) | copy-start | bytes 2359300
  0.7 21.5 %copy-start.1 = (bf16[3,128,1024]{2,1,0:T(8,128)(2,1)S(1)}, bf16[3,128,1024]{2,1,0:T(8,128)(2,1)}, u32[]{:S(2)}) copy-start(bf16[3,128,1024]{2,1,0:T(8,128)(2,1)} %k_here.3) | copy-start | bytes 2359300
  2.9 20.7 %collective-permute-start = (bf16[3,256,512]{2,1,0:T(8,128)(2,1)}, bf16[3,256,512]{2,1,0:T(8,128)(2,1)S(1)}, u32[]{:S(2)}, u32[]{:S(2)}) collective-permute-start(bf16[3,256,512]{2,1,0:T(8,128)(2,1)} %shard_map.95), channel_id=1, source_target_pairs={{0,4},{4,0},{8,12},{12,8},{16,20},{20,16},{24,28},{28,24},{32,36},... | collective-permute-start | bytes 2359304 | tf_op jit(solution)/shard_map/ppermute | solution.py:33
  5.4 51.2 %collective-permute-start.3 = (bf16[256,1024]{1,0:T(8,128)(2,1)}, bf16[256,1024]{1,0:T(8,128)(2,1)}, u32[]{:S(2)}, u32[]{:S(2)}) collective-permute-start(bf16[256,1024]{1,0:T(8,128)(2,1)} %q_ref.1), channel_id=1, source_target_pairs={{0,8},{4,12},{8,0},{12,4},{16,24},{20,28},{24,16},{28,20},{32,40},... | collective-permute-start | bytes 1572872 | tf_op jit(solution)/shard_map/ppermute | solution.py:33
  22.2 1.4 copy-start.5
  22.2 1.5 copy-start.6
  22.2 1.9 copy-start.7
  25.2 61.6 %collective-permute-start.2 = (bf16[2,512,512]{2,1,0:T(8,128)(2,1)}, bf16[2,512,512]{2,1,0:T(8,128)(2,1)S(1)}, u32[]{:S(2)}, u32[]{:S(2)}) collective-permute-start(bf16[2,512,512]{2,1,0:T(8,128)(2,1)} %get-tuple-element.18.refs_1_.refs_2_), channel_id=1, source_target_pairs={{0,16},{4,20},{8,24},{12,28},{16,32},{20,36},{24,40},{28,44},{32,4... | collective-permute-start | bytes 3145736 | tf_op jit(solution)/shard_map/ppermute | solution.py:28
  27.8 58.9 %collective-permute-start.6 = (bf16[2,512,512]{2,1,0:T(8,128)(2,1)}, bf16[2,512,512]{2,1,0:T(8,128)(2,1)}, u32[]{:S(2)}, u32[]{:S(2)}) collective-permute-start(bf16[2,512,512]{2,1,0:T(8,128)(2,1)} %get-tuple-element.18.refs_1_.refs_2_), channel_id=1, source_target_pairs={{104,136},{108,140},{232,264},{236,268},{360,392},{364,396},{488,8... | collective-permute-start | bytes 3145736 | tf_op jit(solution)/shard_map/ppermute | solution.py:28
  29.5 175.6 %collective-permute-start.1 = (bf16[2,512,512]{2,1,0:T(8,128)(2,1)}, bf16[2,512,512]{2,1,0:T(8,128)(2,1)}, u32[]{:S(2)}, u32[]{:S(2)}) collective-permute-start(bf16[2,512,512]{2,1,0:T(8,128)(2,1)} %get-tuple-element.18.refs_1_.refs_2_), channel_id=1, source_target_pairs={{0,24},{4,28},{8,32},{12,36},{16,40},{20,44},{24,48},{28,52},{32,5... | collective-permute-start | bytes 3145736 | tf_op jit(solution)/shard_map/ppermute | solution.py:28
  32.1 7.6 %collective-permute-start.4 = (bf16[2,3,128,1024]{3,2,1,0:T(8,128)(2,1)}, bf16[2,3,128,1024]{3,2,1,0:T(8,128)(2,1)S(1)}, u32[]{:S(2)}, u32[]{:S(2)}) collective-permute-start(bf16[2,3,128,1024]{3,2,1,0:T(8,128)(2,1)} %shard_map.97), channel_id=1, source_target_pairs={{0,4},{4,0},{8,12},{12,8},{16,20},{20,16},{24,28},{28,24},{32,36},... | collective-permute-start | bytes 4718600 | tf_op jit(solution)/shard_map/ppermute | solution.py:33
  44.0 17.0 %copy-start.12 = (f32[256,1024]{1,0:T(8,128)}, f32[256,1024]{1,0:T(8,128)S(1)}, u32[]{:S(2)}) copy-start(f32[256,1024]{1,0:T(8,128)S(1)} %get-tuple-element.31.oa_ref) | copy-start | bytes 3145732
  60.9 62.1 %collective-permute-start.5 = (bf16[272,1024]{1,0:T(8,128)(2,1)S(1)}, bf16[272,1024]{1,0:T(8,128)(2,1)}, u32[]{:S(2)}, u32[]{:S(2)}) collective-permute-start(bf16[272,1024]{1,0:T(8,128)(2,1)S(1)} %shard_map.100.refs_6_), channel_id=1, source_target_pairs={{0,112},{4,116},{8,120},{12,124},{16,8},{20,12},{24,0},{28,4},{32,... | collective-permute-start | bytes 1671176 | tf_op jit(solution)/shard_map/ppermute | solution.py:44
  86.8 1.0 copy-start
  89.0 1.0 copy-start.3
  90.0 1.0 copy-start.8
  91.0 1.1 copy-start.10
  123.1 112.4 %copy-start.4 = (f32[512,512]{1,0:T(8,128)S(1)}, f32[512,512]{1,0:T(8,128)}, u32[]{:S(2)}) copy-start(f32[512,512]{1,0:T(8,128)} %copy-done.3) | copy-start | bytes 3145732
  123.1 112.4 %collective-permute-start.10 = (bf16[2,512,512]{2,1,0:T(8,128)(2,1)}, bf16[2,512,512]{2,1,0:T(8,128)(2,1)}, u32[]{:S(2)}, u32[]{:S(2)}) collective-permute-start(bf16[2,512,512]{2,1,0:T(8,128)(2,1)} %shard_map.103.refs_1_), channel_id=1, source_target_pairs={{0,16},{4,20},{8,24},{12,28},{16,32},{20,36},{24,40},{28,44},{32,4... | collective-permute-start | bytes 3145736 | tf_op jit(solution)/shard_map/ppermute | solution.py:28
  133.0 107.9 %collective-permute-start.9 = (bf16[2,512,512]{2,1,0:T(8,128)(2,1)S(1)}, bf16[2,512,512]{2,1,0:T(8,128)(2,1)}, u32[]{:S(2)}, u32[]{:S(2)}) collective-permute-start(bf16[2,512,512]{2,1,0:T(8,128)(2,1)S(1)} %broadcast_select_fusion.refs_7_), channel_id=1, source_target_pairs={{0,504},{4,508},{8,496},{12,500},{128,120},{132,124},{136,112},{14... | collective-permute-start | bytes 3145736 | tf_op jit(solution)/shard_map/ppermute | solution.py:421
  205.0 35.8 %collective-permute-start.7 = (bf16[2,512,512]{2,1,0:T(8,128)(2,1)}, bf16[2,512,512]{2,1,0:T(8,128)(2,1)S(1)}, u32[]{:S(2)}, u32[]{:S(2)}) collective-permute-start(bf16[2,512,512]{2,1,0:T(8,128)(2,1)} %shard_map.104.refs_4_), channel_id=1, source_target_pairs={{120,128},{124,132},{248,256},{252,260},{376,384},{380,388},{504,0... | collective-permute-start | bytes 3145736 | tf_op jit(solution)/shard_map/ppermute | solution.py:28
  205.8 50.6 %collective-permute-start.8 = (bf16[2,512,512]{2,1,0:T(8,128)(2,1)}, bf16[2,512,512]{2,1,0:T(8,128)(2,1)S(1)}, u32[]{:S(2)}, u32[]{:S(2)}) collective-permute-start(bf16[2,512,512]{2,1,0:T(8,128)(2,1)} %shard_map.104.refs_4_), channel_id=1, source_target_pairs={{16,0},{20,4},{24,8},{28,12},{32,16},{36,20},{40,24},{44,28},{48,3... | collective-permute-start | bytes 3145736 | tf_op jit(solution)/shard_map/ppermute | solution.py:28
  207.7 57.7 %collective-permute-start.12 = (bf16[272,1024]{1,0:T(8,128)(2,1)}, bf16[272,1024]{1,0:T(8,128)(2,1)}, u32[]{:S(2)}, u32[]{:S(2)}) collective-permute-start(bf16[272,1024]{1,0:T(8,128)(2,1)} %shard_map.102.refs_1_), channel_id=1, source_target_pairs={{0,16},{4,20},{8,24},{12,28},{16,32},{20,36},{24,40},{28,44},{32,4... | collective-permute-start | bytes 1671176 | tf_op jit(solution)/shard_map/ppermute | solution.py:44
  235.5 1.2 copy-start.9
  236.7 1.2 copy-start.11
  256.4 9.0 %copy-start.13 = (f32[256,1024]{1,0:T(8,128)S(1)}, f32[256,1024]{1,0:T(8,128)}, u32[]{:S(2)}) copy-start(f32[256,1024]{1,0:T(8,128)} %copy-done.12) | copy-start | bytes 3145732
  262.2 6.2 %collective-permute-start.11 = (bf16[256,512]{1,0:T(8,128)(2,1)S(1)}, bf16[256,512]{1,0:T(8,128)(2,1)S(1)}, u32[]{:S(2)}, u32[]{:S(2)}) collective-permute-start(bf16[256,512]{1,0:T(8,128)(2,1)S(1)} %get-tuple-element.30), channel_id=1, source_target_pairs={{0,4},{4,0},{8,12},{12,8},{16,20},{20,16},{24,28},{28,24},{32,36},... | collective-permute-start | bytes 786440 | tf_op jit(solution)/shard_map/ppermute | solution.py:33
